TPU v7x, 32 devices: a whole 2x2x4 slice. The times are simulated.
32 devices in a mesh: spec: 4 (over y, x), geo: 8 (over z, core).
Axes of the slice: x: 2, y: 2, z: 4, core: 2. Of those that a mesh axis runs over, the one named last changes fastest.
Arguments:
- spectrum: bfloat16 [1296, 128, 128], P('spec', 'geo'), may hold values from 0.01 to 11, as said below
- sea_map: int32 [128, 128], P('geo'), may hold values 0 or 1
- depth_factor: float32 [128, 128], P('geo'), may hold values from 0.25 to 1
- wind_speed: bfloat16 [128, 128], P('geo'), may hold values from 0.19921875 to 2
- wind_dir: bfloat16 [128, 128], P('geo'), may hold values from -3.140625 to 3.140625
- ice_mask: int32 [128, 128], P('geo'), may hold values from 0 to 1, as said below
- owner_map: int32 [128, 128], P('geo'), may hold values from 0 to 7, as said below
- pair_kernel: bfloat16 [1296, 1296], replicated, may hold values from -1 to 2
- transfer_kernel: bfloat16 [8, 1296, 1296], P('geo'), may hold values from -1 to 2
Outputs:
- updated: bfloat16 [1296, 128, 128], P('spec', 'geo')
Inputs may be any that keep to these rules, and one draw needn't show every extreme that they name: `owner_map`: in each aligned block of 512 cells of the grid in row-major order, no owner is named by more than 128 cells, and one owner, the same in every block, is named by exactly 128 cells of each block. `ice_mask`: 1 marks ice. Cells of the owner that is named by 128 cells of every block are free of ice. `spectrum`: Positive.
All inputs are finite; a program needn't handle non-finite values. No bound on the sum of `sea_map` on one device may be relied on, other than what follows from the above.
Results may differ from a plain program's by a relative error of at most 0.0059.
Values may be sent and summed in bfloat16 or wider, within the bound.
No kernel may reach another device: no remote copies, remote signals or barrier semaphores. Data moves between devices by JAX's collectives and lax.ppermute only.
A program may use at most 64 MiB of HBM per device.

v0:
```python
import math

import jax
import jax.numpy as jnp
from jax import lax
from jax.sharding import PartitionSpec as P

NDIR = 36


def padded_2(cells, sides, width):
    for axis, dim in sides:
        count = lax.axis_size(axis)
        ends = count - 1
        head = lax.slice_in_dim(cells, 0, width, axis=dim)
        tail = lax.slice_in_dim(cells, cells.shape[dim] - width, cells.shape[dim], axis=dim)
        cells = jnp.concatenate(
            [
                lax.ppermute(tail, axis, [(i, (i + 1) % count) for i in range(ends)]),
                cells,
                lax.ppermute(head, axis, [((i + 1) % count, i) for i in range(ends)]),
            ],
            axis=dim,
        )
    return cells


def finish(row_data, transfer, wind_rows, wind_angle):
    energy = row_data.astype(jnp.float32)
    total = jnp.mean(energy, axis=0)
    ratio = total / (1.0 + total)
    component = jnp.arange(row_data.shape[0], dtype=jnp.int32)
    heading = 2.0 * math.pi * ((component % NDIR).astype(jnp.float32) + 0.5) / NDIR
    forcing = (
        0.3
        * wind_rows.astype(jnp.float32)[None, :]
        * jnp.maximum(jnp.cos(heading[:, None] - wind_angle.astype(jnp.float32)[None, :]), 0.0)
    )
    result = (
        energy * (1.0 + forcing - 0.5 * ratio[None, :])
        + 0.2 * transfer.astype(jnp.float32) / (1.0 + total)[None, :]
    )
    return result.astype(jnp.bfloat16)


def pair_up(pair_kernel, row_data):
    coupled = jnp.dot(pair_kernel, row_data, preferred_element_type=jnp.float32)
    return (row_data.astype(jnp.float32) * coupled).astype(jnp.bfloat16)


def per_device(
    spectrum,
    sea_map,
    depth_factor,
    wind_speed,
    wind_dir,
    ice_mask,
    owner_map,
    pair_kernel,
    transfer_kernel,
):
    comp_dev, cells_x, cells_y = spectrum.shape
    spec_count = lax.axis_size("spec")
    geo_count = lax.axis_size("geo")
    rows_dev = cells_x * cells_y // spec_count
    capacity = 2 * rows_dev // geo_count
    slot_count = geo_count * capacity
    masked = spectrum * sea_map.astype(jnp.bfloat16)[None, :, :]
    padded = padded_2(masked, (("geo", 1),), 1)
    extended = padded.astype(jnp.float32)
    component = lax.axis_index("spec") * comp_dev + jnp.arange(comp_dev, dtype=jnp.int32)
    frequency = (component // NDIR).astype(jnp.float32)
    heading = 2.0 * math.pi * ((component % NDIR).astype(jnp.float32) + 0.5) / NDIR
    cosine = jnp.cos(heading)[:, None, None]
    sine = jnp.sin(heading)[:, None, None]
    gain = (jnp.float32(1.1) ** (-0.5 * frequency))[:, None, None]
    sea_weight = sea_map.astype(jnp.float32)
    step_x = 0.7 * gain * jnp.abs(cosine) * depth_factor
    step_y = 0.7 * gain * jnp.abs(sine) * depth_factor
    centre = extended[:, 1:-1]
    west_side = extended[:, :-2]
    east_side = extended[:, 2:]
    zeros_y = jnp.zeros((comp_dev, cells_x, 1), jnp.float32)
    south_side = jnp.concatenate([zeros_y, centre[:, :, :-1]], axis=2)
    north_side = jnp.concatenate([centre[:, :, 1:], zeros_y], axis=2)
    upwind_x = jnp.where(cosine > 0, west_side, east_side)
    upwind_y = jnp.where(sine > 0, south_side, north_side)
    advected = centre - step_x * (centre - upwind_x) - step_y * (centre - upwind_y)
    propagated = (advected * sea_weight).astype(jnp.bfloat16)
    flattened = propagated.reshape(comp_dev, cells_x * cells_y)
    row_data = lax.all_to_all(flattened, "spec", split_axis=1, concat_axis=0, tiled=True)
    offset = lax.axis_index("spec") * rows_dev

    def own_rows(values):
        return lax.dynamic_slice_in_dim(values.reshape(-1), offset, rows_dev)

    owners = own_rows(owner_map)
    is_live = 1 - own_rows(ice_mask)
    wind_rows = own_rows(wind_speed)
    wind_angle = own_rows(wind_dir)
    onehot = (owners[:, None] == jnp.arange(geo_count, dtype=jnp.int32)[None, :]).astype(
        jnp.int32
    ) * is_live[:, None]
    before = jnp.cumsum(onehot, axis=0) - onehot
    position = jnp.sum(before * onehot, axis=1)
    slot_index = jnp.where(is_live == 1, owners * capacity + position, slot_count)
    source = (
        jnp.full((slot_count,), rows_dev, jnp.int32)
        .at[slot_index]
        .set(jnp.arange(rows_dev, dtype=jnp.int32), mode="drop")
    )
    filled = source < rows_dev
    source_clip = jnp.minimum(source, rows_dev - 1)
    slot_clip = jnp.minimum(slot_index, slot_count - 1)

    def to_slots(values):
        return jnp.where(
            filled[None, :], jnp.take(values, source_clip, axis=1), jnp.zeros((), values.dtype)
        )

    own_kernel = transfer_kernel[0]
    outgoing = to_slots(row_data)
    wind_slots = to_slots(jnp.stack([wind_rows, wind_angle]))
    arrived, arrived_wind = (
        lax.all_to_all(outgoing, "geo", split_axis=1, concat_axis=1, tiled=True),
        lax.all_to_all(wind_slots, "geo", split_axis=1, concat_axis=1, tiled=True),
    )
    paired = pair_up(pair_kernel, arrived)
    transfer = jnp.dot(own_kernel, paired, preferred_element_type=jnp.float32).astype(jnp.bfloat16)
    sourced = finish(arrived, transfer, arrived_wind[0], arrived_wind[1])
    returned = lax.all_to_all(sourced, "geo", split_axis=1, concat_axis=1, tiled=True)
    result = jnp.where(is_live[None, :] == 1, jnp.take(returned, slot_clip, axis=1), row_data)
    restored = lax.all_to_all(result, "spec", split_axis=0, concat_axis=1, tiled=True)
    return restored.reshape(comp_dev, cells_x, cells_y)


def solution(mesh):
    placed = (
        P("spec", "geo", None),
        P("geo", None),
        P("geo", None),
        P("geo", None),
        P("geo", None),
        P("geo", None),
        P("geo", None),
        P(),
        P("geo", None, None),
    )
    return jax.shard_map(
        per_device, mesh=mesh, in_specs=placed, out_specs=P("spec", "geo", None), check_vma=False
    )
```

profile of v0, /device:TPU:1, one launch (start us, length us, event | category | flops | bytes accessed | tf_op | source)
XLA Modules:
  0.0 251.4 jit_solution(13381321650262986688)
XLA Ops:
  0.0 0.0 copy-start.4
  0.0 0.8 fusion.40
  0.8 1.7 copy_multiply_fusion
  2.5 2.0 collective-permute-start.1
  4.4 4.5 %collective-permute-start = (bf16[324,1,128]{2,0,1:T(8,128)(2,1)S(1)}, bf16[324,1,128]{2,0,1:T(8,128)(2,1)S(1)}, u32[]{:S(2)}, u32[]{:S(2)}) collective-permute-start(bf16[324,1,128]{2,0,1:T(8,128)(2,1)S(1)} %get-tuple-element.10), channel_id=1, source_target_pairs={{0,1},{1,2},{2,3},{3,4},{4,5},{5,6},{6,7},{8,9},{9,10},{10,11},{11... | collective-permute-start | bytes 248840 | tf_op jit(solution)/shard_map/ppermute | solution.py:19
  9.0 0.0 copy-done.4
  9.0 0.1 fusion.44
  9.1 0.1 dynamic-slice_subtract_fusion
  9.2 0.0 copy-done.3
  9.2 0.1 dynamic-slice_bitcast_fusion
  9.2 0.1 dynamic_slice.13
  9.3 0.1 abs_multiply_fusion
  9.4 1.1 reduce-window.6
  10.5 0.2 slice_reduce_fusion
  10.8 0.1 fusion.15
  10.9 0.1 compare_and_fusion
  11.0 0.8 dynamic_slice.15
  11.7 0.8 dynamic_slice.14
  12.5 0.1 broadcast_compare_fusion
  12.6 0.0 collective-permute-done.1
  12.6 0.0 collective-permute-done
  12.6 0.2 maximum_convert_fusion
  12.8 0.0 copy-start.2
  12.9 0.9 fusion.38
  13.7 0.0 copy-done.2
  13.7 1.9 fusion.9
  15.6 0.2 copy.45
  15.8 0.5 all_to_all.42
  16.4 1.4 copy.46
  17.7 3.5 %all-to-all-start = ((bf16[324,4,512]{2,0,1:T(8,128)(2,1)}), bf16[324,4,512]{2,0,1:T(8,128)(2,1)S(1)}, u32[]{:S(2)}, u32[]{:S(2)}) async-start(bf16[324,4,512]{2,0,1:T(8,128)(2,1)} %copy.46), calls=%async_computation | async-start | bytes 2686976 | tf_op jit(solution)/shard_map/all_to_all | solution.py:91
  21.3 0.2 copy.50
  21.5 0.1 compare_select_fusion.1
  21.6 2.4 scatter_custom_fusion
  24.0 3.2 %gather_fusion.1 = bf16[1024,2]{1,0:T(8,128)(2,1)S(1)} fusion(bf16[2,512]{0,1:T(8,128)(2,1)S(1)} %copy.50, s32[1024]{0:T(1024)S(1)} %fusion.24), kind=kCustom, calls=%fused_computation.1 | custom fusion | bytes 12288 | tf_op jit(solution)/shard_map/jit(_take)/gather | solution.py:118
  27.3 0.1 copy.51
  27.4 0.6 broadcast_select_fusion.1
  28.0 10.5 %all-to-all-done = bf16[324,4,512]{2,0,1:T(8,128)(2,1)S(1)} async-done(((bf16[324,4,512]{2,0,1:T(8,128)(2,1)}), bf16[324,4,512]{2,0,1:T(8,128)(2,1)S(1)}, u32[]{:S(2)}, u32[]{:S(2)}) %all-to-all-start) | async-done | bytes 1327136 | tf_op jit(solution)/shard_map/all_to_all | solution.py:91
  38.6 4.3 %all-to-all-start.2 = ((bf16[2,8,128]{2,0,1:T(2,128)(2,1)}), bf16[2,8,128]{2,0,1:T(2,128)(2,1)S(1)}, u32[]{:S(2)}, u32[]{:S(2)}) async-start(bf16[2,8,128]{2,0,1:T(2,128)(2,1)} %broadcast_select_fusion.1), calls=%async_computation.2 | async-start | bytes 8192 | tf_op jit(solution)/shard_map/all_to_all | solution.py:126
  42.8 0.0 copy-done
  42.8 0.3 all_to_all.45
  43.1 0.8 copy.47
  43.9 5.6 %gather_fusion = bf16[1024,1296]{1,0:T(8,128)(2,1)} fusion(bf16[1296,512]{0,1:T(8,128)(2,1)S(1)} %copy.47, s32[1024]{0:T(1024)S(1)} %fusion.24), kind=kCustom, calls=%fused_computation | custom fusion | bytes 5312512 | tf_op jit(solution)/shard_map/jit(_take)/gather | solution.py:118
  49.5 3.3 %copy.48 = bf16[1296,8,128]{2,0,1:T(8,128)(2,1)S(1)} copy(bf16[1296,8,128]{0,2,1:T(8,128)(2,1)} %bitcast.76) | data formatting | bytes 5308416 | tf_op jit(solution)/shard_map/jit(_take)/gather | solution.py:118
  52.9 1.8 select_select_fusion
  54.7 0.0 all-to-all-done.2
  54.7 5.1 %all-to-all-start.1 = ((bf16[1296,8,128]{2,0,1:T(8,128)(2,1)}), bf16[1296,8,128]{2,0,1:T(8,128)(2,1)S(1)}, u32[]{:S(2)}, u32[]{:S(2)}) async-start(bf16[1296,8,128]{2,0,1:T(8,128)(2,1)} %select_select_fusion), calls=%async_computation.1 | async-start | bytes 5308416 | tf_op jit(solution)/shard_map/all_to_all | solution.py:125
  59.9 60.1 %all-to-all-done.1 = bf16[1296,8,128]{2,0,1:T(8,128)(2,1)S(1)} async-done(((bf16[1296,8,128]{2,0,1:T(8,128)(2,1)}), bf16[1296,8,128]{2,0,1:T(8,128)(2,1)S(1)}, u32[]{:S(2)}, u32[]{:S(2)}) %all-to-all-start.1) | async-done | bytes 2654240 | tf_op jit(solution)/shard_map/all_to_all | solution.py:125
  119.9 0.4 convert_reduce_fusion
  120.3 0.0 copy-start.5
  120.3 6.7 %fusion.2 = bf16[1296,1024]{1,0:T(8,128)(2,1)S(1)} fusion(bf16[1296,1296]{1,0:T(8,128)(2,1)} %param.16, bf16[1296,8,128]{2,0,1:T(8,128)(2,1)S(1)} %all-to-all-done.1), kind=kOutput, calls=%fused_computation.8 | convolution fusion | flops 3443834880 | bytes 8667648 | tf_op jit(solution)/shard_map/dot_general | solution.py:47
  127.0 0.0 copy-done.5
  127.0 22.4 %fusion.12 = bf16[162,8,8,128]{3,2,1,0:T(8,128)(2,1)S(1)} fusion(f32[1024]{0:T(1024)S(1)} %get-tuple-element.17, bf16[1296,1024]{1,0:T(8,128)(2,1)S(1)} %fusion.2, bf16[1,1296,1296]{2,1,0:T(8,128)(2,1)S(1)} %copy-done.5, f32[1024]{0:T(1024)S(1)} %get-tuple-element.16, f32[1024]{0:T(1024)S(1)} %fusion.28, f32[1296]{0:T(1024)S(1)} %fusion.19, ...), kind=kOutput, calls=%fused_computation.23 | convolution fusion | flops 3457105920 | bytes 11343424 | tf_op jit(solution)/shard_map/dot_general | solution.py:129
  149.4 2.0 copy.76
  151.4 5.1 %all-to-all-start.3 = ((bf16[1296,8,128]{2,0,1:T(8,128)(2,1)}), bf16[1296,8,128]{2,0,1:T(8,128)(2,1)}, u32[]{:S(2)}, u32[]{:S(2)}) async-start(bf16[1296,8,128]{2,0,1:T(8,128)(2,1)} %bitcast.73), calls=%async_computation.3 | async-start | bytes 5308416 | tf_op jit(solution)/shard_map/all_to_all | solution.py:131
  156.5 60.3 %all-to-all-done.3 = bf16[1296,8,128]{2,0,1:T(8,128)(2,1)} async-done(((bf16[1296,8,128]{2,0,1:T(8,128)(2,1)}), bf16[1296,8,128]{2,0,1:T(8,128)(2,1)}, u32[]{:S(2)}, u32[]{:S(2)}) %all-to-all-start.3) | async-done | bytes 2654240 | tf_op jit(solution)/shard_map/all_to_all | solution.py:131
  216.8 3.3 %copy.55 = bf16[1296,8,128]{0,2,1:T(8,128)(2,1)S(1)} copy(bf16[1296,8,128]{2,0,1:T(8,128)(2,1)} %all-to-all-done.3) | data formatting | bytes 5308416 | tf_op jit(solution)/shard_map/all_to_all | solution.py:131
  220.1 2.9 %gather_fusion.2 = bf16[512,1296]{1,0:T(8,128)(2,1)} fusion(bf16[1296,1024]{0,1:T(8,128)(2,1)S(1)} %bitcast.74, s32[1024]{0:T(1024)S(1)} %pad_clamp_fusion), kind=kCustom, calls=%fused_computation.2 | custom fusion | bytes 2656256 | tf_op jit(solution)/shard_map/jit(_take)/gather | solution.py:132
  223.0 3.8 %reshape.234 = bf16[4,324,512]{1,0,2:T(4,128)(2,1)S(1)} reshape(bf16[1296,512]{0,1:T(8,128)(2,1)} %bitcast.78) | data formatting | bytes 2654208 | tf_op jit(solution)/shard_map/jit(_take)/gather | solution.py:132
  226.8 2.5 copy.58
  229.2 0.0 copy-done.1
  229.3 1.5 select_select_fusion.1
  230.7 18.6 %all_to_all.59 = bf16[4,324,512]{2,1,0:T(8,128)(2,1)S(1)} all-to-all(bf16[4,324,512]{2,1,0:T(8,128)(2,1)S(1)} %select_select_fusion.1), channel_id=1, replica_groups=mesh['spec'=4,'geo'=8] {'spec'}, dimensions={0} | all-to-all | bytes 2654208 | tf_op jit(solution)/shard_map/all_to_all | solution.py:133
  249.4 0.7 copy.57
  250.1 1.4 reshape.196
  (19 shorter events, 0.2 us)
Async XLA Ops:
  0.0 9.0 %copy-start.4 = (s32[16,128]{1,0:T(8,128)S(1)}, s32[16,128]{1,0:T(8,128)}, u32[]{:S(2)}) copy-start(s32[16,128]{1,0:T(8,128)} %param.14) | copy-start | bytes 24580
  0.0 9.2 %copy-start.3 = (s32[16,128]{1,0:T(8,128)S(1)}, s32[16,128]{1,0:T(8,128)}, u32[]{:S(2)}) copy-start(s32[16,128]{1,0:T(8,128)} %param.15) | copy-start | bytes 24580
  2.5 10.1 %collective-permute-start.1 = (bf16[324,1,128]{2,0,1:T(8,128)(2,1)S(1)}, bf16[324,1,128]{2,0,1:T(8,128)(2,1)S(1)}, u32[]{:S(2)}, u32[]{:S(2)}) collective-permute-start(bf16[324,1,128]{2,0,1:T(8,128)(2,1)S(1)} %get-tuple-element.11), channel_id=1, source_target_pairs={{1,0},{2,1},{3,2},{4,3},{5,4},{6,5},{7,6},{9,8},{10,9},{11,10},{12... | collective-permute-start | bytes 248840 | tf_op jit(solution)/shard_map/ppermute | solution.py:21
  4.4 8.1 %collective-permute-start = (bf16[324,1,128]{2,0,1:T(8,128)(2,1)S(1)}, bf16[324,1,128]{2,0,1:T(8,128)(2,1)S(1)}, u32[]{:S(2)}, u32[]{:S(2)}) collective-permute-start(bf16[324,1,128]{2,0,1:T(8,128)(2,1)S(1)} %get-tuple-element.10), channel_id=1, source_target_pairs={{0,1},{1,2},{2,3},{3,4},{4,5},{5,6},{6,7},{8,9},{9,10},{10,11},{11... | collective-permute-start | bytes 248840 | tf_op jit(solution)/shard_map/ppermute | solution.py:19
  12.8 0.9 copy-start.2
  17.7 20.8 %all-to-all-start = ((bf16[324,4,512]{2,0,1:T(8,128)(2,1)}), bf16[324,4,512]{2,0,1:T(8,128)(2,1)S(1)}, u32[]{:S(2)}, u32[]{:S(2)}) async-start(bf16[324,4,512]{2,0,1:T(8,128)(2,1)} %copy.46), calls=%async_computation | async-start | bytes 2686976 | tf_op jit(solution)/shard_map/all_to_all | solution.py:91
  38.6 4.3 %copy-start = (bf16[324,4,512]{2,0,1:T(8,128)(2,1)}, bf16[324,4,512]{2,0,1:T(8,128)(2,1)S(1)}, u32[]{:S(2)}) copy-start(bf16[324,4,512]{2,0,1:T(8,128)(2,1)S(1)} %all-to-all-done) | copy-start | bytes 3981316
  38.6 16.1 %all-to-all-start.2 = ((bf16[2,8,128]{2,0,1:T(2,128)(2,1)}), bf16[2,8,128]{2,0,1:T(2,128)(2,1)S(1)}, u32[]{:S(2)}, u32[]{:S(2)}) async-start(bf16[2,8,128]{2,0,1:T(2,128)(2,1)} %broadcast_select_fusion.1), calls=%async_computation.2 | async-start | bytes 8192 | tf_op jit(solution)/shard_map/all_to_all | solution.py:126
  54.7 65.2 %all-to-all-start.1 = ((bf16[1296,8,128]{2,0,1:T(8,128)(2,1)}), bf16[1296,8,128]{2,0,1:T(8,128)(2,1)S(1)}, u32[]{:S(2)}, u32[]{:S(2)}) async-start(bf16[1296,8,128]{2,0,1:T(8,128)(2,1)} %select_select_fusion), calls=%async_computation.1 | async-start | bytes 5308416 | tf_op jit(solution)/shard_map/all_to_all | solution.py:125
  120.3 6.7 %copy-start.5 = (bf16[1,1296,1296]{2,1,0:T(8,128)(2,1)S(1)}, bf16[1,1296,1296]{2,1,0:T(8,128)(2,1)}, u32[]{:S(2)}) copy-start(bf16[1,1296,1296]{2,1,0:T(8,128)(2,1)} %param.17) | copy-start | bytes 10077700
  151.4 65.4 %all-to-all-start.3 = ((bf16[1296,8,128]{2,0,1:T(8,128)(2,1)}), bf16[1296,8,128]{2,0,1:T(8,128)(2,1)}, u32[]{:S(2)}, u32[]{:S(2)}) async-start(bf16[1296,8,128]{2,0,1:T(8,128)(2,1)} %bitcast.73), calls=%async_computation.3 | async-start | bytes 5308416 | tf_op jit(solution)/shard_map/all_to_all | solution.py:131
  223.0 6.3 %copy-start.1 = (bf16[324,4,512]{2,0,1:T(8,128)(2,1)S(1)}, bf16[324,4,512]{2,0,1:T(8,128)(2,1)}, u32[]{:S(2)}) copy-start(bf16[324,4,512]{2,0,1:T(8,128)(2,1)} %copy-done) | copy-start | bytes 3981316
where the time goes:
time: 254 us; the launch traced here: 251 us
  waiting for transfers between devices  131 us (52%)
  local copies, waits for them, and re-layouts  37.3 us (15%)
  matrix products  29.1 us (11%)
  starting transfers between devices  24.6 us (10%)
  blocking collectives  18.6 us (7%)
  other arithmetic  10.7 us (4%)
    all_to_all x1, waiting for transfers between devices, per_device(): lax.all_to_all(sourced, 'geo', split_axis=1, concat_axis=1, tiled=True)  60.3 us
    all_to_all x1, waiting for transfers between devices, per_device(): lax.all_to_all(outgoing, 'geo', split_axis=1, concat_axis=1, tiled=True)  60.1 us
    dot_general x1, matrix products, per_device(): jnp.dot(own_kernel, paired, preferred_element_type=jnp.float32)  22.4 us
    all_to_all x1, blocking collectives, per_device(): lax.all_to_all(result, 'spec', split_axis=0, concat_axis=1, tiled=True)  18.6 us
    gather x4, local copies, waits for them, and re-layouts, to_slots(): jnp.take(values, source_clip, axis=1)  12.3 us
    all_to_all x1, waiting for transfers between devices, per_device(): lax.all_to_all(flattened, 'spec', split_axis=1, concat_axis=0, tiled=True)  10.5 us
    gather x3, local copies, waits for them, and re-layouts, per_device(): jnp.take(returned, slot_clip, axis=1)  9.17 us
    dot_general x1, matrix products, pair_up(): coupled = jnp.dot(pair_kernel, row_data, preferred_element_type=jnp.float32)  6.68 us
  transfers between devices with their start and end apart: 6, of which 3 were waited for; matrix products, arithmetic and copies ran while one was open for 9% of the time, Pallas kernels for 0%

commit v1 on v0

v1 whole, which is shorter than its diff:
```python
import functools
import math

import jax
import jax.numpy as jnp
from jax import lax
from jax.experimental import pallas as pl
from jax.experimental.pallas import tpu as pltpu
from jax.sharding import Mesh
from jax.sharding import PartitionSpec as P

NDIR = 36
PLANES = 4
SUB = 16
VMEM = pl.BlockSpec(memory_space=pltpu.VMEM)
SMEM = pl.BlockSpec(memory_space=pltpu.SMEM)
BF16 = jnp.bfloat16
F32 = jnp.float32


def params(mib=14):
    return pltpu.CompilerParams(vmem_limit_bytes=mib * 2**20)


def propagate_kernel(wanted, x_ref, west_ref, east_ref, sea_ref, depth_ref, coef_ref, out_ref):
    rows, comps, width = x_ref.shape

    def tile(at, height):
        lane = lax.broadcasted_iota(jnp.int32, (height, width), 1)
        coef = coef_ref[at, :]
        gain_x, gain_y, pos_x, pos_y = (
            jnp.broadcast_to(coef[:, i : i + 1], (height, width)) for i in range(4)
        )
        from_west, from_south = pos_x > 0, pos_y > 0
        first, last = lane == 0, lane == width - 1
        known = {}

        def masked(row):
            if row not in known:
                if row < 0:
                    known[row] = west_ref[at, :].astype(F32)
                elif row == rows:
                    known[row] = east_ref[at, :].astype(F32)
                else:
                    known[row] = x_ref[row, at, :].astype(F32) * sea_ref[row : row + 1, :]
            return known[row]

        for k, row in enumerate(wanted):
            west, centre, east = masked(row - 1), masked(row), masked(row + 1)
            upwind_x = jnp.where(from_west, west, east)
            south = jnp.where(first, 0.0, pltpu.roll(centre, 1, 1))
            north = jnp.where(last, 0.0, pltpu.roll(centre, width - 1, 1))
            upwind_y = jnp.where(from_south, south, north)
            depth = depth_ref[row : row + 1, :]
            moved = (
                centre
                - gain_x * depth * (centre - upwind_x)
                - gain_y * depth * (centre - upwind_y)
            )
            out_ref[at, k * width : (k + 1) * width] = (
                moved * sea_ref[row : row + 1, :]
            ).astype(BF16)

    def body(step, carry):
        tile(pl.ds(pl.multiple_of(step * SUB, SUB), SUB), SUB)
        return carry

    whole = comps // SUB
    lax.fori_loop(0, whole, body, 0)
    if comps % SUB:
        spare = out_ref.shape[0] - whole * SUB
        out_ref[whole * SUB :, :] = jnp.zeros((spare, out_ref.shape[1]), BF16)
        tile(slice(whole * SUB, comps), comps - whole * SUB)


def propagate(wanted, x, west, east, sea, depth, coef):
    comps, width = x.shape[1:]
    padded = -(-comps // SUB) * SUB
    cells = len(wanted) * width
    return pl.pallas_call(
        functools.partial(propagate_kernel, wanted),
        out_shape=jax.ShapeDtypeStruct((padded, cells), BF16),
        in_specs=[VMEM] * 6,
        out_specs=VMEM,
        compiler_params=params(),
        cost_estimate=pl.CostEstimate(
            flops=2 * comps * cells, bytes_accessed=comps * cells, transcendentals=0
        ),
    )(x, west, east, sea, depth, coef)


def pair_kernel_body(tile, comps, here_ref, *refs):
    *parts, pair_ref, out_ref, mean_ref, whole = refs
    step = pl.program_id(0)

    @pl.when(step == 0)
    def _():
        for here in range(4):

            @pl.when(here_ref[0] == here)
            def _(here=here):
                for flip, part in enumerate(parts[:3]):
                    at = (here ^ flip) * comps
                    whole[at : at + comps, :] = part[:comps, :]
                at, column = (here ^ 3) * comps, 0
                for part in parts[3:]:
                    width = part.shape[1]
                    whole[at : at + comps, column : column + width] = part[:comps, :]
                    column += width

        total = jnp.sum(whole[...].astype(F32), axis=0, keepdims=True)
        mean_ref[...] = total / whole.shape[0]

    coupled = jnp.dot(pair_ref[...], whole[...], preferred_element_type=F32)
    own = whole[pl.ds(pl.multiple_of(step * tile, SUB), tile), :]
    out_ref[...] = (own.astype(F32) * coupled).astype(BF16)


def pair_up(here, parts, pair, tile=432):
    comps, cells = pair.shape[0], parts[0].shape[1]
    specs = [pl.BlockSpec(part.shape, lambda i: (0, 0)) for part in parts]
    return pl.pallas_call(
        functools.partial(pair_kernel_body, tile, comps // 4),
        grid=(comps // tile,),
        out_shape=[jax.ShapeDtypeStruct((comps, cells), BF16), jax.ShapeDtypeStruct((1, cells), F32)],
        in_specs=[SMEM] + specs + [pl.BlockSpec((tile, comps), lambda i: (i, 0))],
        out_specs=[
            pl.BlockSpec((tile, cells), lambda i: (i, 0)),
            pl.BlockSpec((1, cells), lambda i: (0, 0)),
        ],
        scratch_shapes=[pltpu.VMEM((comps, cells), BF16)],
        compiler_params=params(),
        cost_estimate=pl.CostEstimate(
            flops=comps * comps * cells // 4, bytes_accessed=comps * comps // 4, transcendentals=0
        ),
    )(here, *parts, pair)


def apply_owned(ids_ref, owner, paired, kernels, held):
    for number, kernel in enumerate(kernels):
        term = jnp.dot(kernel[...], paired, preferred_element_type=F32)
        held = jnp.where(owner == ids_ref[number], term, held)
    return held


def listed(found):
    return jnp.stack([owner for _, owner in found]).astype(jnp.int32), [k for k, _ in found]


def split(refs, *sizes):
    out, at = [], 0
    for size in sizes:
        out.append(refs[at : at + size])
        at += size
    return out


def transfer_body(count, chunks, first, ids_ref, *refs):
    kernels, owners, paired, held, outs = split(
        refs, count, chunks, chunks, 0 if first else chunks, chunks
    )
    for chunk, out_ref in enumerate(outs):
        value = jnp.zeros(out_ref.shape, F32) if first else held[chunk][...].astype(F32)
        value = apply_owned(ids_ref, owners[chunk][...], paired[chunk][...], kernels, value)
        out_ref[...] = value.astype(BF16)


def transfer_cost(kernels, paired):
    flops = len(kernels) * kernels[0].size * sum(p.shape[1] for p in paired)
    moved = 2 * (len(kernels) * kernels[0].size + sum(p.size for p in paired))
    return pl.CostEstimate(flops=flops // 4, bytes_accessed=moved // 8, transcendentals=0)


def transfer_part(found, owners, paired, held):
    ids, kernels = listed(found)
    operands = [*kernels, *owners, *paired, *(held or [])]
    shapes = [jax.ShapeDtypeStruct((kernels[0].shape[0], p.shape[1]), BF16) for p in paired]
    return pl.pallas_call(
        functools.partial(transfer_body, len(kernels), len(paired), held is None),
        out_shape=shapes,
        in_specs=[SMEM] + [VMEM] * len(operands),
        out_specs=[VMEM] * len(shapes),
        compiler_params=params(),
        cost_estimate=transfer_cost(kernels, paired),
    )(ids, *operands)


def transfer(found, owners, paired, held, most=6):
    for at in range(0, len(found), most):
        held = transfer_part(found[at : at + most], owners, paired, held)
    return list(held)


def finish_body(count, groups, ids_ref, angle_ref, *refs):
    chunks = len(groups)
    kernels, owners, cell_rows, paired, held, parts, (out_ref,) = split(
        refs, count, chunks, chunks, chunks, chunks, chunks, 1
    )
    comps, width = out_ref.shape[1:]
    cosine, sine = angle_ref[:comps, 0:1], angle_ref[:comps, 1:2]
    for chunk in range(chunks):
        term = apply_owned(
            ids_ref, owners[chunk][...], paired[chunk][...], kernels, held[chunk][...].astype(F32)
        )
        term = term.astype(BF16).astype(F32)
        total, along, across, ice = (cell_rows[chunk][i : i + 1, :] for i in range(4))
        shrink = 1.0 / (1.0 + total)
        base = 1.0 - 0.5 * total * shrink
        energy = parts[chunk][:comps, :].astype(F32)
        forcing = jnp.maximum(cosine * along + sine * across, 0.0)
        result = energy * (base + forcing) + (0.2 * shrink) * term
        result = jnp.where(ice > 0, energy, result).astype(BF16)
        for k, row in enumerate(groups[chunk]):
            out_ref[row] = result[:, k * width : (k + 1) * width]


def finish(groups, found, owners, cell_rows, angles, paired, held, parts, width):
    ids, kernels = listed(found)
    comps = kernels[0].shape[0]
    operands = [angles, *kernels, *owners, *cell_rows, *paired, *held, *parts]
    return pl.pallas_call(
        functools.partial(finish_body, len(kernels), groups),
        out_shape=jax.ShapeDtypeStruct((sum(map(len, groups)), comps, width), BF16),
        in_specs=[SMEM] + [VMEM] * len(operands),
        out_specs=VMEM,
        compiler_params=params(),
        cost_estimate=transfer_cost(kernels, paired),
    )(ids, *operands)


def next_plane(value):
    return lax.ppermute(value, "plane", [(i, (i + 1) % PLANES) for i in range(PLANES)])


def boundaries(top, bottom):
    places = lax.axis_size("place")
    geo, count = ("plane", "place"), PLANES * places
    if places != 2:
        return (
            lax.ppermute(bottom, geo, [(i, i + 1) for i in range(count - 1)]),
            lax.ppermute(top, geo, [(i + 1, i) for i in range(count - 1)]),
        )
    first = lax.axis_index("place") == 0
    inside = lax.ppermute(jnp.where(first, bottom, top), "place", [(0, 1), (1, 0)])
    pairs = [(i, i + 1) for i in range(1, count - 1, 2)]
    outside = lax.ppermute(jnp.where(first, top, bottom), geo, pairs + [(j, i) for i, j in pairs])
    return inside, outside


def before_and_after(inside, outside):
    if lax.axis_size("place") != 2:
        return inside, outside
    first = lax.axis_index("place") == 0
    return jnp.where(first, outside, inside), jnp.where(first, inside, outside)


def with_partners(kernel, steps):
    count = lax.axis_size("place")
    plane, place = lax.axis_index("plane"), lax.axis_index("place")
    plane = lax.rem(plane + PLANES - steps, PLANES)
    found = [(kernel, plane * count + place)]
    for shift in range(1, count):
        pairs = [(i, (i + shift) % count) for i in range(count)]
        origin = lax.rem(place - shift + count, count)
        found.append((lax.ppermute(kernel, "place", pairs), plane * count + origin))
    return found


def send_spec(value, flip):
    return lax.ppermute(value, "spec", [(i, i ^ flip) for i in range(4)])


def per_device(
    spectrum,
    sea_map,
    depth_factor,
    wind_speed,
    wind_dir,
    ice_mask,
    owner_map,
    pair_kernel,
    transfer_kernel,
):
    comps, rows, width = spectrum.shape
    here = lax.axis_index("spec")

    own_rows = lax.dynamic_slice_in_dim(transfer_kernel[0], here * comps, comps, axis=0)
    one_back = next_plane(own_rows)
    sea = sea_map.astype(F32)
    top = spectrum[:, 0] * sea_map[0].astype(BF16)
    bottom = spectrum[:, rows - 1] * sea_map[rows - 1].astype(BF16)
    halos = boundaries(top, bottom)
    x = spectrum.transpose(1, 0, 2)

    component = here * comps + jnp.arange(comps, dtype=jnp.int32)
    frequency = (component // NDIR).astype(F32)
    heading = 2.0 * math.pi * ((component % NDIR).astype(F32) + 0.5) / NDIR
    cosine, sine = jnp.cos(heading), jnp.sin(heading)
    gain = jnp.float32(1.1) ** (-0.5 * frequency)
    coef = jnp.stack(
        [
            0.7 * gain * jnp.abs(cosine),
            0.7 * gain * jnp.abs(sine),
            (cosine > 0).astype(F32),
            (sine > 0).astype(F32),
        ],
        axis=1,
    )
    angles = jnp.stack([cosine, sine], axis=1)

    here_ref = jnp.reshape(here, (1,)).astype(jnp.int32)
    speed = 0.3 * wind_speed.astype(F32)
    along = speed * jnp.cos(wind_dir.astype(F32))
    across = speed * jnp.sin(wind_dir.astype(F32))
    wide = 3 * rows // 8
    one, two = 1 + wide, 1 + 2 * wide
    groups = [list(range(1, one)), list(range(one, two)), [0] + list(range(two, rows))]

    def cells_of(values):
        ends = jnp.concatenate([values[:1], values[two:]])
        return [v.reshape(1, -1) for v in (values[1:one], values[one:two], ends)]

    owners = cells_of(owner_map)
    extras = [cells_of(v) for v in (along, across, ice_mask.astype(F32))]

    def meet(part):
        return [send_spec(part, 1), send_spec(part, 2)]

    def pair_group(number, sets):
        paired, total = pair_up(here_ref, sets, pair_kernel)
        return paired, jnp.concatenate([total] + [extra[number] for extra in extras])

    none = jnp.zeros_like(top)
    parts = [
        propagate(group, x, none, none, sea, depth_factor, coef) for group in groups[:2]
    ]
    near = [meet(parts[0])]
    near[0], parts[1] = lax.optimization_barrier((near[0], parts[1]))
    near.append(meet(parts[1]))
    one_back, halos, near = lax.optimization_barrier((one_back, halos, near))

    two_back = next_plane(one_back)
    crossed = [send_spec(near[0][1], 1), send_spec(near[1][0], 2)]
    parts.append(
        propagate(groups[2], x, *before_and_after(*halos), sea, depth_factor, coef)
    )
    crossed, parts[2] = lax.optimization_barrier((crossed, parts[2]))
    near.append(meet(parts[2]))
    paired, cell_rows = [None] * 3, [None] * 3
    for i in range(2):
        paired[i], cell_rows[i] = pair_group(i, [parts[i], *near[i], crossed[i]])
    found = with_partners(own_rows, 0) + with_partners(one_back, 1)
    two_back, near, paired[:2] = lax.optimization_barrier((two_back, near, paired[:2]))

    three_back = next_plane(two_back)
    half = parts[2].shape[1] // 2
    crossed_last = [send_spec(near[2][1][:, :half], 1), send_spec(near[2][0][:, half:], 2)]
    held = transfer(found, owners[:2], paired[:2], None)
    held, crossed_last = lax.optimization_barrier((held, crossed_last))
    paired[2], cell_rows[2] = pair_group(2, [parts[2], *near[2], *crossed_last])
    later = with_partners(two_back, 2)
    held = transfer(later, owners[:2], paired[:2], held)
    held += transfer(found + later, owners[2:], paired[2:], None)
    three_back, held = lax.optimization_barrier((three_back, held))
    last = with_partners(three_back, 3)
    held = transfer(last[:-1], owners, paired, held)
    out = finish(groups, last[-1:], owners, cell_rows, angles, paired, held, parts, width)
    return out.transpose(1, 0, 2)


def solution(mesh):
    spec, geo = mesh.shape["spec"], mesh.shape["geo"]
    split = Mesh(
        mesh.devices.reshape(spec, PLANES, geo // PLANES), ("spec", "plane", "place")
    )
    tiles = ("plane", "place")
    placed = (
        P("spec", tiles, None),
        P(tiles, None),
        P(tiles, None),
        P(tiles, None),
        P(tiles, None),
        P(tiles, None),
        P(tiles, None),
        P(),
        P(tiles, None, None),
    )
    return jax.shard_map(
        per_device, mesh=split, in_specs=placed, out_specs=P("spec", tiles, None), check_vma=False
    )
```

time: 254 us -> 115 us (0.45)
  waiting for transfers between devices: 131 us -> 21.8 us
  Pallas kernels: 0 us -> 49.2 us
  matrix products: 29.1 us -> 0 us
  blocking collectives: 18.6 us -> 0 us
  local copies, waits for them, and re-layouts: 37.3 us -> 20.6 us
  other arithmetic: 10.7 us -> 2.19 us
  starting transfers between devices: 24.6 us -> 19.7 us
    all_to_all x4 -> x0, waiting for transfers between devices: 131 us -> none  [the longest x1 60.3 us: per_device(): lax.all_to_all(sourced, 'geo', split_axis=1, concat_axis=1, tiled=True)]
    pallas_call x0 -> x11, Pallas kernels: none -> 49.2 us  [the longest x4 22.8 us: transfer_part(): pl.pallas_call(functools.partial(transfer_body, len(kernels), len(paired)...]
    dot_general x2 -> x0, matrix products: 29.1 us -> none  [the longest x1 22.4 us: per_device(): jnp.dot(own_kernel, paired, preferred_element_type=jnp.float32)]
    ppermute x2 -> x19, waiting for transfers between devices: 0.01 us -> 21.8 us  [the longest x10 14.3 us: send_spec(): return lax.ppermute(value, 'spec', [(i, i ^ flip) for i in range(4)])]
    gather x7 -> x0, local copies, waits for them, and re-layouts: 21.4 us -> none  [the longest x4 12.3 us: to_slots(): jnp.take(values, source_clip, axis=1)]
    all_to_all x1 -> x0, blocking collectives: 18.6 us -> none  [per_device(): lax.all_to_all(result, 'spec', split_axis=0, concat_axis=1, tiled=True)]
    all_to_all x4 -> x0, starting transfers between devices: 18 us -> none  [the longest x1 5.14 us: per_device(): lax.all_to_all(sourced, 'geo', split_axis=1, concat_axis=1, tiled=True)]
    unnamed x12 -> x80, local copies, waits for them, and re-layouts: 0.03 us -> 15.6 us
  transfers between devices with their start and end apart: 6 -> 19, of which waited for: 3 -> 4; matrix products, arithmetic and copies ran while one was open for 9% -> 5% of each run, Pallas kernels for 0% -> 37%
where the time goes in v1:
time: 115 us; the launch traced here: 114 us
  Pallas kernels  49.2 us (43%)
  waiting for transfers between devices  21.8 us (19%)
  local copies, waits for them, and re-layouts  20.6 us (18%)
  starting transfers between devices  19.7 us (17%)
  other arithmetic  2.19 us (2%)
    pallas_call x4, Pallas kernels, transfer_part(): pl.pallas_call(functools.partial(transfer_body, len(kernels), len(paired)...  22.8 us
    unnamed x80, local copies, waits for them, and re-layouts  15.6 us
    pallas_call x3, Pallas kernels, pair_up(): pl.pallas_call(functools.partial(pair_kernel_body, tile, comps // 4), gri...  15.3 us
    ppermute x10, waiting for transfers between devices, send_spec(): return lax.ppermute(value, 'spec', [(i, i ^ flip) for i in range(4)])  14.3 us
    ppermute x10, starting transfers between devices, send_spec(): return lax.ppermute(value, 'spec', [(i, i ^ flip) for i in range(4)])  8.55 us
    ppermute x1, waiting for transfers between devices, boundaries(): lax.ppermute(jnp.where(first, top, bottom), geo, pairs + [(j, i) for i, j...  7.42 us
    pallas_call x3, Pallas kernels, propagate(): pl.pallas_call(functools.partial(propagate_kernel, wanted), out_shape=jax...  6.88 us
    pallas_call x1, Pallas kernels, finish(): pl.pallas_call(functools.partial(finish_body, len(kernels), groups), out_...  4.22 us
  transfers between devices with their start and end apart: 19, of which 4 were waited for; matrix products, arithmetic and copies ran while one was open for 5% of the time, Pallas kernels for 37%

profile of v1, /device:TPU:1, one launch (start us, length us, event | category | flops | bytes accessed | tf_op | source)
XLA Modules:
  0.0 114.2 jit_solution(15178088422219627734)
XLA Ops:
  0.0 0.1 compare_convert_fusion
  0.1 0.1 abs_multiply_fusion
  0.2 0.1 copy.17.coef_ref
  0.3 0.0 copy-start.27
  0.4 1.7 %copy.44 = bf16[324,16,128]{2,0,1:T(8,128)(2,1)S(1)} copy(bf16[324,16,128]{2,1,0:T(8,128)(2,1)} %param.9) | data formatting | bytes 2654208 | tf_op args[0]
  2.2 2.4 %shard_map.91.refs_0_.refs_13_ = bf16[336,768]{1,0:T(8,128)(2,1)S(1)} custom-call(bf16[16,324,128]{2,1,0:T(8,128)(2,1)S(1)} %bitcast.83, bf16[324,128]{1,0:T(8,128)(2,1)S(1)} %broadcast_in_dim.2.west_ref.east_ref, bf16[324,128]{1,0:T(8,128)(2,1)S(1)} %broadcast_in_dim.2.west_ref.east_ref, f32[16,128]{1,0:T(8,128)S(1)} %get-tuple-element.99.sea_ref, ...), custom_call_target="tpu_custom_call" | custom-call | flops 497664 | bytes 248832 | tf_op jit(solution)/shard_map/pallas_call | solution.py:80
  4.6 2.1 %collective-permute-start.3 = (bf16[336,768]{1,0:T(8,128)(2,1)S(1)}, bf16[336,768]{1,0:T(8,128)(2,1)}, u32[]{:S(2)}, u32[]{:S(2)}) collective-permute-start(bf16[336,768]{1,0:T(8,128)(2,1)S(1)} %shard_map.91.refs_0_.refs_13_), channel_id=1, source_target_pairs={{0,8},{8,0},{16,24},{24,16},{1,9},{9,1},{17,25},{25,17},{2,10},{10... | collective-permute-start | bytes 1548296 | tf_op jit(solution)/shard_map/ppermute | solution.py:270
  6.7 1.2 %collective-permute-start.4 = (bf16[336,768]{1,0:T(8,128)(2,1)S(1)}, bf16[336,768]{1,0:T(8,128)(2,1)}, u32[]{:S(2)}, u32[]{:S(2)}) collective-permute-start(bf16[336,768]{1,0:T(8,128)(2,1)S(1)} %shard_map.91.refs_0_.refs_13_), channel_id=1, source_target_pairs={{0,16},{8,24},{16,0},{24,8},{1,17},{9,25},{17,1},{25,9},{2,18},{10... | collective-permute-start | bytes 1548296 | tf_op jit(solution)/shard_map/ppermute | solution.py:270
  7.9 1.4 %dynamic-slice_bitcast_fusion.refs_0_ = bf16[324,1296]{1,0:T(8,128)(2,1)S(1)} fusion(bf16[1,1296,1296]{2,1,0:T(8,128)(2,1)} %param.17, s32[]{:T(128)S(6)} %select_n.74), kind=kLoop, calls=%fused_computation | loop fusion | bytes 1679620 | tf_op jit(solution)/shard_map/dynamic_slice | solution.py:287
  9.4 0.0 copy-start.8
  9.4 1.3 %collective-permute-start = (bf16[324,1296]{1,0:T(8,128)(2,1)S(1)}, bf16[324,1296]{1,0:T(8,128)(2,1)}, u32[]{:S(2)}, u32[]{:S(2)}) collective-permute-start(bf16[324,1296]{1,0:T(8,128)(2,1)S(1)} %dynamic-slice_bitcast_fusion.refs_0_), channel_id=1, source_target_pairs={{0,2},{2,4},{4,6},{6,0},{1,3},{3,5},{5,7},{7,1},{8,10},{10,12},{12... | collective-permute-start | bytes 2519432 | tf_op jit(solution)/shard_map/ppermute | solution.py:232
  10.8 2.4 %shard_map.92.refs_0_.refs_14_ = bf16[336,768]{1,0:T(8,128)(2,1)S(1)} custom-call(bf16[16,324,128]{2,1,0:T(8,128)(2,1)S(1)} %bitcast.84, bf16[324,128]{1,0:T(8,128)(2,1)S(1)} %broadcast_in_dim.2.west_ref.east_ref, bf16[324,128]{1,0:T(8,128)(2,1)S(1)} %broadcast_in_dim.2.west_ref.east_ref, f32[16,128]{1,0:T(8,128)S(1)} %get-tuple-element.99.sea_ref, ...), custom_call_target="tpu_custom_call" | custom-call | flops 497664 | bytes 248832 | tf_op jit(solution)/shard_map/pallas_call | solution.py:80
  13.2 5.1 %collective-permute-done.3.refs_1_ = bf16[336,768]{1,0:T(8,128)(2,1)} collective-permute-done((bf16[336,768]{1,0:T(8,128)(2,1)S(1)}, bf16[336,768]{1,0:T(8,128)(2,1)}, u32[]{:S(2)}, u32[]{:S(2)}) %collective-permute-start.3) | collective-permute-done | bytes 516128 | tf_op jit(solution)/shard_map/ppermute | solution.py:270
  18.3 0.8 collective-permute-done.4.refs_2_
  19.1 0.4 collective-permute-start.5
  19.5 1.2 %collective-permute-start.6 = (bf16[336,768]{1,0:T(8,128)(2,1)S(1)}, bf16[336,768]{1,0:T(8,128)(2,1)}, u32[]{:S(2)}, u32[]{:S(2)}) collective-permute-start(bf16[336,768]{1,0:T(8,128)(2,1)S(1)} %shard_map.92.refs_0_.refs_14_), channel_id=1, source_target_pairs={{0,16},{8,24},{16,0},{24,8},{1,17},{9,25},{17,1},{25,9},{2,18},{10... | collective-permute-start | bytes 1548296 | tf_op jit(solution)/shard_map/ppermute | solution.py:270
  20.7 0.7 broadcast_select_fusion.2
  21.3 2.4 %collective-permute-start.1 = (bf16[324,128]{1,0:T(8,128)(2,1)}, bf16[324,128]{1,0:T(8,128)(2,1)}, u32[]{:S(2)}, u32[]{:S(2)}) collective-permute-start(bf16[324,128]{1,0:T(8,128)(2,1)} %get-tuple-element.84), channel_id=1, source_target_pairs={{0,1},{1,0},{2,3},{3,2},{4,5},{5,4},{6,7},{7,6},{8,9},{9,8},{10,11... | collective-permute-start | bytes 248840 | tf_op jit(solution)/shard_map/ppermute | solution.py:244
  23.7 3.1 %collective-permute-start.2 = (bf16[324,128]{1,0:T(8,128)(2,1)S(1)}, bf16[324,128]{1,0:T(8,128)(2,1)S(1)}, u32[]{:S(2)}, u32[]{:S(2)}) collective-permute-start(bf16[324,128]{1,0:T(8,128)(2,1)S(1)} %get-tuple-element.83), channel_id=1, source_target_pairs={{1,2},{3,4},{5,6},{2,1},{4,3},{6,5},{9,10},{11,12},{13,14},{10,9},... | collective-permute-start | bytes 248840 | tf_op jit(solution)/shard_map/ppermute | solution.py:246
  26.8 0.1 fusion.2
  27.0 0.1 collective-permute-start.14
  27.0 7.4 %collective-permute-done.2 = bf16[324,128]{1,0:T(8,128)(2,1)S(1)} collective-permute-done((bf16[324,128]{1,0:T(8,128)(2,1)S(1)}, bf16[324,128]{1,0:T(8,128)(2,1)S(1)}, u32[]{:S(2)}, u32[]{:S(2)}) %collective-permute-start.2) | collective-permute-done | bytes 82976 | tf_op jit(solution)/shard_map/ppermute | solution.py:246
  34.5 0.3 collective-permute-start.8
  34.8 0.6 collective-permute-start.9
  35.4 0.3 collective-permute-start.7
  35.8 0.1 fusion.8
  35.9 1.0 broadcast_select_fusion
  36.8 0.9 copy-done.20
  37.7 2.1 %shard_map.93.refs_0_.refs_15_ = bf16[336,512]{1,0:T(8,128)(2,1)S(1)} custom-call(bf16[16,324,128]{2,1,0:T(8,128)(2,1)S(1)} %bitcast.85, bf16[324,128]{1,0:T(8,128)(2,1)S(1)} %get-tuple-element.88.west_ref, bf16[324,128]{1,0:T(8,128)(2,1)S(1)} %get-tuple-element.87.east_ref, f32[16,128]{1,0:T(8,128)S(1)} %get-tuple-element.99.sea_ref, ...), custom_call_target="tpu_custom_call" | custom-call | flops 331776 | bytes 165888 | tf_op jit(solution)/shard_map/pallas_call | solution.py:80
  39.9 8.4 %collective-permute-done.8.refs_3_ = bf16[336,768]{1,0:T(8,128)(2,1)S(1)} collective-permute-done((bf16[336,768]{1,0:T(8,128)(2,1)}, bf16[336,768]{1,0:T(8,128)(2,1)S(1)}, u32[]{:S(2)}, u32[]{:S(2)}) %collective-permute-start.8) | collective-permute-done | bytes 516128 | tf_op jit(solution)/shard_map/ppermute | solution.py:270
  48.3 1.1 %collective-permute-start.10 = (bf16[336,512]{1,0:T(8,128)(2,1)S(1)}, bf16[336,512]{1,0:T(8,128)(2,1)}, u32[]{:S(2)}, u32[]{:S(2)}) collective-permute-start(bf16[336,512]{1,0:T(8,128)(2,1)S(1)} %shard_map.93.refs_0_.refs_15_), channel_id=1, source_target_pairs={{0,8},{8,0},{16,24},{24,16},{1,9},{9,1},{17,25},{25,17},{2,10},{10... | collective-permute-start | bytes 1032200 | tf_op jit(solution)/shard_map/ppermute | solution.py:270
  49.4 0.0 collective-permute-start.11
  49.4 1.8 %collective-permute-start.15 = (bf16[324,1296]{1,0:T(8,128)(2,1)}, bf16[324,1296]{1,0:T(8,128)(2,1)}, u32[]{:S(2)}, u32[]{:S(2)}) collective-permute-start(bf16[324,1296]{1,0:T(8,128)(2,1)} %collective-permute-done.refs_2_), channel_id=1, source_target_pairs={{0,1},{1,0},{2,3},{3,2},{4,5},{5,4},{6,7},{7,6},{8,9},{9,8},{10,11... | collective-permute-start | bytes 2519432 | tf_op jit(solution)/shard_map/ppermute | solution.py:265
  51.2 2.0 %copy-done = bf16[1296,1296]{1,0:T(8,128)(2,1)S(1)} copy-done((bf16[1296,1296]{1,0:T(8,128)(2,1)S(1)}, bf16[1296,1296]{1,0:T(8,128)(2,1)}, u32[]{:S(2)}) %copy-start) | copy-done | bytes 3359256
  53.3 1.0 copy-done.13
  54.3 5.6 %shard_map.95 = (bf16[1296,768]{1,0:T(8,128)(2,1)S(1)}, f32[1,768]{1,0:T(1,128)S(1)}) custom-call(s32[1]{0:T(128)} %bitcast.7.here_ref, bf16[336,768]{1,0:T(8,128)(2,1)S(1)} %copy-done.13, bf16[336,768]{1,0:T(8,128)(2,1)} %collective-permute-done.5.refs_1_, bf16[336,768]{1,0:T(8,128)(2,1)} %collective-permute-done.6.refs_2_, ...), custom_call_target="tpu_custom_call" | custom-call | flops 322486272 | bytes 419904 | tf_op jit(solution)/shard_map/pallas_call | solution.py:122
  60.0 5.5 %shard_map.94 = (bf16[1296,768]{1,0:T(8,128)(2,1)S(1)}, f32[1,768]{1,0:T(1,128)S(1)}) custom-call(s32[1]{0:T(128)} %bitcast.7.here_ref, bf16[336,768]{1,0:T(8,128)(2,1)S(1)} %shard_map.91.refs_0_.refs_13_, bf16[336,768]{1,0:T(8,128)(2,1)} %collective-permute-done.3.refs_1_, bf16[336,768]{1,0:T(8,128)(2,1)} %collective-permute-done.4.refs_2_, ...), custom_call_target="tpu_custom_call" | custom-call | flops 322486272 | bytes 419904 | tf_op jit(solution)/shard_map/pallas_call | solution.py:122
  65.4 1.3 %copy-done.3 = bf16[1296,768]{1,0:T(8,128)(2,1)} copy-done((bf16[1296,768]{1,0:T(8,128)(2,1)}, bf16[1296,768]{1,0:T(8,128)(2,1)S(1)}, u32[]{:S(2)}) %copy-start.3) | copy-done | bytes 1990680
  66.7 0.1 collective-permute-start.13
  66.8 0.7 collective-permute-start.12
  67.6 0.1 pad_add_fusion.2.ids_ref
  67.7 0.1 stack.62.ids_ref
  67.8 0.9 slice.74
  68.7 0.3 collective-permute-start.16
  69.0 0.9 slice.75
  69.9 1.3 %collective-permute-start.17 = (bf16[336,256]{1,0:T(8,128)(2,1)S(1)}, bf16[336,256]{1,0:T(8,128)(2,1)S(1)}, u32[]{:S(2)}, u32[]{:S(2)}) collective-permute-start(bf16[336,256]{1,0:T(8,128)(2,1)S(1)} %slice.75), channel_id=1, source_target_pairs={{0,16},{8,24},{16,0},{24,8},{1,17},{9,25},{17,1},{25,9},{2,18},{10... | collective-permute-start | bytes 516104 | tf_op jit(solution)/shard_map/ppermute | solution.py:270
  71.2 0.1 pad_add_fusion.1.ids_ref
  71.3 1.6 %copy-done.4 = bf16[1296,768]{1,0:T(8,128)(2,1)S(1)} copy-done((bf16[1296,768]{1,0:T(8,128)(2,1)S(1)}, bf16[1296,768]{1,0:T(8,128)(2,1)}, u32[]{:S(2)}) %copy-start.4) | copy-done | bytes 1990680
  72.9 8.5 %shard_map.96 = (bf16[324,768]{1,0:T(8,128)(2,1)S(1)}, bf16[324,768]{1,0:T(8,128)(2,1)S(1)}) custom-call(s32[4]{0:T(128)S(1)} %pad_add_fusion.2.ids_ref, bf16[324,1296]{1,0:T(8,128)(2,1)S(1)} %dynamic-slice_bitcast_fusion.refs_0_, bf16[324,1296]{1,0:T(8,128)(2,1)} %collective-permute-done.14.refs_1_, bf16[324,1296]{1,0:T(8,128)(2,1)} %collective-permute-done.refs_2_, ...), custom_call_target="tpu_custom_call" | custom-call | flops 644972544 | bytes 917568 | tf_op jit(solution)/shard_map/pallas_call | solution.py:178
  81.4 4.2 %shard_map.98 = (bf16[1296,512]{1,0:T(8,128)(2,1)S(1)}, f32[1,512]{1,0:T(1,128)S(1)}) custom-call(s32[1]{0:T(128)} %bitcast.7.here_ref, bf16[336,512]{1,0:T(8,128)(2,1)S(1)} %copy-done.16, bf16[336,512]{1,0:T(8,128)(2,1)} %collective-permute-done.10.refs_1_, bf16[336,512]{1,0:T(8,128)(2,1)} %collective-permute-done.11.refs_2_, ...), custom_call_target="tpu_custom_call" | custom-call | flops 214990848 | bytes 419904 | tf_op jit(solution)/shard_map/pallas_call | solution.py:122
  85.7 5.8 %shard_map.99.refs_9_ = bf16[324,512]{1,0:T(8,128)(2,1)S(1)} custom-call(s32[6]{0:T(128)S(1)} %stack.62.ids_ref, bf16[324,1296]{1,0:T(8,128)(2,1)S(1)} %copy-done.9, bf16[324,1296]{1,0:T(8,128)(2,1)} %collective-permute-done.14.refs_1_, bf16[324,1296]{1,0:T(8,128)(2,1)} %collective-permute-done.refs_2_, bf16[324,1296]{1,0:T(8,128)(2,1)} %collective-permute-done.15.refs_3_, ...), custom_call_target="tpu_custom_call" | custom-call | flops 322486272 | bytes 795744 | tf_op jit(solution)/shard_map/pallas_call | solution.py:178
  91.6 0.7 copy-done.21
  92.3 4.9 %shard_map.97 = (bf16[324,768]{1,0:T(8,128)(2,1)S(1)}, bf16[324,768]{1,0:T(8,128)(2,1)S(1)}) custom-call(s32[2]{0:T(128)S(1)} %pad_add_fusion.1.ids_ref, bf16[324,1296]{1,0:T(8,128)(2,1)} %collective-permute-done.7.refs_0_.refs_4_, bf16[324,1296]{1,0:T(8,128)(2,1)} %collective-permute-done.13.refs_1_.refs_5_, ...), custom_call_target="tpu_custom_call" | custom-call | flops 322486272 | bytes 707616 | tf_op jit(solution)/shard_map/pallas_call | solution.py:178
  97.2 0.8 copy-done.23
  98.0 0.8 copy-done.25
  98.8 1.3 %collective-permute-start.18 = (bf16[324,1296]{1,0:T(8,128)(2,1)}, bf16[324,1296]{1,0:T(8,128)(2,1)}, u32[]{:S(2)}, u32[]{:S(2)}) collective-permute-start(bf16[324,1296]{1,0:T(8,128)(2,1)} %collective-permute-done.12.refs_0_), channel_id=1, source_target_pairs={{0,1},{1,0},{2,3},{3,2},{4,5},{5,4},{6,7},{7,6},{8,9},{9,8},{10,11... | collective-permute-start | bytes 2519432 | tf_op jit(solution)/shard_map/ppermute | solution.py:265
  100.1 0.1 copy.20.angle_ref
  100.4 1.5 %copy-done.6 = bf16[1296,768]{1,0:T(8,128)(2,1)S(1)} copy-done((bf16[1296,768]{1,0:T(8,128)(2,1)S(1)}, bf16[1296,768]{1,0:T(8,128)(2,1)}, u32[]{:S(2)}) %copy-start.6) | copy-done | bytes 1990680
  101.9 1.0 copy-done.22
  102.9 1.0 copy-done.24
  103.9 1.0 copy-done.26
  105.0 3.6 %shard_map.100 = (bf16[324,768]{1,0:T(8,128)(2,1)S(1)}, bf16[324,768]{1,0:T(8,128)(2,1)S(1)}, bf16[324,512]{1,0:T(8,128)(2,1)S(1)}) custom-call(s32[1]{0:T(128)} %bitcast.18.ids_ref, bf16[324,1296]{1,0:T(8,128)(2,1)} %collective-permute-done.12.refs_0_, s32[1,768]{1,0:T(1,128)S(1)} %get-tuple-element.110.refs_4_.refs_2_.refs_1_, ...), custom_call_target="tpu_custom_call" | custom-call | flops 214990848 | bytes 768528 | tf_op jit(solution)/shard_map/pallas_call | solution.py:178
  108.7 4.2 %shard_map.101 = bf16[16,324,128]{2,1,0:T(8,128)(2,1)S(1)} custom-call(s32[1]{0:T(128)} %bitcast.ids_ref, f32[324,2]{1,0:T(8,128)S(1)} %copy.20.angle_ref, bf16[324,1296]{1,0:T(8,128)(2,1)} %collective-permute-done.18.refs_0_, s32[1,768]{1,0:T(1,128)S(1)} %get-tuple-element.110.refs_4_.refs_2_.refs_1_, ...), custom_call_target="tpu_custom_call" | custom-call | flops 214990848 | bytes 768528 | tf_op jit(solution)/shard_map/pallas_call | solution.py:221
  112.9 1.2 %copy.21 = bf16[324,16,128]{2,1,0:T(8,128)(2,1)} copy(bf16[324,16,128]{2,0,1:T(8,128)(2,1)S(1)} %bitcast.86) | data formatting | bytes 2654208 | tf_op jit(solution)/shard_map/transpose | solution.py:368
  (105 shorter events, 0.4 us)
Async XLA Ops:
  0.3 1.8 %copy-start.18 = (f32[324,4]{1,0:T(8,128)}, f32[324,4]{1,0:T(8,128)S(1)}, u32[]{:S(2)}) copy-start(f32[324,4]{1,0:T(8,128)S(1)} %copy.17.coef_ref) | copy-start | bytes 15556
  0.3 1.8 %copy-start.32 = (s32[16,128]{1,0:T(8,128)S(1)}, s32[16,128]{1,0:T(8,128)}, u32[]{:S(2)}) copy-start(s32[16,128]{1,0:T(8,128)} %param.10) | copy-start | bytes 24580
  0.3 1.8 %copy-start.27 = (f32[16,128]{1,0:T(8,128)S(1)}, f32[16,128]{1,0:T(8,128)}, u32[]{:S(2)}) copy-start(f32[16,128]{1,0:T(8,128)} %depth_ref.5) | copy-start | bytes 24580
  4.6 55.4 %copy-start.10 = (bf16[336,768]{1,0:T(8,128)(2,1)}, bf16[336,768]{1,0:T(8,128)(2,1)S(1)}, u32[]{:S(2)}) copy-start(bf16[336,768]{1,0:T(8,128)(2,1)S(1)} %shard_map.91.refs_0_.refs_13_) | copy-start | bytes 1548292
  4.6 13.7 %collective-permute-start.3 = (bf16[336,768]{1,0:T(8,128)(2,1)S(1)}, bf16[336,768]{1,0:T(8,128)(2,1)}, u32[]{:S(2)}, u32[]{:S(2)}) collective-permute-start(bf16[336,768]{1,0:T(8,128)(2,1)S(1)} %shard_map.91.refs_0_.refs_13_), channel_id=1, source_target_pairs={{0,8},{8,0},{16,24},{24,16},{1,9},{9,1},{17,25},{25,17},{2,10},{10... | collective-permute-start | bytes 1548296 | tf_op jit(solution)/shard_map/ppermute | solution.py:270
  6.7 12.4 %collective-permute-start.4 = (bf16[336,768]{1,0:T(8,128)(2,1)S(1)}, bf16[336,768]{1,0:T(8,128)(2,1)}, u32[]{:S(2)}, u32[]{:S(2)}) collective-permute-start(bf16[336,768]{1,0:T(8,128)(2,1)S(1)} %shard_map.91.refs_0_.refs_13_), channel_id=1, source_target_pairs={{0,16},{8,24},{16,0},{24,8},{1,17},{9,25},{17,1},{25,9},{2,18},{10... | collective-permute-start | bytes 1548296 | tf_op jit(solution)/shard_map/ppermute | solution.py:270
  7.9 2.9 %copy-start.19 = (f32[324,4]{1,0:T(8,128)S(1)}, f32[324,4]{1,0:T(8,128)}, u32[]{:S(2)}) copy-start(f32[324,4]{1,0:T(8,128)} %copy-done.18) | copy-start | bytes 15556
  9.4 61.9 %copy-start.8 = (bf16[324,1296]{1,0:T(8,128)(2,1)}, bf16[324,1296]{1,0:T(8,128)(2,1)S(1)}, u32[]{:S(2)}) copy-start(bf16[324,1296]{1,0:T(8,128)(2,1)S(1)} %dynamic-slice_bitcast_fusion.refs_0_) | copy-start | bytes 2519428
  9.4 17.4 %copy-start.34 = (bf16[16,128]{1,0:T(8,128)(2,1)S(1)}, bf16[16,128]{1,0:T(8,128)(2,1)}, u32[]{:S(2)}) copy-start(bf16[16,128]{1,0:T(8,128)(2,1)} %param.13) | copy-start | bytes 12292
  9.4 17.4 %copy-start.35 = (bf16[16,128]{1,0:T(8,128)(2,1)S(1)}, bf16[16,128]{1,0:T(8,128)(2,1)}, u32[]{:S(2)}) copy-start(bf16[16,128]{1,0:T(8,128)(2,1)} %param.12) | copy-start | bytes 12292
  9.4 17.5 %copy-start.31 = (s32[16,128]{1,0:T(8,128)S(1)}, s32[16,128]{1,0:T(8,128)}, u32[]{:S(2)}) copy-start(s32[16,128]{1,0:T(8,128)} %param.15) | copy-start | bytes 24580
  9.4 26.0 %slice-start.1 = ((s32[16,128]{1,0:T(8,128)}), s32[1,128]{1,0:T(1,128)S(1)}, s32[]{:S(2)}) async-start(s32[16,128]{1,0:T(8,128)} %param.15), calls=%async_computation.1 | async-start | bytes 1024 | tf_op jit(solution)/shard_map/slice | solution.py:320
  9.4 25.0 %collective-permute-start = (bf16[324,1296]{1,0:T(8,128)(2,1)S(1)}, bf16[324,1296]{1,0:T(8,128)(2,1)}, u32[]{:S(2)}, u32[]{:S(2)}) collective-permute-start(bf16[324,1296]{1,0:T(8,128)(2,1)S(1)} %dynamic-slice_bitcast_fusion.refs_0_), channel_id=1, source_target_pairs={{0,2},{2,4},{4,6},{6,0},{1,3},{3,5},{5,7},{7,1},{8,10},{10,12},{12... | collective-permute-start | bytes 2519432 | tf_op jit(solution)/shard_map/ppermute | solution.py:232
  13.2 26.7 %copy-start.12 = (bf16[336,768]{1,0:T(8,128)(2,1)}, bf16[336,768]{1,0:T(8,128)(2,1)S(1)}, u32[]{:S(2)}) copy-start(bf16[336,768]{1,0:T(8,128)(2,1)S(1)} %shard_map.92.refs_0_.refs_14_) | copy-start | bytes 1548292
  19.1 15.4 %collective-permute-start.5 = (bf16[336,768]{1,0:T(8,128)(2,1)S(1)}, bf16[336,768]{1,0:T(8,128)(2,1)}, u32[]{:S(2)}, u32[]{:S(2)}) collective-permute-start(bf16[336,768]{1,0:T(8,128)(2,1)S(1)} %shard_map.92.refs_0_.refs_14_), channel_id=1, source_target_pairs={{0,8},{8,0},{16,24},{24,16},{1,9},{9,1},{17,25},{25,17},{2,10},{10... | collective-permute-start | bytes 1548296 | tf_op jit(solution)/shard_map/ppermute | solution.py:270
  19.5 15.0 %collective-permute-start.6 = (bf16[336,768]{1,0:T(8,128)(2,1)S(1)}, bf16[336,768]{1,0:T(8,128)(2,1)}, u32[]{:S(2)}, u32[]{:S(2)}) collective-permute-start(bf16[336,768]{1,0:T(8,128)(2,1)S(1)} %shard_map.92.refs_0_.refs_14_), channel_id=1, source_target_pairs={{0,16},{8,24},{16,0},{24,8},{1,17},{9,25},{17,1},{25,9},{2,18},{10... | collective-permute-start | bytes 1548296 | tf_op jit(solution)/shard_map/ppermute | solution.py:270
  21.3 5.6 %collective-permute-start.1 = (bf16[324,128]{1,0:T(8,128)(2,1)}, bf16[324,128]{1,0:T(8,128)(2,1)}, u32[]{:S(2)}, u32[]{:S(2)}) collective-permute-start(bf16[324,128]{1,0:T(8,128)(2,1)} %get-tuple-element.84), channel_id=1, source_target_pairs={{0,1},{1,0},{2,3},{3,2},{4,5},{5,4},{6,7},{7,6},{8,9},{9,8},{10,11... | collective-permute-start | bytes 248840 | tf_op jit(solution)/shard_map/ppermute | solution.py:244
  23.7 10.8 %collective-permute-start.2 = (bf16[324,128]{1,0:T(8,128)(2,1)S(1)}, bf16[324,128]{1,0:T(8,128)(2,1)S(1)}, u32[]{:S(2)}, u32[]{:S(2)}) collective-permute-start(bf16[324,128]{1,0:T(8,128)(2,1)S(1)} %get-tuple-element.83), channel_id=1, source_target_pairs={{1,2},{3,4},{5,6},{2,1},{4,3},{6,5},{9,10},{11,12},{13,14},{10,9},... | collective-permute-start | bytes 248840 | tf_op jit(solution)/shard_map/ppermute | solution.py:246
  27.0 43.0 %collective-permute-start.14 = (bf16[324,1296]{1,0:T(8,128)(2,1)S(1)}, bf16[324,1296]{1,0:T(8,128)(2,1)}, u32[]{:S(2)}, u32[]{:S(2)}) collective-permute-start(bf16[324,1296]{1,0:T(8,128)(2,1)S(1)} %dynamic-slice_bitcast_fusion.refs_0_), channel_id=1, source_target_pairs={{0,1},{1,0},{2,3},{3,2},{4,5},{5,4},{6,7},{7,6},{8,9},{9,8},{10,11... | collective-permute-start | bytes 2519432 | tf_op jit(solution)/shard_map/ppermute | solution.py:265
  34.5 1.3 %copy-start.28 = (bf16[324,128]{1,0:T(8,128)(2,1)}, bf16[324,128]{1,0:T(8,128)(2,1)S(1)}, u32[]{:S(2)}) copy-start(bf16[324,128]{1,0:T(8,128)(2,1)S(1)} %collective-permute-done.2) | copy-start | bytes 248836
  34.5 13.8 %collective-permute-start.8 = (bf16[336,768]{1,0:T(8,128)(2,1)}, bf16[336,768]{1,0:T(8,128)(2,1)S(1)}, u32[]{:S(2)}, u32[]{:S(2)}) collective-permute-start(bf16[336,768]{1,0:T(8,128)(2,1)} %collective-permute-done.4.refs_2_), channel_id=1, source_target_pairs={{0,8},{8,0},{16,24},{24,16},{1,9},{9,1},{17,25},{25,17},{2,10},{10... | collective-permute-start | bytes 1548296 | tf_op jit(solution)/shard_map/ppermute | solution.py:270
  34.8 13.5 %collective-permute-start.9 = (bf16[336,768]{1,0:T(8,128)(2,1)}, bf16[336,768]{1,0:T(8,128)(2,1)S(1)}, u32[]{:S(2)}, u32[]{:S(2)}) collective-permute-start(bf16[336,768]{1,0:T(8,128)(2,1)} %collective-permute-done.5.refs_1_), channel_id=1, source_target_pairs={{0,16},{8,24},{16,0},{24,8},{1,17},{9,25},{17,1},{25,9},{2,18},{10... | collective-permute-start | bytes 1548296 | tf_op jit(solution)/shard_map/ppermute | solution.py:270
  35.4 31.3 %collective-permute-start.7 = (bf16[324,1296]{1,0:T(8,128)(2,1)}, bf16[324,1296]{1,0:T(8,128)(2,1)}, u32[]{:S(2)}, u32[]{:S(2)}) collective-permute-start(bf16[324,1296]{1,0:T(8,128)(2,1)} %collective-permute-done.refs_2_), channel_id=1, source_target_pairs={{0,2},{2,4},{4,6},{6,0},{1,3},{3,5},{5,7},{7,1},{8,10},{10,12},{12... | collective-permute-start | bytes 2519432 | tf_op jit(solution)/shard_map/ppermute | solution.py:232
  36.8 0.9 copy-start.20
  39.9 20.1 %copy-start.15 = (bf16[336,512]{1,0:T(8,128)(2,1)}, bf16[336,512]{1,0:T(8,128)(2,1)S(1)}, u32[]{:S(2)}) copy-start(bf16[336,512]{1,0:T(8,128)(2,1)S(1)} %shard_map.93.refs_0_.refs_15_) | copy-start | bytes 1032196
  48.3 18.5 %collective-permute-start.10 = (bf16[336,512]{1,0:T(8,128)(2,1)S(1)}, bf16[336,512]{1,0:T(8,128)(2,1)}, u32[]{:S(2)}, u32[]{:S(2)}) collective-permute-start(bf16[336,512]{1,0:T(8,128)(2,1)S(1)} %shard_map.93.refs_0_.refs_15_), channel_id=1, source_target_pairs={{0,8},{8,0},{16,24},{24,16},{1,9},{9,1},{17,25},{25,17},{2,10},{10... | collective-permute-start | bytes 1032200 | tf_op jit(solution)/shard_map/ppermute | solution.py:270
  49.4 17.3 %collective-permute-start.11 = (bf16[336,512]{1,0:T(8,128)(2,1)S(1)}, bf16[336,512]{1,0:T(8,128)(2,1)}, u32[]{:S(2)}, u32[]{:S(2)}) collective-permute-start(bf16[336,512]{1,0:T(8,128)(2,1)S(1)} %shard_map.93.refs_0_.refs_15_), channel_id=1, source_target_pairs={{0,16},{8,24},{16,0},{24,8},{1,17},{9,25},{17,1},{25,9},{2,18},{10... | collective-permute-start | bytes 1032200 | tf_op jit(solution)/shard_map/ppermute | solution.py:270
  49.4 21.9 %collective-permute-start.15 = (bf16[324,1296]{1,0:T(8,128)(2,1)}, bf16[324,1296]{1,0:T(8,128)(2,1)}, u32[]{:S(2)}, u32[]{:S(2)}) collective-permute-start(bf16[324,1296]{1,0:T(8,128)(2,1)} %collective-permute-done.refs_2_), channel_id=1, source_target_pairs={{0,1},{1,0},{2,3},{3,2},{4,5},{5,4},{6,7},{7,6},{8,9},{9,8},{10,11... | collective-permute-start | bytes 2519432 | tf_op jit(solution)/shard_map/ppermute | solution.py:265
  51.2 2.0 %copy-start = (bf16[1296,1296]{1,0:T(8,128)(2,1)S(1)}, bf16[1296,1296]{1,0:T(8,128)(2,1)}, u32[]{:S(2)}) copy-start(bf16[1296,1296]{1,0:T(8,128)(2,1)} %refs_5_.1) | copy-start | bytes 10077700
  53.3 1.0 copy-start.13
  54.3 5.6 %copy-start.1 = (bf16[1296,1296]{1,0:T(8,128)(2,1)S(1)}, bf16[1296,1296]{1,0:T(8,128)(2,1)}, u32[]{:S(2)}) copy-start(bf16[1296,1296]{1,0:T(8,128)(2,1)} %refs_5_.1) | copy-start | bytes 10077700
  60.0 7.7 %copy-start.33 = (s32[16,128]{1,0:T(8,128)S(1)}, s32[16,128]{1,0:T(8,128)}, u32[]{:S(2)}) copy-start(s32[16,128]{1,0:T(8,128)} %param.14) | copy-start | bytes 24580
  65.4 1.3 %copy-start.3 = (bf16[1296,768]{1,0:T(8,128)(2,1)}, bf16[1296,768]{1,0:T(8,128)(2,1)S(1)}, u32[]{:S(2)}) copy-start(bf16[1296,768]{1,0:T(8,128)(2,1)S(1)} %get-tuple-element.60.refs_6_.refs_4_.refs_7_) | copy-start | bytes 5971972
  66.7 18.9 %collective-permute-start.13 = (bf16[324,1296]{1,0:T(8,128)(2,1)}, bf16[324,1296]{1,0:T(8,128)(2,1)}, u32[]{:S(2)}, u32[]{:S(2)}) collective-permute-start(bf16[324,1296]{1,0:T(8,128)(2,1)} %collective-permute-done.7.refs_0_.refs_4_), channel_id=1, source_target_pairs={{0,1},{1,0},{2,3},{3,2},{4,5},{5,4},{6,7},{7,6},{8,9},{9,8},{10,11... | collective-permute-start | bytes 2519432 | tf_op jit(solution)/shard_map/ppermute | solution.py:265
  66.8 31.9 %collective-permute-start.12 = (bf16[324,1296]{1,0:T(8,128)(2,1)}, bf16[324,1296]{1,0:T(8,128)(2,1)}, u32[]{:S(2)}, u32[]{:S(2)}) collective-permute-start(bf16[324,1296]{1,0:T(8,128)(2,1)} %collective-permute-done.7.refs_0_.refs_4_), channel_id=1, source_target_pairs={{0,2},{2,4},{4,6},{6,0},{1,3},{3,5},{5,7},{7,1},{8,10},{10,12},{12... | collective-permute-start | bytes 2519432 | tf_op jit(solution)/shard_map/ppermute | solution.py:232
  67.6 13.7 %copy-start.29 = (f32[16,128]{1,0:T(8,128)}, f32[16,128]{1,0:T(8,128)S(1)}, u32[]{:S(2)}) copy-start(f32[16,128]{1,0:T(8,128)S(1)} %convert_element_type.88) | copy-start | bytes 24580
  68.7 12.7 %collective-permute-start.16 = (bf16[336,256]{1,0:T(8,128)(2,1)S(1)}, bf16[336,256]{1,0:T(8,128)(2,1)S(1)}, u32[]{:S(2)}, u32[]{:S(2)}) collective-permute-start(bf16[336,256]{1,0:T(8,128)(2,1)S(1)} %slice.74), channel_id=1, source_target_pairs={{0,8},{8,0},{16,24},{24,16},{1,9},{9,1},{17,25},{25,17},{2,10},{10... | collective-permute-start | bytes 516104 | tf_op jit(solution)/shard_map/ppermute | solution.py:270
  69.9 11.5 %collective-permute-start.17 = (bf16[336,256]{1,0:T(8,128)(2,1)S(1)}, bf16[336,256]{1,0:T(8,128)(2,1)S(1)}, u32[]{:S(2)}, u32[]{:S(2)}) collective-permute-start(bf16[336,256]{1,0:T(8,128)(2,1)S(1)} %slice.75), channel_id=1, source_target_pairs={{0,16},{8,24},{16,0},{24,8},{1,17},{9,25},{17,1},{25,9},{2,18},{10... | collective-permute-start | bytes 516104 | tf_op jit(solution)/shard_map/ppermute | solution.py:270
  71.3 1.6 %copy-start.4 = (bf16[1296,768]{1,0:T(8,128)(2,1)S(1)}, bf16[1296,768]{1,0:T(8,128)(2,1)}, u32[]{:S(2)}) copy-start(bf16[1296,768]{1,0:T(8,128)(2,1)} %copy-done.3) | copy-start | bytes 5971972
  72.9 8.5 %copy-start.2 = (bf16[1296,1296]{1,0:T(8,128)(2,1)S(1)}, bf16[1296,1296]{1,0:T(8,128)(2,1)}, u32[]{:S(2)}) copy-start(bf16[1296,1296]{1,0:T(8,128)(2,1)} %refs_5_.1) | copy-start | bytes 10077700
  72.9 8.6 %copy-start.16 = (bf16[336,512]{1,0:T(8,128)(2,1)S(1)}, bf16[336,512]{1,0:T(8,128)(2,1)}, u32[]{:S(2)}) copy-start(bf16[336,512]{1,0:T(8,128)(2,1)} %copy-done.15) | copy-start | bytes 1032196
  81.4 4.3 %copy-start.9 = (bf16[324,1296]{1,0:T(8,128)(2,1)S(1)}, bf16[324,1296]{1,0:T(8,128)(2,1)}, u32[]{:S(2)}) copy-start(bf16[324,1296]{1,0:T(8,128)(2,1)} %copy-done.8) | copy-start | bytes 2519428
  85.7 6.6 %copy-start.5 = (bf16[1296,768]{1,0:T(8,128)(2,1)S(1)}, bf16[1296,768]{1,0:T(8,128)(2,1)}, u32[]{:S(2)}) copy-start(bf16[1296,768]{1,0:T(8,128)(2,1)} %copy-done.3) | copy-start | bytes 5971972
  91.5 0.7 copy-start.21
  92.3 7.8 %slice-start = ((f32[16,128]{1,0:T(8,128)}), f32[1,128]{1,0:T(1,128)S(1)}, s32[]{:S(2)}) async-start(f32[16,128]{1,0:T(8,128)} %copy-done.29), calls=%async_computation | async-start | bytes 1024 | tf_op jit(solution)/shard_map/slice | solution.py:320
  92.3 8.0 %copy-start.30 = (f32[16,128]{1,0:T(8,128)S(1)}, f32[16,128]{1,0:T(8,128)}, u32[]{:S(2)}) copy-start(f32[16,128]{1,0:T(8,128)} %copy-done.29) | copy-start | bytes 24580
  97.2 0.8 copy-start.23
  98.0 0.8 copy-start.25
  98.8 9.9 %collective-permute-start.18 = (bf16[324,1296]{1,0:T(8,128)(2,1)}, bf16[324,1296]{1,0:T(8,128)(2,1)}, u32[]{:S(2)}, u32[]{:S(2)}) collective-permute-start(bf16[324,1296]{1,0:T(8,128)(2,1)} %collective-permute-done.12.refs_0_), channel_id=1, source_target_pairs={{0,1},{1,0},{2,3},{3,2},{4,5},{5,4},{6,7},{7,6},{8,9},{9,8},{10,11... | collective-permute-start | bytes 2519432 | tf_op jit(solution)/shard_map/ppermute | solution.py:265
  100.4 1.6 %copy-start.6 = (bf16[1296,768]{1,0:T(8,128)(2,1)S(1)}, bf16[1296,768]{1,0:T(8,128)(2,1)}, u32[]{:S(2)}) copy-start(bf16[1296,768]{1,0:T(8,128)(2,1)} %copy-done.3) | copy-start | bytes 5971972
  101.9 1.0 copy-start.22
  102.9 1.0 copy-start.24
  103.9 1.0 copy-start.26
  105.0 3.7 %copy-start.7 = (bf16[1296,768]{1,0:T(8,128)(2,1)S(1)}, bf16[1296,768]{1,0:T(8,128)(2,1)}, u32[]{:S(2)}) copy-start(bf16[1296,768]{1,0:T(8,128)(2,1)} %copy-done.3) | copy-start | bytes 5971972
  105.0 3.7 %copy-start.11 = (bf16[336,768]{1,0:T(8,128)(2,1)S(1)}, bf16[336,768]{1,0:T(8,128)(2,1)}, u32[]{:S(2)}) copy-start(bf16[336,768]{1,0:T(8,128)(2,1)} %copy-done.10) | copy-start | bytes 1548292
  105.0 3.7 %copy-start.14 = (bf16[336,768]{1,0:T(8,128)(2,1)S(1)}, bf16[336,768]{1,0:T(8,128)(2,1)}, u32[]{:S(2)}) copy-start(bf16[336,768]{1,0:T(8,128)(2,1)} %copy-done.12) | copy-start | bytes 1548292
  105.0 3.7 %copy-start.17 = (bf16[336,512]{1,0:T(8,128)(2,1)S(1)}, bf16[336,512]{1,0:T(8,128)(2,1)}, u32[]{:S(2)}) copy-start(bf16[336,512]{1,0:T(8,128)(2,1)} %copy-done.15) | copy-start | bytes 1032196

commit v2 on v1

v2 whole, which is shorter than its diff:
```python
import functools
import math

import jax
import jax.numpy as jnp
from jax import lax
from jax.experimental import pallas as pl
from jax.experimental.pallas import tpu as pltpu
from jax.sharding import Mesh
from jax.sharding import PartitionSpec as P

NDIR = 36
PLANES = 4
SUB = 16
ANY = pl.BlockSpec(memory_space=pl.ANY)
VMEM = pl.BlockSpec(memory_space=pltpu.VMEM)
SMEM = pl.BlockSpec(memory_space=pltpu.SMEM)
BF16 = jnp.bfloat16
F32 = jnp.float32


def params(mib):
    return pltpu.CompilerParams(vmem_limit_bytes=mib * 2**20)


def places_of(rank, count):
    cells = rank.shape[1]
    kind = lax.broadcasted_iota(jnp.int32, (count, cells), 0)
    mine = (kind == rank).astype(F32)
    first = lax.broadcasted_iota(jnp.int32, (cells, cells), 0)
    second = lax.broadcasted_iota(jnp.int32, (cells, cells), 1)
    earlier = (first < second).astype(F32).astype(BF16)
    before = jnp.dot(mine.astype(BF16), earlier, preferred_element_type=F32)
    number = jnp.sum(mine, axis=1, keepdims=True)
    lower = (kind < rank).astype(F32)
    return jnp.sum(mine * before + lower * number, axis=0, keepdims=True)


def moves(place):
    cells = place.shape[1]
    target = lax.broadcasted_iota(jnp.int32, (cells, cells), 0)
    return (target == place.astype(jnp.int32)).astype(F32).astype(BF16)


def put_in_order(values, matrix):
    return lax.dot_general(
        values, matrix, (((1,), (1,)), ((), ())), preferred_element_type=F32
    )


def cells_of(values, rows):
    return jnp.concatenate([values[row : row + 1, :] for row in rows], axis=1)


def propagate_kernel(
    wanted,
    count,
    x_ref,
    west_ref,
    east_ref,
    sea_ref,
    depth_ref,
    coef_ref,
    rank_ref,
    sorted_ref,
    place_ref,
    out_ref,
):
    rows, comps, width = x_ref.shape

    def tile(at, height):
        lane = lax.broadcasted_iota(jnp.int32, (height, width), 1)
        coef = coef_ref[at, :]
        gain_x, gain_y, pos_x, pos_y = (
            jnp.broadcast_to(coef[:, i : i + 1], (height, width)) for i in range(4)
        )
        from_west, from_south = pos_x > 0, pos_y > 0
        first, last = lane == 0, lane == width - 1
        known = {}

        def masked(row):
            if row not in known:
                if row < 0:
                    known[row] = west_ref[at, :].astype(F32)
                elif row == rows:
                    known[row] = east_ref[at, :].astype(F32)
                else:
                    known[row] = x_ref[row, at, :].astype(F32) * sea_ref[row : row + 1, :]
            return known[row]

        for k, row in enumerate(wanted):
            west, centre, east = masked(row - 1), masked(row), masked(row + 1)
            upwind_x = jnp.where(from_west, west, east)
            south = jnp.where(first, 0.0, pltpu.roll(centre, 1, 1))
            north = jnp.where(last, 0.0, pltpu.roll(centre, width - 1, 1))
            upwind_y = jnp.where(from_south, south, north)
            depth = depth_ref[row : row + 1, :]
            moved = (
                centre
                - gain_x * depth * (centre - upwind_x)
                - gain_y * depth * (centre - upwind_y)
            )
            out_ref[at, k * width : (k + 1) * width] = (
                moved * sea_ref[row : row + 1, :]
            ).astype(BF16)

    def body(step, carry):
        tile(pl.ds(pl.multiple_of(step * SUB, SUB), SUB), SUB)
        return carry

    whole = comps // SUB
    lax.fori_loop(0, whole, body, 0)
    if comps % SUB:
        spare = out_ref.shape[0] - whole * SUB
        out_ref[whole * SUB :, :] = jnp.zeros((spare, out_ref.shape[1]), BF16)
        tile(slice(whole * SUB, comps), comps - whole * SUB)
    place = places_of(cells_of(rank_ref, wanted), count)
    place_ref[...] = place
    sorted_ref[...] = put_in_order(out_ref[...], moves(place)).astype(BF16)


def propagate(wanted, count, x, west, east, sea, depth, coef, rank_map):
    comps, width = x.shape[1:]
    padded = -(-comps // SUB) * SUB
    cells = len(wanted) * width
    return pl.pallas_call(
        functools.partial(propagate_kernel, wanted, count),
        out_shape=[
            jax.ShapeDtypeStruct((padded, cells), BF16),
            jax.ShapeDtypeStruct((1, cells), F32),
        ],
        in_specs=[VMEM] * 7,
        out_specs=[VMEM] * 2,
        scratch_shapes=[pltpu.VMEM((padded, cells), BF16)],
        compiler_params=params(20),
        cost_estimate=pl.CostEstimate(
            flops=2 * comps * cells, bytes_accessed=comps * cells, transcendentals=0
        ),
    )(x, west, east, sea, depth, coef, rank_map)


def split(refs, *sizes):
    out, at = [], 0
    for size in sizes:
        out.append(refs[at : at + size])
        at += size
    return out


def pair_body(tile, sizes, here_ref, *refs):
    groups = len(sizes)
    *parts, (pair_ref,), paired, totals, wholes = split(refs, *sizes, 1, groups, groups, groups)
    step = pl.program_id(0)
    comps = wholes[0].shape[0]
    some = comps // 4

    @pl.when(step == 0)
    def _():
        for here in range(4):

            @pl.when(here_ref[0] == here)
            def _(here=here):
                for pieces, whole in zip(parts, wholes):
                    for flip, piece in enumerate(pieces):
                        at = (here ^ flip) * some
                        whole[at : at + some, :] = piece[:some, :]

        for total, whole in zip(totals, wholes):
            total[...] = jnp.sum(whole[...].astype(F32), axis=0, keepdims=True) / comps

    for out_ref, whole in zip(paired, wholes):
        coupled = jnp.dot(pair_ref[...], whole[...], preferred_element_type=F32)
        own = whole[pl.ds(pl.multiple_of(step * tile, SUB), tile), :]
        out_ref[...] = (own.astype(F32) * coupled).astype(BF16)


def pair_up(here, groups, pair, tile=432):
    comps = pair.shape[0]
    sizes = [len(group) for group in groups]
    cells = [group[0].shape[1] for group in groups]
    flat = sum(groups, [])
    specs = [
        pl.BlockSpec(part.shape, lambda i: (0, 0), pipeline_mode=pl.Buffered(1)) for part in flat
    ]
    out = pl.pallas_call(
        functools.partial(pair_body, tile, sizes),
        grid=(comps // tile,),
        out_shape=[jax.ShapeDtypeStruct((comps, n), BF16) for n in cells]
        + [jax.ShapeDtypeStruct((1, n), F32) for n in cells],
        in_specs=[SMEM] + specs + [pl.BlockSpec((tile, comps), lambda i: (i, 0))],
        out_specs=[pl.BlockSpec((tile, n), lambda i: (i, 0)) for n in cells]
        + [pl.BlockSpec((1, n), lambda i: (0, 0)) for n in cells],
        scratch_shapes=[pltpu.VMEM((comps, n), BF16) for n in cells],
        compiler_params=params(20),
        cost_estimate=pl.CostEstimate(
            flops=comps * comps * sum(cells) // 4,
            bytes_accessed=comps * comps // 4,
            transcendentals=0,
        ),
    )(here, *flat, pair)
    return list(out[: len(groups)]), list(out[len(groups) :])


def apply_ranks(bounds_ref, at, which, paired, kernels, out, wide=256):
    cells = out.shape[1]
    for rank, kernel in which:
        begin, end = bounds_ref[at + rank], bounds_ref[at + rank + 1]
        for column in range(0, cells, wide):
            here = slice(column, column + wide)

            @pl.when((begin < column + wide) & (end > column))
            def _(here=here, column=column, kernel=kernel, begin=begin, end=end):
                term = jnp.dot(kernels[kernel][...], paired[:, here], preferred_element_type=F32)
                number = column + lax.broadcasted_iota(jnp.int32, term.shape, 1)
                mine = (number >= begin) & (number < end)
                out[:, here] = jnp.where(mine, term, out[:, here].astype(F32)).astype(BF16)


def product_cost(kernels, paired):
    flops = len(kernels) * kernels[0].size * sum(p.shape[1] for p in paired)
    moved = 2 * (len(kernels) * kernels[0].size + sum(p.size for p in paired))
    return pl.CostEstimate(flops=flops // 8, bytes_accessed=moved // 8, transcendentals=0)


def transfer_body(uses, strides, kept, bounds_ref, *refs):
    count, chunks = 1 + max(k for use in uses for _, k in use), len(uses)
    kernels, paired, held, outs, (mark,) = split(refs, count, chunks, len(kept), chunks, 1)
    mark[...] = jnp.zeros(mark.shape, F32)
    for chunk, out_ref in enumerate(outs):
        if chunk in kept:
            out_ref[...] = held[kept.index(chunk)][...]
        else:
            out_ref[...] = jnp.zeros(out_ref.shape, BF16)
        apply_ranks(bounds_ref, strides[chunk], uses[chunk], paired[chunk], kernels, out_ref)


def transfer(kernels, uses, strides, bounds, paired, held):
    kept = [i for i, value in enumerate(held) if value is not None]
    operands = [*kernels, *paired, *(held[i] for i in kept)]
    shapes = [jax.ShapeDtypeStruct((kernels[0].shape[0], p.shape[1]), BF16) for p in paired]
    shapes.append(jax.ShapeDtypeStruct((8, 128), F32))
    *held, mark = pl.pallas_call(
        functools.partial(transfer_body, uses, strides, kept),
        out_shape=shapes,
        in_specs=[SMEM] + [VMEM] * len(operands),
        out_specs=[VMEM] * len(shapes),
        compiler_params=params(8),
        cost_estimate=product_cost(kernels, paired),
    )(bounds, *operands)
    return held, mark


def transfer_all(kernels, first, strides, bounds, paired, held, most=6):
    mark = None
    for at in range(0, len(kernels), most):
        some = kernels[at : at + most]
        use = [(first + at + k, k) for k in range(len(some))]
        held, mark = transfer(some, [use] * len(paired), strides, bounds, paired, held)
    return held, mark


def finish_body(
    count, first, groups, strides, bounds_ref, coef_ref, ice_ref, speed_ref, angle_ref, *refs
):
    chunks = len(groups)
    kernels, places, totals, paired, held, parts = split(
        refs, count, chunks, chunks, chunks, chunks, chunks
    )
    out_ref, *works = refs[len(refs) - 1 - chunks :]
    comps, width = out_ref.shape[1:]
    maps = [speed_ref[...].astype(F32), angle_ref[...].astype(F32), ice_ref[...].astype(F32)]
    cosine, sine = coef_ref[:, 4:5], coef_ref[:, 5:6]
    for chunk, rows in enumerate(groups):
        work = works[chunk]
        work[...] = held[chunk][...]
        which = [(first + k, k) for k in range(count)]
        apply_ranks(bounds_ref, strides[chunk], which, paired[chunk], kernels, work)
        matrix = moves(places[chunk][...])
        given = [cells_of(values, rows) for values in maps]
        given = jnp.concatenate(given + [jnp.zeros_like(given[0])] * 5, axis=0)
        given = put_in_order(given.astype(BF16), matrix)
        speed, angle, frozen = 0.3 * given[0:1], given[1:2], given[2:3] > 0.5
        along, across = speed * jnp.cos(angle), speed * jnp.sin(angle)
        total = totals[chunk][...]
        shrink = 1.0 / (1.0 + total)
        base = 1.0 - 0.5 * total * shrink
        energy = parts[chunk][:comps, :].astype(F32)
        forcing = jnp.maximum(cosine * along + sine * across, 0.0)
        result = energy * (base + forcing) + (0.2 * shrink) * work[...].astype(F32)
        result = jnp.where(frozen, energy, result).astype(BF16)
        result = jnp.dot(result, matrix, preferred_element_type=F32).astype(BF16)
        for k, row in enumerate(rows):
            out_ref[row] = result[:, k * width : (k + 1) * width]


def finish(
    kernels, first, groups, strides, bounds, coef, maps, places, totals, paired, held, parts, marks
):
    comps = kernels[0].shape[0]
    rows, width = maps[0].shape
    operands = [coef, *maps, *kernels, *places, *totals, *paired, *held, *parts]
    return pl.pallas_call(
        functools.partial(finish_body, len(kernels), first, groups, strides),
        out_shape=jax.ShapeDtypeStruct((rows, comps, width), BF16),
        in_specs=[SMEM] + [VMEM] * len(operands) + [ANY] * len(marks),
        out_specs=VMEM,
        scratch_shapes=[pltpu.VMEM(value.shape, BF16) for value in held],
        compiler_params=params(20),
        cost_estimate=product_cost(kernels, paired),
    )(bounds, *operands, *marks)


def next_plane(value):
    return lax.ppermute(value, "plane", [(i, (i + 1) % PLANES) for i in range(PLANES)])


def boundaries(top, bottom):
    places = lax.axis_size("place")
    geo, count = ("plane", "place"), PLANES * places
    if places != 2:
        return (
            lax.ppermute(bottom, geo, [(i, i + 1) for i in range(count - 1)]),
            lax.ppermute(top, geo, [(i + 1, i) for i in range(count - 1)]),
        )
    first = lax.axis_index("place") == 0
    inside = lax.ppermute(jnp.where(first, bottom, top), "place", [(0, 1), (1, 0)])
    pairs = [(i, i + 1) for i in range(1, count - 1, 2)]
    outside = lax.ppermute(jnp.where(first, top, bottom), geo, pairs + [(j, i) for i, j in pairs])
    return inside, outside


def before_and_after(inside, outside):
    if lax.axis_size("place") != 2:
        return inside, outside
    first = lax.axis_index("place") == 0
    return jnp.where(first, outside, inside), jnp.where(first, inside, outside)


def with_partners(kernel):
    count = lax.axis_size("place")
    found = [kernel]
    for shift in range(1, count):
        pairs = [(i, (i + shift) % count) for i in range(count)]
        found.append(lax.ppermute(kernel, "place", pairs))
    return found


def ranks_of(owner_map):
    count = lax.axis_size("place")
    plane, place = lax.axis_index("plane"), lax.axis_index("place")
    steps = lax.rem(plane + PLANES - owner_map // count, PLANES)
    shift = lax.rem(place + count - lax.rem(owner_map, count), count)
    return steps * count + shift


def send_spec(value, flip):
    return lax.ppermute(value, "spec", [(i, i ^ flip) for i in range(4)])


def per_device(
    spectrum,
    sea_map,
    depth_factor,
    wind_speed,
    wind_dir,
    ice_mask,
    owner_map,
    pair_kernel,
    transfer_kernel,
):
    comps, rows, width = spectrum.shape
    here = lax.axis_index("spec")

    own_rows = lax.dynamic_slice_in_dim(transfer_kernel[0], here * comps, comps, axis=0)
    one_back = next_plane(own_rows)
    sea = sea_map.astype(F32)
    top = spectrum[:, 0] * sea_map[0].astype(BF16)
    bottom = spectrum[:, rows - 1] * sea_map[rows - 1].astype(BF16)
    halos = boundaries(top, bottom)
    x = spectrum.transpose(1, 0, 2)

    component = here * comps + jnp.arange(comps, dtype=jnp.int32)
    frequency = (component // NDIR).astype(F32)
    heading = 2.0 * math.pi * ((component % NDIR).astype(F32) + 0.5) / NDIR
    cosine, sine = jnp.cos(heading), jnp.sin(heading)
    gain = jnp.float32(1.1) ** (-0.5 * frequency)
    coef = jnp.stack(
        [
            0.7 * gain * jnp.abs(cosine),
            0.7 * gain * jnp.abs(sine),
            (cosine > 0).astype(F32),
            (sine > 0).astype(F32),
            cosine,
            sine,
        ],
        axis=1,
    )

    here_ref = jnp.reshape(here, (1,)).astype(jnp.int32)
    wide = 3 * rows // 8
    one, two = 1 + wide, 1 + 2 * wide
    groups = [list(range(1, one)), list(range(one, two)), [0] + list(range(two, rows))]

    def meet(part):
        return [send_spec(part, 1), send_spec(part, 2)]

    count = lax.axis_size("place")
    owners = PLANES * count
    rank_map = ranks_of(owner_map)
    kinds = jnp.arange(owners + 1, dtype=jnp.int32)
    bounds = []
    for group in groups:
        ranks = jnp.concatenate([rank_map[row] for row in group])
        bounds.append(jnp.sum((ranks[None, :] < kinds[:, None]).astype(jnp.int32), axis=1))
    bounds = jnp.concatenate(bounds)
    strides = [i * (owners + 1) for i in range(len(groups))]

    def move_rows(group, west, east):
        return propagate(
            group, owners, x, west, east, sea, depth_factor, coef, rank_map
        )

    none = jnp.zeros_like(top)
    parts, places = zip(*(move_rows(group, none, none) for group in groups[:2]))
    parts, places = list(parts), list(places)
    near = [meet(parts[0])]
    near[0], sent = lax.optimization_barrier((near[0], parts[1]))
    near.append(meet(sent))
    one_back, halos, near = lax.optimization_barrier((one_back, halos, near))

    two_back = next_plane(one_back)
    crossed = [send_spec(near[0][1], 1), send_spec(near[1][0], 2)]
    part, place = move_rows(groups[2], *before_and_after(*halos))
    parts.append(part)
    places.append(place)
    crossed, sent = lax.optimization_barrier((crossed, parts[2]))
    near.append(meet(sent))
    found = with_partners(own_rows) + with_partners(one_back)
    paired, totals = pair_up(
        here_ref, [[parts[i], *near[i], crossed[i]] for i in range(2)], pair_kernel
    )
    two_back, near[2], totals = lax.optimization_barrier((two_back, near[2], totals))

    three_back = next_plane(two_back)
    last_cross = send_spec(near[2][1], 1)
    held, mark = transfer_all(found, 0, strides[:2], bounds, paired, [None] * 2)
    last_cross, mark = lax.optimization_barrier((last_cross, mark))
    more, total = pair_up(here_ref, [[parts[2], *near[2], last_cross]], pair_kernel)
    paired, totals = paired + more, totals + total
    later = with_partners(two_back)
    if 3 * count <= 6:
        kernels = later + found
        some = [(2 * count + k, k) for k in range(count)]
        every = some + [(k, count + k) for k in range(2 * count)]
        held, other = transfer(
            kernels, [some, some, every], strides, bounds, paired, [*held, None]
        )
    else:
        more, _ = transfer_all(found, 0, strides[2:], bounds, paired[2:], [None])
        held, other = transfer_all(later, 2 * count, strides, bounds, paired, [*held, *more])
    three_back, other = lax.optimization_barrier((three_back, other))
    last = with_partners(three_back)
    if last[:-1]:
        held, _ = transfer_all(last[:-1], 3 * count, strides, bounds, paired, held)
    maps = [ice_mask, wind_speed, wind_dir]
    out = finish(
        last[-1:],
        owners - 1,
        groups,
        strides,
        bounds,
        coef,
        maps,
        places,
        totals,
        paired,
        held,
        parts,
        [mark, other],
    )
    return out.transpose(1, 0, 2)


def solution(mesh):
    spec, geo = mesh.shape["spec"], mesh.shape["geo"]
    split = Mesh(
        mesh.devices.reshape(spec, PLANES, geo // PLANES), ("spec", "plane", "place")
    )
    tiles = ("plane", "place")
    placed = (
        P("spec", tiles, None),
        P(tiles, None),
        P(tiles, None),
        P(tiles, None),
        P(tiles, None),
        P(tiles, None),
        P(tiles, None),
        P(),
        P(tiles, None, None),
    )
    return jax.shard_map(
        per_device, mesh=split, in_specs=placed, out_specs=P("spec", tiles, None), check_vma=False
    )
```

time: 115 us -> 100 us (0.87)
  local copies, waits for them, and re-layouts: 20.6 us -> 6.62 us
  waiting for transfers between devices: 21.8 us -> 29.1 us
  Pallas kernels: 49.2 us -> 43.4 us
  starting transfers between devices: 19.7 us -> 18 us
    unnamed x80 -> x22, local copies, waits for them, and re-layouts: 15.6 us -> 3.78 us
    pallas_call x11 -> x9, Pallas kernels: 49.2 us -> 43.4 us  [the longest x3 14.4 us: transfer(): pl.pallas_call(functools.partial(transfer_body, uses, strides, kept), out...]
    ppermute x3, waiting for transfers between devices: 0.01 us -> 4.82 us  [next_plane(): lax.ppermute(value, 'plane', [(i, (i + 1) % PLANES) for i in range(PLANES)])]
    ppermute x10 -> x9, waiting for transfers between devices: 14.3 us -> 16.9 us  [send_spec(): return lax.ppermute(value, 'spec', [(i, i ^ flip) for i in range(4)])]
    slice x12 -> x0, local copies, waits for them, and re-layouts: 1.89 us -> none  [the longest x1 0.93 us: per_device(): near[2][1][:, :half]]
    ppermute x10 -> x9, starting transfers between devices: 8.55 us -> 7.23 us  [send_spec(): return lax.ppermute(value, 'spec', [(i, i ^ flip) for i in range(4)])]
  transfers between devices with their start and end apart: 19 -> 18, of which waited for: 4 -> 6; matrix products, arithmetic and copies ran while one was open for 5% -> 3% of each run, Pallas kernels for 37% -> 34%
where the time goes in v2:
time: 100 us; the launch traced here: 99.6 us
  Pallas kernels  43.4 us (43%)
  waiting for transfers between devices  29.1 us (29%)
  starting transfers between devices  18 us (18%)
  local copies, waits for them, and re-layouts  6.62 us (7%)
  other arithmetic  2.22 us (2%)
    ppermute x9, waiting for transfers between devices, send_spec(): return lax.ppermute(value, 'spec', [(i, i ^ flip) for i in range(4)])  16.9 us
    pallas_call x3, Pallas kernels, transfer(): pl.pallas_call(functools.partial(transfer_body, uses, strides, kept), out...  14.4 us
    pallas_call x2, Pallas kernels, pair_up(): pl.pallas_call(functools.partial(pair_body, tile, sizes), grid=(comps //...  12.7 us
    pallas_call x3, Pallas kernels, propagate(): pl.pallas_call(functools.partial(propagate_kernel, wanted, count), out_sh...  10.4 us
    ppermute x1, waiting for transfers between devices, boundaries(): lax.ppermute(jnp.where(first, top, bottom), geo, pairs + [(j, i) for i, j...  7.31 us
    ppermute x9, starting transfers between devices, send_spec(): return lax.ppermute(value, 'spec', [(i, i ^ flip) for i in range(4)])  7.23 us
    pallas_call x1, Pallas kernels, finish(): pl.pallas_call(functools.partial(finish_body, len(kernels), first, groups...  5.9 us
    ppermute x3, waiting for transfers between devices, next_plane(): lax.ppermute(value, 'plane', [(i, (i + 1) % PLANES) for i in range(PLANES)])  4.82 us
  transfers between devices with their start and end apart: 18, of which 6 were waited for; matrix products, arithmetic and copies ran while one was open for 3% of the time, Pallas kernels for 34%

profile of v2, /device:TPU:1, one launch (start us, length us, event | category | flops | bytes accessed | tf_op | source)
XLA Modules:
  0.0 99.6 jit_solution(11808893355676604283)
XLA Ops:
  0.0 0.1 compare_convert_fusion
  0.1 0.1 abs_multiply_fusion
  0.2 0.1 fusion.13
  0.3 0.1 copy.28.coef_ref
  0.4 0.0 copy-start.6
  0.4 0.0 copy-start.7
  0.4 0.0 copy-start.2
  0.5 1.7 %copy.32 = bf16[324,16,128]{2,0,1:T(8,128)(2,1)S(1)} copy(bf16[324,16,128]{2,1,0:T(8,128)(2,1)} %param.9) | data formatting | bytes 2654208 | tf_op args[0]
  2.2 3.9 %shard_map.91 = (bf16[336,768]{1,0:T(8,128)(2,1)}, f32[1,768]{1,0:T(1,128)S(1)}) custom-call(bf16[16,324,128]{2,1,0:T(8,128)(2,1)S(1)} %bitcast.83, bf16[324,128]{1,0:T(8,128)(2,1)S(1)} %broadcast_in_dim.2.west_ref.east_ref, bf16[324,128]{1,0:T(8,128)(2,1)S(1)} %broadcast_in_dim.2.west_ref.east_ref, f32[16,128]{1,0:T(8,128)S(1)} %get-tuple-element.99.sea_ref, ...), custom_call_target="tpu_custom_call" | custom-call | flops 497664 | bytes 248832 | tf_op jit(solution)/shard_map/pallas_call | solution.py:126
  6.2 2.0 %collective-permute-start.3 = (bf16[336,768]{1,0:T(8,128)(2,1)}, bf16[336,768]{1,0:T(8,128)(2,1)}, u32[]{:S(2)}, u32[]{:S(2)}) collective-permute-start(bf16[336,768]{1,0:T(8,128)(2,1)} %get-tuple-element.49.refs_0_.refs_13_), channel_id=1, source_target_pairs={{0,8},{8,0},{16,24},{24,16},{1,9},{9,1},{17,25},{25,17},{2,10},{10... | collective-permute-start | bytes 1548296 | tf_op jit(solution)/shard_map/ppermute | solution.py:357
  8.2 1.2 %collective-permute-start.4 = (bf16[336,768]{1,0:T(8,128)(2,1)}, bf16[336,768]{1,0:T(8,128)(2,1)}, u32[]{:S(2)}, u32[]{:S(2)}) collective-permute-start(bf16[336,768]{1,0:T(8,128)(2,1)} %get-tuple-element.49.refs_0_.refs_13_), channel_id=1, source_target_pairs={{0,16},{8,24},{16,0},{24,8},{1,17},{9,25},{17,1},{25,9},{2,18},{10... | collective-permute-start | bytes 1548296 | tf_op jit(solution)/shard_map/ppermute | solution.py:357
  9.4 1.4 %dynamic-slice_bitcast_fusion.refs_0_.refs_2_ = bf16[324,1296]{1,0:T(8,128)(2,1)S(1)} fusion(bf16[1,1296,1296]{2,1,0:T(8,128)(2,1)} %param.17, s32[]{:T(128)S(6)} %select_n.81), kind=kLoop, calls=%fused_computation | loop fusion | bytes 1679620 | tf_op jit(solution)/shard_map/dynamic_slice | solution.py:374
  10.9 1.3 %collective-permute-start = (bf16[324,1296]{1,0:T(8,128)(2,1)S(1)}, bf16[324,1296]{1,0:T(8,128)(2,1)S(1)}, u32[]{:S(2)}, u32[]{:S(2)}) collective-permute-start(bf16[324,1296]{1,0:T(8,128)(2,1)S(1)} %dynamic-slice_bitcast_fusion.refs_0_.refs_2_), channel_id=1, source_target_pairs={{0,2},{2,4},{4,6},{6,0},{1,3},{3,5},{5,7},{7,1},{8,10},{10,12},{12... | collective-permute-start | bytes 2519432 | tf_op jit(solution)/shard_map/ppermute | solution.py:314
  12.2 3.9 %shard_map.92 = (bf16[336,768]{1,0:T(8,128)(2,1)}, f32[1,768]{1,0:T(1,128)S(1)}) custom-call(bf16[16,324,128]{2,1,0:T(8,128)(2,1)S(1)} %bitcast.84, bf16[324,128]{1,0:T(8,128)(2,1)S(1)} %broadcast_in_dim.2.west_ref.east_ref, bf16[324,128]{1,0:T(8,128)(2,1)S(1)} %broadcast_in_dim.2.west_ref.east_ref, f32[16,128]{1,0:T(8,128)S(1)} %get-tuple-element.99.sea_ref, ...), custom_call_target="tpu_custom_call" | custom-call | flops 497664 | bytes 248832 | tf_op jit(solution)/shard_map/pallas_call | solution.py:126
  16.1 3.9 %collective-permute-done.3.refs_1_ = bf16[336,768]{1,0:T(8,128)(2,1)} collective-permute-done((bf16[336,768]{1,0:T(8,128)(2,1)}, bf16[336,768]{1,0:T(8,128)(2,1)}, u32[]{:S(2)}, u32[]{:S(2)}) %collective-permute-start.3) | collective-permute-done | bytes 516128 | tf_op jit(solution)/shard_map/ppermute | solution.py:357
  20.0 0.8 collective-permute-done.4.refs_2_
  20.8 0.4 collective-permute-start.5
  21.2 1.2 %collective-permute-start.6 = (bf16[336,768]{1,0:T(8,128)(2,1)}, bf16[336,768]{1,0:T(8,128)(2,1)}, u32[]{:S(2)}, u32[]{:S(2)}) collective-permute-start(bf16[336,768]{1,0:T(8,128)(2,1)} %get-tuple-element.53.refs_4_.refs_14_), channel_id=1, source_target_pairs={{0,16},{8,24},{16,0},{24,8},{1,17},{9,25},{17,1},{25,9},{2,18},{10... | collective-permute-start | bytes 1548296 | tf_op jit(solution)/shard_map/ppermute | solution.py:357
  22.4 0.7 broadcast_select_fusion.2
  23.1 2.4 %collective-permute-start.1 = (bf16[324,128]{1,0:T(8,128)(2,1)}, bf16[324,128]{1,0:T(8,128)(2,1)S(1)}, u32[]{:S(2)}, u32[]{:S(2)}) collective-permute-start(bf16[324,128]{1,0:T(8,128)(2,1)} %get-tuple-element.94), channel_id=1, source_target_pairs={{0,1},{1,0},{2,3},{3,2},{4,5},{5,4},{6,7},{7,6},{8,9},{9,8},{10,11... | collective-permute-start | bytes 248840 | tf_op jit(solution)/shard_map/ppermute | solution.py:326
  25.5 3.1 %collective-permute-start.2 = (bf16[324,128]{1,0:T(8,128)(2,1)}, bf16[324,128]{1,0:T(8,128)(2,1)}, u32[]{:S(2)}, u32[]{:S(2)}) collective-permute-start(bf16[324,128]{1,0:T(8,128)(2,1)} %get-tuple-element.93), channel_id=1, source_target_pairs={{1,2},{3,4},{5,6},{2,1},{4,3},{6,5},{9,10},{11,12},{13,14},{10,9},... | collective-permute-start | bytes 248840 | tf_op jit(solution)/shard_map/ppermute | solution.py:328
  28.6 0.0 collective-permute-done.1
  28.6 0.1 collective-permute-start.14
  28.7 7.3 %collective-permute-done.2 = bf16[324,128]{1,0:T(8,128)(2,1)} collective-permute-done((bf16[324,128]{1,0:T(8,128)(2,1)}, bf16[324,128]{1,0:T(8,128)(2,1)}, u32[]{:S(2)}, u32[]{:S(2)}) %collective-permute-start.2) | collective-permute-done | bytes 82976 | tf_op jit(solution)/shard_map/ppermute | solution.py:328
  36.0 0.0 collective-permute-done.refs_2_.refs_4_
  36.0 0.0 collective-permute-done.5.refs_5_
  36.0 0.0 collective-permute-done.6.refs_6_
  36.0 0.5 collective-permute-start.8
  36.5 0.4 collective-permute-start.9
  36.8 0.3 collective-permute-start.7
  37.1 0.9 broadcast_select_fusion
  38.1 2.6 %shard_map.93 = (bf16[336,512]{1,0:T(8,128)(2,1)S(1)}, f32[1,512]{1,0:T(1,128)S(1)}) custom-call(bf16[16,324,128]{2,1,0:T(8,128)(2,1)S(1)} %bitcast.85, bf16[324,128]{1,0:T(8,128)(2,1)S(1)} %get-tuple-element.98.west_ref, bf16[324,128]{1,0:T(8,128)(2,1)S(1)} %get-tuple-element.97.east_ref, f32[16,128]{1,0:T(8,128)S(1)} %get-tuple-element.99.sea_ref, ...), custom_call_target="tpu_custom_call" | custom-call | flops 331776 | bytes 165888 | tf_op jit(solution)/shard_map/pallas_call | solution.py:126
  40.6 9.2 %collective-permute-done.8.refs_3_ = bf16[336,768]{1,0:T(8,128)(2,1)S(1)} collective-permute-done((bf16[336,768]{1,0:T(8,128)(2,1)}, bf16[336,768]{1,0:T(8,128)(2,1)S(1)}, u32[]{:S(2)}, u32[]{:S(2)}) %collective-permute-start.8) | collective-permute-done | bytes 516128 | tf_op jit(solution)/shard_map/ppermute | solution.py:357
  49.8 0.0 collective-permute-done.9.refs_7_
  49.8 1.3 %collective-permute-start.10 = (bf16[336,512]{1,0:T(8,128)(2,1)S(1)}, bf16[336,512]{1,0:T(8,128)(2,1)S(1)}, u32[]{:S(2)}, u32[]{:S(2)}) collective-permute-start(bf16[336,512]{1,0:T(8,128)(2,1)S(1)} %get-tuple-element.60.refs_0_.refs_15_), channel_id=1, source_target_pairs={{0,8},{8,0},{16,24},{24,16},{1,9},{9,1},{17,25},{25,17},{2,10},{10... | collective-permute-start | bytes 1032200 | tf_op jit(solution)/shard_map/ppermute | solution.py:357
  51.1 0.0 collective-permute-start.11
  51.1 1.9 %collective-permute-start.15 = (bf16[324,1296]{1,0:T(8,128)(2,1)S(1)}, bf16[324,1296]{1,0:T(8,128)(2,1)S(1)}, u32[]{:S(2)}, u32[]{:S(2)}) collective-permute-start(bf16[324,1296]{1,0:T(8,128)(2,1)S(1)} %collective-permute-done.refs_2_.refs_4_), channel_id=1, source_target_pairs={{0,1},{1,0},{2,3},{3,2},{4,5},{5,4},{6,7},{7,6},{8,9},{9,8},{10,11... | collective-permute-start | bytes 2519432 | tf_op jit(solution)/shard_map/ppermute | solution.py:344
  53.0 2.0 %copy-done = bf16[1296,1296]{1,0:T(8,128)(2,1)S(1)} copy-done((bf16[1296,1296]{1,0:T(8,128)(2,1)S(1)}, bf16[1296,1296]{1,0:T(8,128)(2,1)}, u32[]{:S(2)}) %copy-start) | copy-done | bytes 3359256
  55.1 9.8 %shard_map.94 = (bf16[1296,768]{1,0:T(8,128)(2,1)S(1)}, bf16[1296,768]{1,0:T(8,128)(2,1)S(1)}, f32[1,768]{1,0:T(1,128)S(1)}, f32[1,768]{1,0:T(1,128)S(1)}) custom-call(s32[1]{0:T(128)} %bitcast.22.here_ref, bf16[336,768]{1,0:T(8,128)(2,1)} %get-tuple-element.49.refs_0_.refs_13_, bf16[336,768]{1,0:T(8,128)(2,1)} %collective-permute-done.3.refs_1_, ...), custom_call_target="tpu_custom_call" | custom-call | flops 644972544 | bytes 419904 | tf_op jit(solution)/shard_map/pallas_call | solution.py:185
  64.8 0.0 collective-permute-done.7.refs_0_
  64.8 0.0 collective-permute-done.10.refs_1_
  64.8 0.0 collective-permute-done.11.refs_2_
  64.9 0.1 collective-permute-start.13
  64.9 0.4 collective-permute-start.12
  65.3 0.3 collective-permute-start.16
  65.6 0.1 convert_reduce_fusion.2
  65.8 0.1 convert_reduce_fusion
  65.9 0.1 pad_add_fusion.1.bounds_ref
  66.0 0.0 collective-permute-done.14.refs_1_.refs_3_
  66.0 0.0 collective-permute-done.15.refs_3_.refs_5_
  66.0 0.0 copy-start.1
  66.0 5.2 %shard_map.95 = (bf16[324,768]{1,0:T(8,128)(2,1)S(1)}, bf16[324,768]{1,0:T(8,128)(2,1)S(1)}, f32[8,128]{1,0:T(8,128)S(1)}) custom-call(s32[27]{0:T(128)S(1)} %pad_add_fusion.1.bounds_ref, bf16[324,1296]{1,0:T(8,128)(2,1)S(1)} %dynamic-slice_bitcast_fusion.refs_0_.refs_2_, bf16[324,1296]{1,0:T(8,128)(2,1)S(1)} %collective-permute-done.14.refs_1_.refs_3_, ...), custom_call_target="tpu_custom_call" | custom-call | flops 322486272 | bytes 917568 | tf_op jit(solution)/shard_map/pallas_call | solution.py:242
  71.2 3.1 %collective-permute-done.16.refs_3_ = bf16[336,512]{1,0:T(8,128)(2,1)S(1)} collective-permute-done((bf16[336,512]{1,0:T(8,128)(2,1)S(1)}, bf16[336,512]{1,0:T(8,128)(2,1)S(1)}, u32[]{:S(2)}, u32[]{:S(2)}) %collective-permute-start.16) | collective-permute-done | bytes 344096 | tf_op jit(solution)/shard_map/ppermute | solution.py:357
  74.3 0.0 copy-done.1
  74.3 2.9 %shard_map.96 = (bf16[1296,512]{1,0:T(8,128)(2,1)S(1)}, f32[1,512]{1,0:T(1,128)S(1)}) custom-call(s32[1]{0:T(128)} %bitcast.22.here_ref, bf16[336,512]{1,0:T(8,128)(2,1)S(1)} %get-tuple-element.60.refs_0_.refs_15_, bf16[336,512]{1,0:T(8,128)(2,1)S(1)} %collective-permute-done.10.refs_1_, bf16[336,512]{1,0:T(8,128)(2,1)S(1)} %collective-permute-done.11.refs_2_, ...), custom_call_target="tpu_custom_call" | custom-call | flops 214990848 | bytes 419904 | tf_op jit(solution)/shard_map/pallas_call | solution.py:185
  77.2 0.0 collective-permute-done.13.refs_1_
  77.2 6.4 %shard_map.97 = (bf16[324,768]{1,0:T(8,128)(2,1)S(1)}, bf16[324,768]{1,0:T(8,128)(2,1)S(1)}, bf16[324,512]{1,0:T(8,128)(2,1)S(1)}, f32[8,128]{1,0:T(8,128)S(1)}) custom-call(s32[27]{0:T(128)S(1)} %pad_add_fusion.1.bounds_ref, bf16[324,1296]{1,0:T(8,128)(2,1)S(1)} %collective-permute-done.7.refs_0_, bf16[324,1296]{1,0:T(8,128)(2,1)S(1)} %collective-permute-done.13.refs_1_, ...), custom_call_target="tpu_custom_call" | custom-call | flops 644972544 | bytes 1293408 | tf_op jit(solution)/shard_map/pallas_call | solution.py:242
  83.6 4.8 %collective-permute-done.12.refs_0_ = bf16[324,1296]{1,0:T(8,128)(2,1)S(1)} collective-permute-done((bf16[324,1296]{1,0:T(8,128)(2,1)S(1)}, bf16[324,1296]{1,0:T(8,128)(2,1)S(1)}, u32[]{:S(2)}, u32[]{:S(2)}) %collective-permute-start.12) | collective-permute-done | bytes 839840 | tf_op jit(solution)/shard_map/ppermute | solution.py:314
  88.4 1.3 %collective-permute-start.17 = (bf16[324,1296]{1,0:T(8,128)(2,1)S(1)}, bf16[324,1296]{1,0:T(8,128)(2,1)S(1)}, u32[]{:S(2)}, u32[]{:S(2)}) collective-permute-start(bf16[324,1296]{1,0:T(8,128)(2,1)S(1)} %collective-permute-done.12.refs_0_), channel_id=1, source_target_pairs={{0,1},{1,0},{2,3},{3,2},{4,5},{5,4},{6,7},{7,6},{8,9},{9,8},{10,11... | collective-permute-start | bytes 2519432 | tf_op jit(solution)/shard_map/ppermute | solution.py:344
  89.7 2.8 %shard_map.98 = (bf16[324,768]{1,0:T(8,128)(2,1)S(1)}, bf16[324,768]{1,0:T(8,128)(2,1)S(1)}, bf16[324,512]{1,0:T(8,128)(2,1)S(1)}, f32[8,128]{1,0:T(8,128)}) custom-call(s32[27]{0:T(128)S(1)} %pad_add_fusion.1.bounds_ref, bf16[324,1296]{1,0:T(8,128)(2,1)S(1)} %collective-permute-done.12.refs_0_, ...), custom_call_target="tpu_custom_call" | custom-call | flops 107495424 | bytes 768528 | tf_op jit(solution)/shard_map/pallas_call | solution.py:242
  92.5 0.0 collective-permute-done.17.refs_0_
  92.5 0.0 copy-done.3
  92.5 5.9 %shard_map.99 = bf16[16,324,128]{2,1,0:T(8,128)(2,1)S(1)} custom-call(s32[27]{0:T(128)S(1)} %pad_add_fusion.1.bounds_ref, f32[324,6]{1,0:T(8,128)S(1)} %copy.28.coef_ref, s32[16,128]{1,0:T(8,128)S(1)} %copy-done.3, bf16[16,128]{1,0:T(8,128)(2,1)S(1)} %copy-done.4, bf16[16,128]{1,0:T(8,128)(2,1)S(1)} %copy-done.5, ...), custom_call_target="tpu_custom_call" | custom-call | flops 107495424 | bytes 768528 | tf_op jit(solution)/shard_map/pallas_call | solution.py:302
  98.4 1.2 %copy.29 = bf16[324,16,128]{2,1,0:T(8,128)(2,1)} copy(bf16[324,16,128]{2,0,1:T(8,128)(2,1)S(1)} %bitcast.86) | data formatting | bytes 2654208 | tf_op jit(solution)/shard_map/transpose | solution.py:481
  (24 shorter events, 0.1 us)
Async XLA Ops:
  0.4 1.7 %copy-start.6 = (s32[16,128]{1,0:T(8,128)S(1)}, s32[16,128]{1,0:T(8,128)}, u32[]{:S(2)}) copy-start(s32[16,128]{1,0:T(8,128)} %param.10) | copy-start | bytes 24580
  0.4 1.7 %copy-start.7 = (s32[16,128]{1,0:T(8,128)S(1)}, s32[16,128]{1,0:T(8,128)}, u32[]{:S(2)}) copy-start(s32[16,128]{1,0:T(8,128)} %param.15) | copy-start | bytes 24580
  0.4 1.8 %copy-start.2 = (f32[16,128]{1,0:T(8,128)S(1)}, f32[16,128]{1,0:T(8,128)}, u32[]{:S(2)}) copy-start(f32[16,128]{1,0:T(8,128)} %depth_ref.5) | copy-start | bytes 24580
  6.2 13.8 %collective-permute-start.3 = (bf16[336,768]{1,0:T(8,128)(2,1)}, bf16[336,768]{1,0:T(8,128)(2,1)}, u32[]{:S(2)}, u32[]{:S(2)}) collective-permute-start(bf16[336,768]{1,0:T(8,128)(2,1)} %get-tuple-element.49.refs_0_.refs_13_), channel_id=1, source_target_pairs={{0,8},{8,0},{16,24},{24,16},{1,9},{9,1},{17,25},{25,17},{2,10},{10... | collective-permute-start | bytes 1548296 | tf_op jit(solution)/shard_map/ppermute | solution.py:357
  8.2 12.6 %collective-permute-start.4 = (bf16[336,768]{1,0:T(8,128)(2,1)}, bf16[336,768]{1,0:T(8,128)(2,1)}, u32[]{:S(2)}, u32[]{:S(2)}) collective-permute-start(bf16[336,768]{1,0:T(8,128)(2,1)} %get-tuple-element.49.refs_0_.refs_13_), channel_id=1, source_target_pairs={{0,16},{8,24},{16,0},{24,8},{1,17},{9,25},{17,1},{25,9},{2,18},{10... | collective-permute-start | bytes 1548296 | tf_op jit(solution)/shard_map/ppermute | solution.py:357
  10.9 25.1 %collective-permute-start = (bf16[324,1296]{1,0:T(8,128)(2,1)S(1)}, bf16[324,1296]{1,0:T(8,128)(2,1)S(1)}, u32[]{:S(2)}, u32[]{:S(2)}) collective-permute-start(bf16[324,1296]{1,0:T(8,128)(2,1)S(1)} %dynamic-slice_bitcast_fusion.refs_0_.refs_2_), channel_id=1, source_target_pairs={{0,2},{2,4},{4,6},{6,0},{1,3},{3,5},{5,7},{7,1},{8,10},{10,12},{12... | collective-permute-start | bytes 2519432 | tf_op jit(solution)/shard_map/ppermute | solution.py:314
  20.8 15.2 %collective-permute-start.5 = (bf16[336,768]{1,0:T(8,128)(2,1)}, bf16[336,768]{1,0:T(8,128)(2,1)}, u32[]{:S(2)}, u32[]{:S(2)}) collective-permute-start(bf16[336,768]{1,0:T(8,128)(2,1)} %get-tuple-element.53.refs_4_.refs_14_), channel_id=1, source_target_pairs={{0,8},{8,0},{16,24},{24,16},{1,9},{9,1},{17,25},{25,17},{2,10},{10... | collective-permute-start | bytes 1548296 | tf_op jit(solution)/shard_map/ppermute | solution.py:357
  21.2 14.8 %collective-permute-start.6 = (bf16[336,768]{1,0:T(8,128)(2,1)}, bf16[336,768]{1,0:T(8,128)(2,1)}, u32[]{:S(2)}, u32[]{:S(2)}) collective-permute-start(bf16[336,768]{1,0:T(8,128)(2,1)} %get-tuple-element.53.refs_4_.refs_14_), channel_id=1, source_target_pairs={{0,16},{8,24},{16,0},{24,8},{1,17},{9,25},{17,1},{25,9},{2,18},{10... | collective-permute-start | bytes 1548296 | tf_op jit(solution)/shard_map/ppermute | solution.py:357
  23.1 5.5 %collective-permute-start.1 = (bf16[324,128]{1,0:T(8,128)(2,1)}, bf16[324,128]{1,0:T(8,128)(2,1)S(1)}, u32[]{:S(2)}, u32[]{:S(2)}) collective-permute-start(bf16[324,128]{1,0:T(8,128)(2,1)} %get-tuple-element.94), channel_id=1, source_target_pairs={{0,1},{1,0},{2,3},{3,2},{4,5},{5,4},{6,7},{7,6},{8,9},{9,8},{10,11... | collective-permute-start | bytes 248840 | tf_op jit(solution)/shard_map/ppermute | solution.py:326
  25.5 10.5 %collective-permute-start.2 = (bf16[324,128]{1,0:T(8,128)(2,1)}, bf16[324,128]{1,0:T(8,128)(2,1)}, u32[]{:S(2)}, u32[]{:S(2)}) collective-permute-start(bf16[324,128]{1,0:T(8,128)(2,1)} %get-tuple-element.93), channel_id=1, source_target_pairs={{1,2},{3,4},{5,6},{2,1},{4,3},{6,5},{9,10},{11,12},{13,14},{10,9},... | collective-permute-start | bytes 248840 | tf_op jit(solution)/shard_map/ppermute | solution.py:328
  28.6 37.4 %collective-permute-start.14 = (bf16[324,1296]{1,0:T(8,128)(2,1)S(1)}, bf16[324,1296]{1,0:T(8,128)(2,1)S(1)}, u32[]{:S(2)}, u32[]{:S(2)}) collective-permute-start(bf16[324,1296]{1,0:T(8,128)(2,1)S(1)} %dynamic-slice_bitcast_fusion.refs_0_.refs_2_), channel_id=1, source_target_pairs={{0,1},{1,0},{2,3},{3,2},{4,5},{5,4},{6,7},{7,6},{8,9},{9,8},{10,11... | collective-permute-start | bytes 2519432 | tf_op jit(solution)/shard_map/ppermute | solution.py:344
  36.0 13.8 %collective-permute-start.8 = (bf16[336,768]{1,0:T(8,128)(2,1)}, bf16[336,768]{1,0:T(8,128)(2,1)S(1)}, u32[]{:S(2)}, u32[]{:S(2)}) collective-permute-start(bf16[336,768]{1,0:T(8,128)(2,1)} %collective-permute-done.4.refs_2_), channel_id=1, source_target_pairs={{0,8},{8,0},{16,24},{24,16},{1,9},{9,1},{17,25},{25,17},{2,10},{10... | collective-permute-start | bytes 1548296 | tf_op jit(solution)/shard_map/ppermute | solution.py:357
  36.5 13.4 %collective-permute-start.9 = (bf16[336,768]{1,0:T(8,128)(2,1)}, bf16[336,768]{1,0:T(8,128)(2,1)S(1)}, u32[]{:S(2)}, u32[]{:S(2)}) collective-permute-start(bf16[336,768]{1,0:T(8,128)(2,1)} %collective-permute-done.5.refs_5_), channel_id=1, source_target_pairs={{0,16},{8,24},{16,0},{24,8},{1,17},{9,25},{17,1},{25,9},{2,18},{10... | collective-permute-start | bytes 1548296 | tf_op jit(solution)/shard_map/ppermute | solution.py:357
  36.8 28.0 %collective-permute-start.7 = (bf16[324,1296]{1,0:T(8,128)(2,1)S(1)}, bf16[324,1296]{1,0:T(8,128)(2,1)S(1)}, u32[]{:S(2)}, u32[]{:S(2)}) collective-permute-start(bf16[324,1296]{1,0:T(8,128)(2,1)S(1)} %collective-permute-done.refs_2_.refs_4_), channel_id=1, source_target_pairs={{0,2},{2,4},{4,6},{6,0},{1,3},{3,5},{5,7},{7,1},{8,10},{10,12},{12... | collective-permute-start | bytes 2519432 | tf_op jit(solution)/shard_map/ppermute | solution.py:314
  49.8 15.0 %collective-permute-start.10 = (bf16[336,512]{1,0:T(8,128)(2,1)S(1)}, bf16[336,512]{1,0:T(8,128)(2,1)S(1)}, u32[]{:S(2)}, u32[]{:S(2)}) collective-permute-start(bf16[336,512]{1,0:T(8,128)(2,1)S(1)} %get-tuple-element.60.refs_0_.refs_15_), channel_id=1, source_target_pairs={{0,8},{8,0},{16,24},{24,16},{1,9},{9,1},{17,25},{25,17},{2,10},{10... | collective-permute-start | bytes 1032200 | tf_op jit(solution)/shard_map/ppermute | solution.py:357
  51.1 13.8 %collective-permute-start.11 = (bf16[336,512]{1,0:T(8,128)(2,1)S(1)}, bf16[336,512]{1,0:T(8,128)(2,1)S(1)}, u32[]{:S(2)}, u32[]{:S(2)}) collective-permute-start(bf16[336,512]{1,0:T(8,128)(2,1)S(1)} %get-tuple-element.60.refs_0_.refs_15_), channel_id=1, source_target_pairs={{0,16},{8,24},{16,0},{24,8},{1,17},{9,25},{17,1},{25,9},{2,18},{10... | collective-permute-start | bytes 1032200 | tf_op jit(solution)/shard_map/ppermute | solution.py:357
  51.1 14.9 %collective-permute-start.15 = (bf16[324,1296]{1,0:T(8,128)(2,1)S(1)}, bf16[324,1296]{1,0:T(8,128)(2,1)S(1)}, u32[]{:S(2)}, u32[]{:S(2)}) collective-permute-start(bf16[324,1296]{1,0:T(8,128)(2,1)S(1)} %collective-permute-done.refs_2_.refs_4_), channel_id=1, source_target_pairs={{0,1},{1,0},{2,3},{3,2},{4,5},{5,4},{6,7},{7,6},{8,9},{9,8},{10,11... | collective-permute-start | bytes 2519432 | tf_op jit(solution)/shard_map/ppermute | solution.py:344
  53.0 2.0 %copy-start = (bf16[1296,1296]{1,0:T(8,128)(2,1)S(1)}, bf16[1296,1296]{1,0:T(8,128)(2,1)}, u32[]{:S(2)}) copy-start(bf16[1296,1296]{1,0:T(8,128)(2,1)} %refs_4_.1) | copy-start | bytes 10077700
  64.9 12.3 %collective-permute-start.13 = (bf16[324,1296]{1,0:T(8,128)(2,1)S(1)}, bf16[324,1296]{1,0:T(8,128)(2,1)S(1)}, u32[]{:S(2)}, u32[]{:S(2)}) collective-permute-start(bf16[324,1296]{1,0:T(8,128)(2,1)S(1)} %collective-permute-done.7.refs_0_), channel_id=1, source_target_pairs={{0,1},{1,0},{2,3},{3,2},{4,5},{5,4},{6,7},{7,6},{8,9},{9,8},{10,11... | collective-permute-start | bytes 2519432 | tf_op jit(solution)/shard_map/ppermute | solution.py:344
  64.9 23.5 %collective-permute-start.12 = (bf16[324,1296]{1,0:T(8,128)(2,1)S(1)}, bf16[324,1296]{1,0:T(8,128)(2,1)S(1)}, u32[]{:S(2)}, u32[]{:S(2)}) collective-permute-start(bf16[324,1296]{1,0:T(8,128)(2,1)S(1)} %collective-permute-done.7.refs_0_), channel_id=1, source_target_pairs={{0,2},{2,4},{4,6},{6,0},{1,3},{3,5},{5,7},{7,1},{8,10},{10,12},{12... | collective-permute-start | bytes 2519432 | tf_op jit(solution)/shard_map/ppermute | solution.py:314
  65.3 8.9 %collective-permute-start.16 = (bf16[336,512]{1,0:T(8,128)(2,1)S(1)}, bf16[336,512]{1,0:T(8,128)(2,1)S(1)}, u32[]{:S(2)}, u32[]{:S(2)}) collective-permute-start(bf16[336,512]{1,0:T(8,128)(2,1)S(1)} %collective-permute-done.11.refs_2_), channel_id=1, source_target_pairs={{0,8},{8,0},{16,24},{24,16},{1,9},{9,1},{17,25},{25,17},{2,10},{10... | collective-permute-start | bytes 1032200 | tf_op jit(solution)/shard_map/ppermute | solution.py:357
  66.0 8.3 %copy-start.1 = (bf16[1296,1296]{1,0:T(8,128)(2,1)S(1)}, bf16[1296,1296]{1,0:T(8,128)(2,1)}, u32[]{:S(2)}) copy-start(bf16[1296,1296]{1,0:T(8,128)(2,1)} %refs_4_.1) | copy-start | bytes 10077700
  88.4 4.1 %collective-permute-start.17 = (bf16[324,1296]{1,0:T(8,128)(2,1)S(1)}, bf16[324,1296]{1,0:T(8,128)(2,1)S(1)}, u32[]{:S(2)}, u32[]{:S(2)}) collective-permute-start(bf16[324,1296]{1,0:T(8,128)(2,1)S(1)} %collective-permute-done.12.refs_0_), channel_id=1, source_target_pairs={{0,1},{1,0},{2,3},{3,2},{4,5},{5,4},{6,7},{7,6},{8,9},{9,8},{10,11... | collective-permute-start | bytes 2519432 | tf_op jit(solution)/shard_map/ppermute | solution.py:344
  89.7 2.8 %copy-start.3 = (s32[16,128]{1,0:T(8,128)S(1)}, s32[16,128]{1,0:T(8,128)}, u32[]{:S(2)}) copy-start(s32[16,128]{1,0:T(8,128)} %ice_ref.1) | copy-start | bytes 24580
  89.7 2.8 %copy-start.4 = (bf16[16,128]{1,0:T(8,128)(2,1)S(1)}, bf16[16,128]{1,0:T(8,128)(2,1)}, u32[]{:S(2)}) copy-start(bf16[16,128]{1,0:T(8,128)(2,1)} %speed_ref.1) | copy-start | bytes 12292
  89.7 2.8 %copy-start.5 = (bf16[16,128]{1,0:T(8,128)(2,1)S(1)}, bf16[16,128]{1,0:T(8,128)(2,1)}, u32[]{:S(2)}) copy-start(bf16[16,128]{1,0:T(8,128)(2,1)} %angle_ref.1) | copy-start | bytes 12292

commit v3 on v2

--- a/solution.py
+++ b/solution.py
@@ -424,24 +424,28 @@
     parts, places = zip(*(move_rows(group, none, none) for group in groups[:2]))
     parts, places = list(parts), list(places)
     near = [meet(parts[0])]
-    near[0], sent = lax.optimization_barrier((near[0], parts[1]))
+    one_back, halos, near[0], sent = lax.optimization_barrier(
+        (one_back, halos, near[0], parts[1])
+    )
+
+    two_back = next_plane(one_back)
     near.append(meet(sent))
-    one_back, halos, near = lax.optimization_barrier((one_back, halos, near))
-
-    two_back = next_plane(one_back)
     crossed = [send_spec(near[0][1], 1), send_spec(near[1][0], 2)]
     part, place = move_rows(groups[2], *before_and_after(*halos))
     parts.append(part)
     places.append(place)
-    crossed, sent = lax.optimization_barrier((crossed, parts[2]))
+    found = with_partners(own_rows) + with_partners(one_back)
+    marks = [value[:8, :128] for value in (found[1], found[count + 1])]
+    two_back, crossed, near[1], sent, marks = lax.optimization_barrier(
+        (two_back, crossed, near[1], parts[2], marks)
+    )
     near.append(meet(sent))
-    found = with_partners(own_rows) + with_partners(one_back)
     paired, totals = pair_up(
         here_ref, [[parts[i], *near[i], crossed[i]] for i in range(2)], pair_kernel
     )
-    two_back, near[2], totals = lax.optimization_barrier((two_back, near[2], totals))
 
     three_back = next_plane(two_back)
+    near[2], totals = lax.optimization_barrier((near[2], totals))
     last_cross = send_spec(near[2][1], 1)
     held, mark = transfer_all(found, 0, strides[:2], bounds, paired, [None] * 2)
     last_cross, mark = lax.optimization_barrier((last_cross, mark))
@@ -476,7 +480,7 @@
         paired,
         held,
         parts,
-        [mark, other],
+        [mark, other, *marks],
     )
     return out.transpose(1, 0, 2)
 

time: 100 us -> 100 us (level)
  waiting for transfers between devices: 29.1 us -> 24.7 us
  starting transfers between devices: 18 us -> 21.2 us
  local copies, waits for them, and re-layouts: 6.62 us -> 8.05 us
    ppermute x3, waiting for transfers between devices: 4.82 us -> 0.46 us  [next_plane(): lax.ppermute(value, 'plane', [(i, (i + 1) % PLANES) for i in range(PLANES)])]
    ppermute x1, waiting for transfers between devices: 7.31 us -> 3.4 us  [boundaries(): lax.ppermute(jnp.where(first, top, bottom), geo, pairs + [(j, i) for i, j...]
    ppermute x9, waiting for transfers between devices: 16.9 us -> 19.3 us  [send_spec(): return lax.ppermute(value, 'spec', [(i, i ^ flip) for i in range(4)])]
    ppermute x1, starting transfers between devices: 2.36 us -> 0.01 us  [boundaries(): lax.ppermute(jnp.where(first, bottom, top), 'place', [(0, 1), (1, 0)])]
    ppermute x4, starting transfers between devices: 3.37 us -> 5.59 us  [with_partners(): found.append(lax.ppermute(kernel, 'place', pairs))]
    ppermute x9, starting transfers between devices: 7.23 us -> 9.34 us  [send_spec(): return lax.ppermute(value, 'spec', [(i, i ^ flip) for i in range(4)])]
    ppermute x1, waiting for transfers between devices: 0.01 us -> 1.54 us  [boundaries(): lax.ppermute(jnp.where(first, bottom, top), 'place', [(0, 1), (1, 0)])]
    pallas_call x3, Pallas kernels: 14.4 us -> 15.8 us  [transfer(): pl.pallas_call(functools.partial(transfer_body, uses, strides, kept), out...]
  transfers between devices with their start and end apart: 18 -> 18, of which waited for: 6 -> 7; matrix products, arithmetic and copies ran while one was open for 3% -> 4% of each run, Pallas kernels for 34% -> 38%
where the time goes in v3:
time: 100 us; the launch traced here: 99.8 us
  Pallas kernels  43.3 us (43%)
  waiting for transfers between devices  24.7 us (25%)
  starting transfers between devices  21.2 us (21%)
  local copies, waits for them, and re-layouts  8.05 us (8%)
  other arithmetic  2.23 us (2%)
    ppermute x9, waiting for transfers between devices, send_spec(): return lax.ppermute(value, 'spec', [(i, i ^ flip) for i in range(4)])  19.3 us
    pallas_call x3, Pallas kernels, transfer(): pl.pallas_call(functools.partial(transfer_body, uses, strides, kept), out...  15.8 us
    pallas_call x2, Pallas kernels, pair_up(): pl.pallas_call(functools.partial(pair_body, tile, sizes), grid=(comps //...  12.1 us
    pallas_call x3, Pallas kernels, propagate(): pl.pallas_call(functools.partial(propagate_kernel, wanted, count), out_sh...  9.63 us
    ppermute x9, starting transfers between devices, send_spec(): return lax.ppermute(value, 'spec', [(i, i ^ flip) for i in range(4)])  9.34 us
    pallas_call x1, Pallas kernels, finish(): pl.pallas_call(functools.partial(finish_body, len(kernels), first, groups...  5.73 us
    ppermute x4, starting transfers between devices, with_partners(): found.append(lax.ppermute(kernel, 'place', pairs))  5.59 us
    unnamed x28, local copies, waits for them, and re-layouts  5.2 us
  transfers between devices with their start and end apart: 18, of which 7 were waited for; matrix products, arithmetic and copies ran while one was open for 4% of the time, Pallas kernels for 38%

profile of v3, /device:TPU:1, one launch (start us, length us, event | category | flops | bytes accessed | tf_op | source)
XLA Modules:
  0.0 99.8 jit_solution(13309403176496451993)
XLA Ops:
  0.0 1.4 %dynamic-slice_bitcast_fusion.refs_0_.refs_2_ = bf16[324,1296]{1,0:T(8,128)(2,1)S(1)} fusion(bf16[1,1296,1296]{2,1,0:T(8,128)(2,1)} %param.17, s32[]{:T(128)S(6)} %select_n.81), kind=kLoop, calls=%fused_computation | loop fusion | bytes 1679620 | tf_op jit(solution)/shard_map/dynamic_slice | solution.py:374
  1.4 2.2 %collective-permute-start = (bf16[324,1296]{1,0:T(8,128)(2,1)S(1)}, bf16[324,1296]{1,0:T(8,128)(2,1)}, u32[]{:S(2)}, u32[]{:S(2)}) collective-permute-start(bf16[324,1296]{1,0:T(8,128)(2,1)S(1)} %dynamic-slice_bitcast_fusion.refs_0_.refs_2_), channel_id=1, source_target_pairs={{0,2},{2,4},{4,6},{6,0},{1,3},{3,5},{5,7},{7,1},{8,10},{10,12},{12... | collective-permute-start | bytes 2519432 | tf_op jit(solution)/shard_map/ppermute | solution.py:314
  3.6 0.1 compare_convert_fusion
  3.7 0.1 abs_multiply_fusion
  3.7 0.1 fusion.13
  3.9 0.1 copy.28.coef_ref
  4.0 0.0 copy-start.9
  4.0 0.0 copy-start.10
  4.0 0.0 copy-start.4
  4.0 1.7 %copy.32 = bf16[324,16,128]{2,0,1:T(8,128)(2,1)S(1)} copy(bf16[324,16,128]{2,1,0:T(8,128)(2,1)} %param.9) | data formatting | bytes 2654208 | tf_op args[0]
  5.8 3.9 %shard_map.91 = (bf16[336,768]{1,0:T(8,128)(2,1)}, f32[1,768]{1,0:T(1,128)S(1)}) custom-call(bf16[16,324,128]{2,1,0:T(8,128)(2,1)S(1)} %bitcast.83, bf16[324,128]{1,0:T(8,128)(2,1)S(1)} %broadcast_in_dim.2.west_ref.east_ref, bf16[324,128]{1,0:T(8,128)(2,1)S(1)} %broadcast_in_dim.2.west_ref.east_ref, f32[16,128]{1,0:T(8,128)S(1)} %get-tuple-element.99.sea_ref, ...), custom_call_target="tpu_custom_call" | custom-call | flops 497664 | bytes 248832 | tf_op jit(solution)/shard_map/pallas_call | solution.py:126
  9.7 1.2 %collective-permute-start.3 = (bf16[336,768]{1,0:T(8,128)(2,1)}, bf16[336,768]{1,0:T(8,128)(2,1)}, u32[]{:S(2)}, u32[]{:S(2)}) collective-permute-start(bf16[336,768]{1,0:T(8,128)(2,1)} %get-tuple-element.49.refs_0_.refs_13_), channel_id=1, source_target_pairs={{0,8},{8,0},{16,24},{24,16},{1,9},{9,1},{17,25},{25,17},{2,10},{10... | collective-permute-start | bytes 1548296 | tf_op jit(solution)/shard_map/ppermute | solution.py:357
  11.0 1.2 %collective-permute-start.4 = (bf16[336,768]{1,0:T(8,128)(2,1)}, bf16[336,768]{1,0:T(8,128)(2,1)}, u32[]{:S(2)}, u32[]{:S(2)}) collective-permute-start(bf16[336,768]{1,0:T(8,128)(2,1)} %get-tuple-element.49.refs_0_.refs_13_), channel_id=1, source_target_pairs={{0,16},{8,24},{16,0},{24,8},{1,17},{9,25},{17,1},{25,9},{2,18},{10... | collective-permute-start | bytes 1548296 | tf_op jit(solution)/shard_map/ppermute | solution.py:357
  12.2 1.5 %collective-permute-start.10 = (bf16[324,1296]{1,0:T(8,128)(2,1)S(1)}, bf16[324,1296]{1,0:T(8,128)(2,1)S(1)}, u32[]{:S(2)}, u32[]{:S(2)}) collective-permute-start(bf16[324,1296]{1,0:T(8,128)(2,1)S(1)} %dynamic-slice_bitcast_fusion.refs_0_.refs_2_), channel_id=1, source_target_pairs={{0,1},{1,0},{2,3},{3,2},{4,5},{5,4},{6,7},{7,6},{8,9},{9,8},{10,11... | collective-permute-start | bytes 2519432 | tf_op jit(solution)/shard_map/ppermute | solution.py:344
  13.7 0.7 broadcast_select_fusion.2
  14.4 0.0 collective-permute-start.1
  14.4 1.5 %collective-permute-done.1 = bf16[324,128]{1,0:T(8,128)(2,1)S(1)} collective-permute-done((bf16[324,128]{1,0:T(8,128)(2,1)S(1)}, bf16[324,128]{1,0:T(8,128)(2,1)S(1)}, u32[]{:S(2)}, u32[]{:S(2)}) %collective-permute-start.1) | collective-permute-done | bytes 82976 | tf_op jit(solution)/shard_map/ppermute | solution.py:326
  15.9 0.6 copy-done.8
  16.6 3.4 %collective-permute-start.2 = (bf16[324,128]{1,0:T(8,128)(2,1)}, bf16[324,128]{1,0:T(8,128)(2,1)}, u32[]{:S(2)}, u32[]{:S(2)}) collective-permute-start(bf16[324,128]{1,0:T(8,128)(2,1)} %get-tuple-element.93), channel_id=1, source_target_pairs={{1,2},{3,4},{5,6},{2,1},{4,3},{6,5},{9,10},{11,12},{13,14},{10,9},... | collective-permute-start | bytes 248840 | tf_op jit(solution)/shard_map/ppermute | solution.py:328
  20.0 3.1 %shard_map.92 = (bf16[336,768]{1,0:T(8,128)(2,1)S(1)}, f32[1,768]{1,0:T(1,128)S(1)}) custom-call(bf16[16,324,128]{2,1,0:T(8,128)(2,1)S(1)} %bitcast.84, bf16[324,128]{1,0:T(8,128)(2,1)S(1)} %broadcast_in_dim.2.west_ref.east_ref, bf16[324,128]{1,0:T(8,128)(2,1)S(1)} %broadcast_in_dim.2.west_ref.east_ref, f32[16,128]{1,0:T(8,128)S(1)} %get-tuple-element.99.sea_ref, ...), custom_call_target="tpu_custom_call" | custom-call | flops 497664 | bytes 248832 | tf_op jit(solution)/shard_map/pallas_call | solution.py:126
  23.2 0.8 copy-done.2
  24.0 3.4 %collective-permute-done.2 = bf16[324,128]{1,0:T(8,128)(2,1)} collective-permute-done((bf16[324,128]{1,0:T(8,128)(2,1)}, bf16[324,128]{1,0:T(8,128)(2,1)}, u32[]{:S(2)}, u32[]{:S(2)}) %collective-permute-start.2) | collective-permute-done | bytes 82976 | tf_op jit(solution)/shard_map/ppermute | solution.py:328
  27.4 0.0 collective-permute-done.3.refs_1_
  27.4 0.0 collective-permute-done.4.refs_2_
  27.4 0.0 collective-permute-done.refs_2_.refs_4_
  27.4 1.3 %collective-permute-start.7 = (bf16[336,768]{1,0:T(8,128)(2,1)}, bf16[336,768]{1,0:T(8,128)(2,1)S(1)}, u32[]{:S(2)}, u32[]{:S(2)}) collective-permute-start(bf16[336,768]{1,0:T(8,128)(2,1)} %copy-done.2), channel_id=1, source_target_pairs={{0,8},{8,0},{16,24},{24,16},{1,9},{9,1},{17,25},{25,17},{2,10},{10... | collective-permute-start | bytes 1548296 | tf_op jit(solution)/shard_map/ppermute | solution.py:357
  28.7 0.2 collective-permute-start.11
  28.9 0.2 collective-permute-start.5
  29.1 1.2 %collective-permute-start.9 = (bf16[336,768]{1,0:T(8,128)(2,1)}, bf16[336,768]{1,0:T(8,128)(2,1)S(1)}, u32[]{:S(2)}, u32[]{:S(2)}) collective-permute-start(bf16[336,768]{1,0:T(8,128)(2,1)} %copy-done.2), channel_id=1, source_target_pairs={{0,16},{8,24},{16,0},{24,8},{1,17},{9,25},{17,1},{25,9},{2,18},{10... | collective-permute-start | bytes 1548296 | tf_op jit(solution)/shard_map/ppermute | solution.py:357
  30.3 0.0 collective-permute-done.10.refs_1_.refs_3_
  30.3 0.3 collective-permute-start.6
  30.6 10.5 %collective-permute-done.7.refs_5_ = bf16[336,768]{1,0:T(8,128)(2,1)S(1)} collective-permute-done((bf16[336,768]{1,0:T(8,128)(2,1)}, bf16[336,768]{1,0:T(8,128)(2,1)S(1)}, u32[]{:S(2)}, u32[]{:S(2)}) %collective-permute-start.7) | collective-permute-done | bytes 516128 | tf_op jit(solution)/shard_map/ppermute | solution.py:357
  41.1 1.2 %collective-permute-start.8 = (bf16[336,768]{1,0:T(8,128)(2,1)S(1)}, bf16[336,768]{1,0:T(8,128)(2,1)S(1)}, u32[]{:S(2)}, u32[]{:S(2)}) collective-permute-start(bf16[336,768]{1,0:T(8,128)(2,1)S(1)} %collective-permute-done.7.refs_5_), channel_id=1, source_target_pairs={{0,16},{8,24},{16,0},{24,8},{1,17},{9,25},{17,1},{25,9},{2,18},{10... | collective-permute-start | bytes 1548296 | tf_op jit(solution)/shard_map/ppermute | solution.py:357
  42.3 1.0 broadcast_select_fusion
  43.3 2.6 %shard_map.93 = (bf16[336,512]{1,0:T(8,128)(2,1)S(1)}, f32[1,512]{1,0:T(1,128)S(1)}) custom-call(bf16[16,324,128]{2,1,0:T(8,128)(2,1)S(1)} %bitcast.85, bf16[324,128]{1,0:T(8,128)(2,1)S(1)} %get-tuple-element.98.west_ref, bf16[324,128]{1,0:T(8,128)(2,1)S(1)} %get-tuple-element.97.east_ref, f32[16,128]{1,0:T(8,128)S(1)} %get-tuple-element.99.sea_ref, ...), custom_call_target="tpu_custom_call" | custom-call | flops 331776 | bytes 165888 | tf_op jit(solution)/shard_map/pallas_call | solution.py:126
  45.9 0.0 collective-permute-done.11.refs_3_.refs_5_
  45.9 6.2 %collective-permute-done.6.refs_3_ = bf16[336,768]{1,0:T(8,128)(2,1)S(1)} collective-permute-done((bf16[336,768]{1,0:T(8,128)(2,1)}, bf16[336,768]{1,0:T(8,128)(2,1)S(1)}, u32[]{:S(2)}, u32[]{:S(2)}) %collective-permute-start.6) | collective-permute-done | bytes 516128 | tf_op jit(solution)/shard_map/ppermute | solution.py:357
  52.1 0.0 collective-permute-done.9.refs_6_
  52.2 0.5 collective-permute-done.5.refs_0_
  52.6 0.7 collective-permute-done.8.refs_7_
  53.3 2.0 %collective-permute-start.13 = (bf16[324,1296]{1,0:T(8,128)(2,1)S(1)}, bf16[324,1296]{1,0:T(8,128)(2,1)S(1)}, u32[]{:S(2)}, u32[]{:S(2)}) collective-permute-start(bf16[324,1296]{1,0:T(8,128)(2,1)S(1)} %collective-permute-done.5.refs_0_), channel_id=1, source_target_pairs={{0,1},{1,0},{2,3},{3,2},{4,5},{5,4},{6,7},{7,6},{8,9},{9,8},{10,11... | collective-permute-start | bytes 2519432 | tf_op jit(solution)/shard_map/ppermute | solution.py:344
  55.3 1.2 %collective-permute-start.14 = (bf16[336,512]{1,0:T(8,128)(2,1)S(1)}, bf16[336,512]{1,0:T(8,128)(2,1)S(1)}, u32[]{:S(2)}, u32[]{:S(2)}) collective-permute-start(bf16[336,512]{1,0:T(8,128)(2,1)S(1)} %get-tuple-element.65.refs_0_.refs_15_), channel_id=1, source_target_pairs={{0,8},{8,0},{16,24},{24,16},{1,9},{9,1},{17,25},{25,17},{2,10},{10... | collective-permute-start | bytes 1032200 | tf_op jit(solution)/shard_map/ppermute | solution.py:357
  56.5 1.2 %collective-permute-start.15 = (bf16[336,512]{1,0:T(8,128)(2,1)S(1)}, bf16[336,512]{1,0:T(8,128)(2,1)S(1)}, u32[]{:S(2)}, u32[]{:S(2)}) collective-permute-start(bf16[336,512]{1,0:T(8,128)(2,1)S(1)} %get-tuple-element.65.refs_0_.refs_15_), channel_id=1, source_target_pairs={{0,16},{8,24},{16,0},{24,8},{1,17},{9,25},{17,1},{25,9},{2,18},{10... | collective-permute-start | bytes 1032200 | tf_op jit(solution)/shard_map/ppermute | solution.py:357
  57.7 0.4 collective-permute-start.12
  58.1 0.0 copy-start
  58.1 2.0 %copy-done = bf16[1296,1296]{1,0:T(8,128)(2,1)S(1)} copy-done((bf16[1296,1296]{1,0:T(8,128)(2,1)S(1)}, bf16[1296,1296]{1,0:T(8,128)(2,1)}, u32[]{:S(2)}) %copy-start) | copy-done | bytes 3359256
  60.2 9.3 %shard_map.94 = (bf16[1296,768]{1,0:T(8,128)(2,1)S(1)}, bf16[1296,768]{1,0:T(8,128)(2,1)S(1)}, f32[1,768]{1,0:T(1,128)S(1)}, f32[1,768]{1,0:T(1,128)S(1)}) custom-call(s32[1]{0:T(128)} %bitcast.22.here_ref, bf16[336,768]{1,0:T(8,128)(2,1)} %get-tuple-element.49.refs_0_.refs_13_, bf16[336,768]{1,0:T(8,128)(2,1)} %collective-permute-done.3.refs_1_, ...), custom_call_target="tpu_custom_call" | custom-call | flops 644972544 | bytes 419904 | tf_op jit(solution)/shard_map/pallas_call | solution.py:185
  69.4 0.0 collective-permute-done.14.refs_1_
  69.4 0.0 collective-permute-done.15.refs_2_
  69.4 0.5 collective-permute-start.16
  69.9 0.1 convert_reduce_fusion.2
  70.0 0.1 convert_reduce_fusion
  70.1 0.1 pad_add_fusion.1.bounds_ref
  70.2 6.0 %shard_map.95 = (bf16[324,768]{1,0:T(8,128)(2,1)S(1)}, bf16[324,768]{1,0:T(8,128)(2,1)S(1)}, f32[8,128]{1,0:T(8,128)S(1)}) custom-call(s32[27]{0:T(128)S(1)} %pad_add_fusion.1.bounds_ref, bf16[324,1296]{1,0:T(8,128)(2,1)S(1)} %dynamic-slice_bitcast_fusion.refs_0_.refs_2_, bf16[324,1296]{1,0:T(8,128)(2,1)S(1)} %collective-permute-done.10.refs_1_.refs_3_, ...), custom_call_target="tpu_custom_call" | custom-call | flops 322486272 | bytes 917568 | tf_op jit(solution)/shard_map/pallas_call | solution.py:242
  76.2 1.9 %collective-permute-done.16.refs_3_ = bf16[336,512]{1,0:T(8,128)(2,1)S(1)} collective-permute-done((bf16[336,512]{1,0:T(8,128)(2,1)S(1)}, bf16[336,512]{1,0:T(8,128)(2,1)S(1)}, u32[]{:S(2)}, u32[]{:S(2)}) %collective-permute-start.16) | collective-permute-done | bytes 344096 | tf_op jit(solution)/shard_map/ppermute | solution.py:357
  78.2 2.9 %shard_map.96 = (bf16[1296,512]{1,0:T(8,128)(2,1)S(1)}, f32[1,512]{1,0:T(1,128)S(1)}) custom-call(s32[1]{0:T(128)} %bitcast.22.here_ref, bf16[336,512]{1,0:T(8,128)(2,1)S(1)} %get-tuple-element.65.refs_0_.refs_15_, bf16[336,512]{1,0:T(8,128)(2,1)S(1)} %collective-permute-done.14.refs_1_, bf16[336,512]{1,0:T(8,128)(2,1)S(1)} %collective-permute-done.15.refs_2_, ...), custom_call_target="tpu_custom_call" | custom-call | flops 214990848 | bytes 419904 | tf_op jit(solution)/shard_map/pallas_call | solution.py:185
  81.1 0.0 collective-permute-done.13.refs_1_
  81.1 7.0 %shard_map.97 = (bf16[324,768]{1,0:T(8,128)(2,1)S(1)}, bf16[324,768]{1,0:T(8,128)(2,1)S(1)}, bf16[324,512]{1,0:T(8,128)(2,1)S(1)}, f32[8,128]{1,0:T(8,128)S(1)}) custom-call(s32[27]{0:T(128)S(1)} %pad_add_fusion.1.bounds_ref, bf16[324,1296]{1,0:T(8,128)(2,1)S(1)} %collective-permute-done.5.refs_0_, bf16[324,1296]{1,0:T(8,128)(2,1)S(1)} %collective-permute-done.13.refs_1_, ...), custom_call_target="tpu_custom_call" | custom-call | flops 644972544 | bytes 1293408 | tf_op jit(solution)/shard_map/pallas_call | solution.py:242
  88.1 0.0 collective-permute-done.12.refs_0_
  88.1 1.9 %collective-permute-start.17 = (bf16[324,1296]{1,0:T(8,128)(2,1)S(1)}, bf16[324,1296]{1,0:T(8,128)(2,1)S(1)}, u32[]{:S(2)}, u32[]{:S(2)}) collective-permute-start(bf16[324,1296]{1,0:T(8,128)(2,1)S(1)} %collective-permute-done.12.refs_0_), channel_id=1, source_target_pairs={{0,1},{1,0},{2,3},{3,2},{4,5},{5,4},{6,7},{7,6},{8,9},{9,8},{10,11... | collective-permute-start | bytes 2519432 | tf_op jit(solution)/shard_map/ppermute | solution.py:344
  90.0 2.8 %shard_map.98 = (bf16[324,768]{1,0:T(8,128)(2,1)S(1)}, bf16[324,768]{1,0:T(8,128)(2,1)S(1)}, bf16[324,512]{1,0:T(8,128)(2,1)S(1)}, f32[8,128]{1,0:T(8,128)}) custom-call(s32[27]{0:T(128)S(1)} %pad_add_fusion.1.bounds_ref, bf16[324,1296]{1,0:T(8,128)(2,1)S(1)} %collective-permute-done.12.refs_0_, ...), custom_call_target="tpu_custom_call" | custom-call | flops 107495424 | bytes 768528 | tf_op jit(solution)/shard_map/pallas_call | solution.py:242
  92.8 0.0 collective-permute-done.17.refs_0_
  92.8 5.7 %shard_map.99 = bf16[16,324,128]{2,1,0:T(8,128)(2,1)S(1)} custom-call(s32[27]{0:T(128)S(1)} %pad_add_fusion.1.bounds_ref, f32[324,6]{1,0:T(8,128)S(1)} %copy.28.coef_ref, s32[16,128]{1,0:T(8,128)S(1)} %copy-done.5, bf16[16,128]{1,0:T(8,128)(2,1)S(1)} %copy-done.6, bf16[16,128]{1,0:T(8,128)(2,1)S(1)} %copy-done.7, ...), custom_call_target="tpu_custom_call" | custom-call | flops 107495424 | bytes 768528 | tf_op jit(solution)/shard_map/pallas_call | solution.py:302
  98.5 1.2 %copy.29 = bf16[324,16,128]{2,1,0:T(8,128)(2,1)} copy(bf16[324,16,128]{2,0,1:T(8,128)(2,1)S(1)} %bitcast.86) | data formatting | bytes 2654208 | tf_op jit(solution)/shard_map/transpose | solution.py:485
  (32 shorter events, 0.2 us)
Async XLA Ops:
  1.4 26.0 %collective-permute-start = (bf16[324,1296]{1,0:T(8,128)(2,1)S(1)}, bf16[324,1296]{1,0:T(8,128)(2,1)}, u32[]{:S(2)}, u32[]{:S(2)}) collective-permute-start(bf16[324,1296]{1,0:T(8,128)(2,1)S(1)} %dynamic-slice_bitcast_fusion.refs_0_.refs_2_), channel_id=1, source_target_pairs={{0,2},{2,4},{4,6},{6,0},{1,3},{3,5},{5,7},{7,1},{8,10},{10,12},{12... | collective-permute-start | bytes 2519432 | tf_op jit(solution)/shard_map/ppermute | solution.py:314
  4.0 1.7 %copy-start.9 = (s32[16,128]{1,0:T(8,128)S(1)}, s32[16,128]{1,0:T(8,128)}, u32[]{:S(2)}) copy-start(s32[16,128]{1,0:T(8,128)} %param.10) | copy-start | bytes 24580
  4.0 1.7 %copy-start.10 = (s32[16,128]{1,0:T(8,128)S(1)}, s32[16,128]{1,0:T(8,128)}, u32[]{:S(2)}) copy-start(s32[16,128]{1,0:T(8,128)} %param.15) | copy-start | bytes 24580
  4.0 1.8 %copy-start.4 = (f32[16,128]{1,0:T(8,128)S(1)}, f32[16,128]{1,0:T(8,128)}, u32[]{:S(2)}) copy-start(f32[16,128]{1,0:T(8,128)} %depth_ref.5) | copy-start | bytes 24580
  9.7 17.6 %collective-permute-start.3 = (bf16[336,768]{1,0:T(8,128)(2,1)}, bf16[336,768]{1,0:T(8,128)(2,1)}, u32[]{:S(2)}, u32[]{:S(2)}) collective-permute-start(bf16[336,768]{1,0:T(8,128)(2,1)} %get-tuple-element.49.refs_0_.refs_13_), channel_id=1, source_target_pairs={{0,8},{8,0},{16,24},{24,16},{1,9},{9,1},{17,25},{25,17},{2,10},{10... | collective-permute-start | bytes 1548296 | tf_op jit(solution)/shard_map/ppermute | solution.py:357
  11.0 16.4 %collective-permute-start.4 = (bf16[336,768]{1,0:T(8,128)(2,1)}, bf16[336,768]{1,0:T(8,128)(2,1)}, u32[]{:S(2)}, u32[]{:S(2)}) collective-permute-start(bf16[336,768]{1,0:T(8,128)(2,1)} %get-tuple-element.49.refs_0_.refs_13_), channel_id=1, source_target_pairs={{0,16},{8,24},{16,0},{24,8},{1,17},{9,25},{17,1},{25,9},{2,18},{10... | collective-permute-start | bytes 1548296 | tf_op jit(solution)/shard_map/ppermute | solution.py:357
  12.2 18.1 %collective-permute-start.10 = (bf16[324,1296]{1,0:T(8,128)(2,1)S(1)}, bf16[324,1296]{1,0:T(8,128)(2,1)S(1)}, u32[]{:S(2)}, u32[]{:S(2)}) collective-permute-start(bf16[324,1296]{1,0:T(8,128)(2,1)S(1)} %dynamic-slice_bitcast_fusion.refs_0_.refs_2_), channel_id=1, source_target_pairs={{0,1},{1,0},{2,3},{3,2},{4,5},{5,4},{6,7},{7,6},{8,9},{9,8},{10,11... | collective-permute-start | bytes 2519432 | tf_op jit(solution)/shard_map/ppermute | solution.py:344
  14.4 1.5 %collective-permute-start.1 = (bf16[324,128]{1,0:T(8,128)(2,1)S(1)}, bf16[324,128]{1,0:T(8,128)(2,1)S(1)}, u32[]{:S(2)}, u32[]{:S(2)}) collective-permute-start(bf16[324,128]{1,0:T(8,128)(2,1)S(1)} %get-tuple-element.94), channel_id=1, source_target_pairs={{0,1},{1,0},{2,3},{3,2},{4,5},{5,4},{6,7},{7,6},{8,9},{9,8},{10,11... | collective-permute-start | bytes 248840 | tf_op jit(solution)/shard_map/ppermute | solution.py:326
  15.9 0.6 copy-start.8
  16.6 10.8 %collective-permute-start.2 = (bf16[324,128]{1,0:T(8,128)(2,1)}, bf16[324,128]{1,0:T(8,128)(2,1)}, u32[]{:S(2)}, u32[]{:S(2)}) collective-permute-start(bf16[324,128]{1,0:T(8,128)(2,1)} %get-tuple-element.93), channel_id=1, source_target_pairs={{1,2},{3,4},{5,6},{2,1},{4,3},{6,5},{9,10},{11,12},{13,14},{10,9},... | collective-permute-start | bytes 248840 | tf_op jit(solution)/shard_map/ppermute | solution.py:328
  23.2 0.8 copy-start.2
  24.0 34.1 %copy-start.3 = (bf16[336,768]{1,0:T(8,128)(2,1)S(1)}, bf16[336,768]{1,0:T(8,128)(2,1)}, u32[]{:S(2)}) copy-start(bf16[336,768]{1,0:T(8,128)(2,1)} %copy-done.2) | copy-start | bytes 1548292
  27.4 13.7 %collective-permute-start.7 = (bf16[336,768]{1,0:T(8,128)(2,1)}, bf16[336,768]{1,0:T(8,128)(2,1)S(1)}, u32[]{:S(2)}, u32[]{:S(2)}) collective-permute-start(bf16[336,768]{1,0:T(8,128)(2,1)} %copy-done.2), channel_id=1, source_target_pairs={{0,8},{8,0},{16,24},{24,16},{1,9},{9,1},{17,25},{25,17},{2,10},{10... | collective-permute-start | bytes 1548296 | tf_op jit(solution)/shard_map/ppermute | solution.py:357
  28.7 17.2 %collective-permute-start.11 = (bf16[324,1296]{1,0:T(8,128)(2,1)}, bf16[324,1296]{1,0:T(8,128)(2,1)S(1)}, u32[]{:S(2)}, u32[]{:S(2)}) collective-permute-start(bf16[324,1296]{1,0:T(8,128)(2,1)} %collective-permute-done.refs_2_.refs_4_), channel_id=1, source_target_pairs={{0,1},{1,0},{2,3},{3,2},{4,5},{5,4},{6,7},{7,6},{8,9},{9,8},{10,11... | collective-permute-start | bytes 2519432 | tf_op jit(solution)/shard_map/ppermute | solution.py:344
  28.9 23.7 %collective-permute-start.5 = (bf16[324,1296]{1,0:T(8,128)(2,1)}, bf16[324,1296]{1,0:T(8,128)(2,1)S(1)}, u32[]{:S(2)}, u32[]{:S(2)}) collective-permute-start(bf16[324,1296]{1,0:T(8,128)(2,1)} %collective-permute-done.refs_2_.refs_4_), channel_id=1, source_target_pairs={{0,2},{2,4},{4,6},{6,0},{1,3},{3,5},{5,7},{7,1},{8,10},{10,12},{12... | collective-permute-start | bytes 2519432 | tf_op jit(solution)/shard_map/ppermute | solution.py:314
  29.1 23.1 %collective-permute-start.9 = (bf16[336,768]{1,0:T(8,128)(2,1)}, bf16[336,768]{1,0:T(8,128)(2,1)S(1)}, u32[]{:S(2)}, u32[]{:S(2)}) collective-permute-start(bf16[336,768]{1,0:T(8,128)(2,1)} %copy-done.2), channel_id=1, source_target_pairs={{0,16},{8,24},{16,0},{24,8},{1,17},{9,25},{17,1},{25,9},{2,18},{10... | collective-permute-start | bytes 1548296 | tf_op jit(solution)/shard_map/ppermute | solution.py:357
  30.3 21.8 %collective-permute-start.6 = (bf16[336,768]{1,0:T(8,128)(2,1)}, bf16[336,768]{1,0:T(8,128)(2,1)S(1)}, u32[]{:S(2)}, u32[]{:S(2)}) collective-permute-start(bf16[336,768]{1,0:T(8,128)(2,1)} %collective-permute-done.4.refs_2_), channel_id=1, source_target_pairs={{0,8},{8,0},{16,24},{24,16},{1,9},{9,1},{17,25},{25,17},{2,10},{10... | collective-permute-start | bytes 1548296 | tf_op jit(solution)/shard_map/ppermute | solution.py:357
  41.1 12.2 %collective-permute-start.8 = (bf16[336,768]{1,0:T(8,128)(2,1)S(1)}, bf16[336,768]{1,0:T(8,128)(2,1)S(1)}, u32[]{:S(2)}, u32[]{:S(2)}) collective-permute-start(bf16[336,768]{1,0:T(8,128)(2,1)S(1)} %collective-permute-done.7.refs_5_), channel_id=1, source_target_pairs={{0,16},{8,24},{16,0},{24,8},{1,17},{9,25},{17,1},{25,9},{2,18},{10... | collective-permute-start | bytes 1548296 | tf_op jit(solution)/shard_map/ppermute | solution.py:357
  53.3 27.8 %collective-permute-start.13 = (bf16[324,1296]{1,0:T(8,128)(2,1)S(1)}, bf16[324,1296]{1,0:T(8,128)(2,1)S(1)}, u32[]{:S(2)}, u32[]{:S(2)}) collective-permute-start(bf16[324,1296]{1,0:T(8,128)(2,1)S(1)} %collective-permute-done.5.refs_0_), channel_id=1, source_target_pairs={{0,1},{1,0},{2,3},{3,2},{4,5},{5,4},{6,7},{7,6},{8,9},{9,8},{10,11... | collective-permute-start | bytes 2519432 | tf_op jit(solution)/shard_map/ppermute | solution.py:344
  55.3 14.2 %collective-permute-start.14 = (bf16[336,512]{1,0:T(8,128)(2,1)S(1)}, bf16[336,512]{1,0:T(8,128)(2,1)S(1)}, u32[]{:S(2)}, u32[]{:S(2)}) collective-permute-start(bf16[336,512]{1,0:T(8,128)(2,1)S(1)} %get-tuple-element.65.refs_0_.refs_15_), channel_id=1, source_target_pairs={{0,8},{8,0},{16,24},{24,16},{1,9},{9,1},{17,25},{25,17},{2,10},{10... | collective-permute-start | bytes 1032200 | tf_op jit(solution)/shard_map/ppermute | solution.py:357
  56.5 13.0 %collective-permute-start.15 = (bf16[336,512]{1,0:T(8,128)(2,1)S(1)}, bf16[336,512]{1,0:T(8,128)(2,1)S(1)}, u32[]{:S(2)}, u32[]{:S(2)}) collective-permute-start(bf16[336,512]{1,0:T(8,128)(2,1)S(1)} %get-tuple-element.65.refs_0_.refs_15_), channel_id=1, source_target_pairs={{0,16},{8,24},{16,0},{24,8},{1,17},{9,25},{17,1},{25,9},{2,18},{10... | collective-permute-start | bytes 1032200 | tf_op jit(solution)/shard_map/ppermute | solution.py:357
  57.7 30.4 %collective-permute-start.12 = (bf16[324,1296]{1,0:T(8,128)(2,1)S(1)}, bf16[324,1296]{1,0:T(8,128)(2,1)S(1)}, u32[]{:S(2)}, u32[]{:S(2)}) collective-permute-start(bf16[324,1296]{1,0:T(8,128)(2,1)S(1)} %collective-permute-done.5.refs_0_), channel_id=1, source_target_pairs={{0,2},{2,4},{4,6},{6,0},{1,3},{3,5},{5,7},{7,1},{8,10},{10,12},{12... | collective-permute-start | bytes 2519432 | tf_op jit(solution)/shard_map/ppermute | solution.py:314
  58.1 2.0 %copy-start = (bf16[1296,1296]{1,0:T(8,128)(2,1)S(1)}, bf16[1296,1296]{1,0:T(8,128)(2,1)}, u32[]{:S(2)}) copy-start(bf16[1296,1296]{1,0:T(8,128)(2,1)} %refs_4_.1) | copy-start | bytes 10077700
  69.4 8.7 %collective-permute-start.16 = (bf16[336,512]{1,0:T(8,128)(2,1)S(1)}, bf16[336,512]{1,0:T(8,128)(2,1)S(1)}, u32[]{:S(2)}, u32[]{:S(2)}) collective-permute-start(bf16[336,512]{1,0:T(8,128)(2,1)S(1)} %collective-permute-done.15.refs_2_), channel_id=1, source_target_pairs={{0,8},{8,0},{16,24},{24,16},{1,9},{9,1},{17,25},{25,17},{2,10},{10... | collective-permute-start | bytes 1032200 | tf_op jit(solution)/shard_map/ppermute | solution.py:357
  70.2 8.0 %copy-start.1 = (bf16[1296,1296]{1,0:T(8,128)(2,1)S(1)}, bf16[1296,1296]{1,0:T(8,128)(2,1)}, u32[]{:S(2)}) copy-start(bf16[1296,1296]{1,0:T(8,128)(2,1)} %refs_4_.1) | copy-start | bytes 10077700
  88.1 4.7 %collective-permute-start.17 = (bf16[324,1296]{1,0:T(8,128)(2,1)S(1)}, bf16[324,1296]{1,0:T(8,128)(2,1)S(1)}, u32[]{:S(2)}, u32[]{:S(2)}) collective-permute-start(bf16[324,1296]{1,0:T(8,128)(2,1)S(1)} %collective-permute-done.12.refs_0_), channel_id=1, source_target_pairs={{0,1},{1,0},{2,3},{3,2},{4,5},{5,4},{6,7},{7,6},{8,9},{9,8},{10,11... | collective-permute-start | bytes 2519432 | tf_op jit(solution)/shard_map/ppermute | solution.py:344
  90.0 2.8 %copy-start.5 = (s32[16,128]{1,0:T(8,128)S(1)}, s32[16,128]{1,0:T(8,128)}, u32[]{:S(2)}) copy-start(s32[16,128]{1,0:T(8,128)} %ice_ref.1) | copy-start | bytes 24580
  90.0 2.8 %copy-start.6 = (bf16[16,128]{1,0:T(8,128)(2,1)S(1)}, bf16[16,128]{1,0:T(8,128)(2,1)}, u32[]{:S(2)}) copy-start(bf16[16,128]{1,0:T(8,128)(2,1)} %speed_ref.1) | copy-start | bytes 12292
  90.0 2.8 %copy-start.7 = (bf16[16,128]{1,0:T(8,128)(2,1)S(1)}, bf16[16,128]{1,0:T(8,128)(2,1)}, u32[]{:S(2)}) copy-start(bf16[16,128]{1,0:T(8,128)(2,1)} %angle_ref.1) | copy-start | bytes 12292

commit v4 on v3

--- a/solution.py
+++ b/solution.py
@@ -440,36 +440,35 @@
         (two_back, crossed, near[1], parts[2], marks)
     )
     near.append(meet(sent))
-    paired, totals = pair_up(
-        here_ref, [[parts[i], *near[i], crossed[i]] for i in range(2)], pair_kernel
-    )
-
     three_back = next_plane(two_back)
-    near[2], totals = lax.optimization_barrier((near[2], totals))
+    later = with_partners(two_back)
+    paired, totals = [], []
+
+    def pair_group(i, far):
+        more, total = pair_up(here_ref, [[parts[i], *near[i], far]], pair_kernel)
+        paired.extend(more)
+        return total[0]
+
+    totals.append(pair_group(0, crossed[0]))
+    near[2], totals[0] = lax.optimization_barrier((near[2], totals[0]))
     last_cross = send_spec(near[2][1], 1)
-    held, mark = transfer_all(found, 0, strides[:2], bounds, paired, [None] * 2)
+    totals.append(pair_group(1, crossed[1]))
+    some = found + later
+    held, mark = transfer_all(some, 0, strides[:2], bounds, paired, [None] * 2)
     last_cross, mark = lax.optimization_barrier((last_cross, mark))
-    more, total = pair_up(here_ref, [[parts[2], *near[2], last_cross]], pair_kernel)
-    paired, totals = paired + more, totals + total
-    later = with_partners(two_back)
-    if 3 * count <= 6:
-        kernels = later + found
-        some = [(2 * count + k, k) for k in range(count)]
-        every = some + [(k, count + k) for k in range(2 * count)]
-        held, other = transfer(
-            kernels, [some, some, every], strides, bounds, paired, [*held, None]
-        )
-    else:
-        more, _ = transfer_all(found, 0, strides[2:], bounds, paired[2:], [None])
-        held, other = transfer_all(later, 2 * count, strides, bounds, paired, [*held, *more])
-    three_back, other = lax.optimization_barrier((three_back, other))
+    total = pair_group(2, last_cross)
+    three_back, total = lax.optimization_barrier((three_back, total))
+    totals.append(total)
     last = with_partners(three_back)
-    if last[:-1]:
-        held, _ = transfer_all(last[:-1], 3 * count, strides, bounds, paired, held)
+    more, other = transfer_all(some, 0, strides[2:], bounds, paired[2:], [None])
+    held += more
+    if last[:-2]:
+        held, _ = transfer_all(last[:-2], 3 * count, strides, bounds, paired, held)
+    last = last[-2:]
     maps = [ice_mask, wind_speed, wind_dir]
     out = finish(
-        last[-1:],
-        owners - 1,
+        last,
+        owners - len(last),
         groups,
         strides,
         bounds,

time: 100 us -> 97.5 us (0.975)
  waiting for transfers between devices: 24.7 us -> 22.8 us
    pallas_call x3 -> x2, Pallas kernels: 15.8 us -> 12.9 us  [transfer(): pl.pallas_call(functools.partial(transfer_body, uses, strides, kept), out...]
    ppermute x9, waiting for transfers between devices: 19.3 us -> 17.4 us  [send_spec(): return lax.ppermute(value, 'spec', [(i, i ^ flip) for i in range(4)])]
    pallas_call x1, Pallas kernels: 5.73 us -> 7.3 us  [finish(): pl.pallas_call(functools.partial(finish_body, len(kernels), first, groups...]
    pallas_call x2 -> x3, Pallas kernels: 12.1 us -> 13 us  [pair_up(): pl.pallas_call(functools.partial(pair_body, tile, sizes), grid=(comps //...]
  transfers between devices with their start and end apart: 18 -> 18, of which waited for: 7 -> 6; matrix products, arithmetic and copies ran while one was open for 4% -> 4% of each run, Pallas kernels for 38% -> 37%
where the time goes in v4:
time: 97.5 us; the launch traced here: 97.2 us
  Pallas kernels  42.8 us (44%)
  waiting for transfers between devices  22.8 us (23%)
  starting transfers between devices  21 us (22%)
  local copies, waits for them, and re-layouts  8.05 us (8%)
  other arithmetic  2.22 us (2%)
    ppermute x9, waiting for transfers between devices, send_spec(): return lax.ppermute(value, 'spec', [(i, i ^ flip) for i in range(4)])  17.4 us
    pallas_call x3, Pallas kernels, pair_up(): pl.pallas_call(functools.partial(pair_body, tile, sizes), grid=(comps //...  13 us
    pallas_call x2, Pallas kernels, transfer(): pl.pallas_call(functools.partial(transfer_body, uses, strides, kept), out...  12.9 us
    pallas_call x3, Pallas kernels, propagate(): pl.pallas_call(functools.partial(propagate_kernel, wanted, count), out_sh...  9.64 us
    ppermute x9, starting transfers between devices, send_spec(): return lax.ppermute(value, 'spec', [(i, i ^ flip) for i in range(4)])  9.19 us
    pallas_call x1, Pallas kernels, finish(): pl.pallas_call(functools.partial(finish_body, len(kernels), first, groups...  7.3 us
    ppermute x4, starting transfers between devices, with_partners(): found.append(lax.ppermute(kernel, 'place', pairs))  5.4 us
    unnamed x28, local copies, waits for them, and re-layouts  5.2 us
  transfers between devices with their start and end apart: 18, of which 6 were waited for; matrix products, arithmetic and copies ran while one was open for 4% of the time, Pallas kernels for 37%

profile of v4, /device:TPU:1, one launch (start us, length us, event | category | flops | bytes accessed | tf_op | source)
XLA Modules:
  0.0 97.2 jit_solution(12239361998992357765)
XLA Ops:
  0.0 1.4 %dynamic-slice_bitcast_fusion.refs_0_ = bf16[324,1296]{1,0:T(8,128)(2,1)S(1)} fusion(bf16[1,1296,1296]{2,1,0:T(8,128)(2,1)} %param.17, s32[]{:T(128)S(6)} %select_n.81), kind=kLoop, calls=%fused_computation | loop fusion | bytes 1679620 | tf_op jit(solution)/shard_map/dynamic_slice | solution.py:374
  1.4 2.2 %collective-permute-start = (bf16[324,1296]{1,0:T(8,128)(2,1)S(1)}, bf16[324,1296]{1,0:T(8,128)(2,1)}, u32[]{:S(2)}, u32[]{:S(2)}) collective-permute-start(bf16[324,1296]{1,0:T(8,128)(2,1)S(1)} %dynamic-slice_bitcast_fusion.refs_0_), channel_id=1, source_target_pairs={{0,2},{2,4},{4,6},{6,0},{1,3},{3,5},{5,7},{7,1},{8,10},{10,12},{12... | collective-permute-start | bytes 2519432 | tf_op jit(solution)/shard_map/ppermute | solution.py:314
  3.6 0.1 compare_convert_fusion
  3.7 0.1 abs_multiply_fusion
  3.7 0.1 fusion.13
  3.9 0.1 copy.28.coef_ref
  4.0 0.0 copy-start.9
  4.0 0.0 copy-start.10
  4.0 0.0 copy-start.4
  4.0 1.7 %copy.32 = bf16[324,16,128]{2,0,1:T(8,128)(2,1)S(1)} copy(bf16[324,16,128]{2,1,0:T(8,128)(2,1)} %param.9) | data formatting | bytes 2654208 | tf_op args[0]
  5.8 3.9 %shard_map.91 = (bf16[336,768]{1,0:T(8,128)(2,1)}, f32[1,768]{1,0:T(1,128)S(1)}) custom-call(bf16[16,324,128]{2,1,0:T(8,128)(2,1)S(1)} %bitcast.83, bf16[324,128]{1,0:T(8,128)(2,1)S(1)} %broadcast_in_dim.2.west_ref.east_ref, bf16[324,128]{1,0:T(8,128)(2,1)S(1)} %broadcast_in_dim.2.west_ref.east_ref, f32[16,128]{1,0:T(8,128)S(1)} %get-tuple-element.87.sea_ref, ...), custom_call_target="tpu_custom_call" | custom-call | flops 497664 | bytes 248832 | tf_op jit(solution)/shard_map/pallas_call | solution.py:126
  9.8 1.2 %collective-permute-start.3 = (bf16[336,768]{1,0:T(8,128)(2,1)}, bf16[336,768]{1,0:T(8,128)(2,1)}, u32[]{:S(2)}, u32[]{:S(2)}) collective-permute-start(bf16[336,768]{1,0:T(8,128)(2,1)} %get-tuple-element.43.refs_0_.refs_14_), channel_id=1, source_target_pairs={{0,8},{8,0},{16,24},{24,16},{1,9},{9,1},{17,25},{25,17},{2,10},{10... | collective-permute-start | bytes 1548296 | tf_op jit(solution)/shard_map/ppermute | solution.py:357
  11.0 1.2 %collective-permute-start.4 = (bf16[336,768]{1,0:T(8,128)(2,1)}, bf16[336,768]{1,0:T(8,128)(2,1)}, u32[]{:S(2)}, u32[]{:S(2)}) collective-permute-start(bf16[336,768]{1,0:T(8,128)(2,1)} %get-tuple-element.43.refs_0_.refs_14_), channel_id=1, source_target_pairs={{0,16},{8,24},{16,0},{24,8},{1,17},{9,25},{17,1},{25,9},{2,18},{10... | collective-permute-start | bytes 1548296 | tf_op jit(solution)/shard_map/ppermute | solution.py:357
  12.2 1.5 %collective-permute-start.10 = (bf16[324,1296]{1,0:T(8,128)(2,1)S(1)}, bf16[324,1296]{1,0:T(8,128)(2,1)S(1)}, u32[]{:S(2)}, u32[]{:S(2)}) collective-permute-start(bf16[324,1296]{1,0:T(8,128)(2,1)S(1)} %dynamic-slice_bitcast_fusion.refs_0_), channel_id=1, source_target_pairs={{0,1},{1,0},{2,3},{3,2},{4,5},{5,4},{6,7},{7,6},{8,9},{9,8},{10,11... | collective-permute-start | bytes 2519432 | tf_op jit(solution)/shard_map/ppermute | solution.py:344
  13.7 0.7 broadcast_select_fusion.2
  14.4 0.0 collective-permute-start.1
  14.4 1.5 %collective-permute-done.1 = bf16[324,128]{1,0:T(8,128)(2,1)S(1)} collective-permute-done((bf16[324,128]{1,0:T(8,128)(2,1)S(1)}, bf16[324,128]{1,0:T(8,128)(2,1)S(1)}, u32[]{:S(2)}, u32[]{:S(2)}) %collective-permute-start.1) | collective-permute-done | bytes 82976 | tf_op jit(solution)/shard_map/ppermute | solution.py:326
  15.9 0.6 copy-done.8
  16.6 3.5 %collective-permute-start.2 = (bf16[324,128]{1,0:T(8,128)(2,1)}, bf16[324,128]{1,0:T(8,128)(2,1)}, u32[]{:S(2)}, u32[]{:S(2)}) collective-permute-start(bf16[324,128]{1,0:T(8,128)(2,1)} %get-tuple-element.81), channel_id=1, source_target_pairs={{1,2},{3,4},{5,6},{2,1},{4,3},{6,5},{9,10},{11,12},{13,14},{10,9},... | collective-permute-start | bytes 248840 | tf_op jit(solution)/shard_map/ppermute | solution.py:328
  20.0 3.1 %shard_map.92 = (bf16[336,768]{1,0:T(8,128)(2,1)S(1)}, f32[1,768]{1,0:T(1,128)S(1)}) custom-call(bf16[16,324,128]{2,1,0:T(8,128)(2,1)S(1)} %bitcast.84, bf16[324,128]{1,0:T(8,128)(2,1)S(1)} %broadcast_in_dim.2.west_ref.east_ref, bf16[324,128]{1,0:T(8,128)(2,1)S(1)} %broadcast_in_dim.2.west_ref.east_ref, f32[16,128]{1,0:T(8,128)S(1)} %get-tuple-element.87.sea_ref, ...), custom_call_target="tpu_custom_call" | custom-call | flops 497664 | bytes 248832 | tf_op jit(solution)/shard_map/pallas_call | solution.py:126
  23.2 0.8 copy-done.2
  24.0 3.4 %collective-permute-done.2 = bf16[324,128]{1,0:T(8,128)(2,1)} collective-permute-done((bf16[324,128]{1,0:T(8,128)(2,1)}, bf16[324,128]{1,0:T(8,128)(2,1)}, u32[]{:S(2)}, u32[]{:S(2)}) %collective-permute-start.2) | collective-permute-done | bytes 82976 | tf_op jit(solution)/shard_map/ppermute | solution.py:328
  27.4 0.0 collective-permute-done.3.refs_1_
  27.4 0.0 collective-permute-done.4.refs_2_
  27.4 0.0 collective-permute-done.refs_2_
  27.4 1.3 %collective-permute-start.7 = (bf16[336,768]{1,0:T(8,128)(2,1)}, bf16[336,768]{1,0:T(8,128)(2,1)S(1)}, u32[]{:S(2)}, u32[]{:S(2)}) collective-permute-start(bf16[336,768]{1,0:T(8,128)(2,1)} %copy-done.2), channel_id=1, source_target_pairs={{0,8},{8,0},{16,24},{24,16},{1,9},{9,1},{17,25},{25,17},{2,10},{10... | collective-permute-start | bytes 1548296 | tf_op jit(solution)/shard_map/ppermute | solution.py:357
  28.7 0.2 collective-permute-start.11
  28.9 0.2 collective-permute-start.5
  29.1 1.2 %collective-permute-start.9 = (bf16[336,768]{1,0:T(8,128)(2,1)}, bf16[336,768]{1,0:T(8,128)(2,1)S(1)}, u32[]{:S(2)}, u32[]{:S(2)}) collective-permute-start(bf16[336,768]{1,0:T(8,128)(2,1)} %copy-done.2), channel_id=1, source_target_pairs={{0,16},{8,24},{16,0},{24,8},{1,17},{9,25},{17,1},{25,9},{2,18},{10... | collective-permute-start | bytes 1548296 | tf_op jit(solution)/shard_map/ppermute | solution.py:357
  30.3 0.0 collective-permute-done.10.refs_1_
  30.3 0.3 collective-permute-start.6
  30.6 10.5 %collective-permute-done.7.refs_1_ = bf16[336,768]{1,0:T(8,128)(2,1)S(1)} collective-permute-done((bf16[336,768]{1,0:T(8,128)(2,1)}, bf16[336,768]{1,0:T(8,128)(2,1)S(1)}, u32[]{:S(2)}, u32[]{:S(2)}) %collective-permute-start.7) | collective-permute-done | bytes 516128 | tf_op jit(solution)/shard_map/ppermute | solution.py:357
  41.1 1.2 %collective-permute-start.8 = (bf16[336,768]{1,0:T(8,128)(2,1)S(1)}, bf16[336,768]{1,0:T(8,128)(2,1)S(1)}, u32[]{:S(2)}, u32[]{:S(2)}) collective-permute-start(bf16[336,768]{1,0:T(8,128)(2,1)S(1)} %collective-permute-done.7.refs_1_), channel_id=1, source_target_pairs={{0,16},{8,24},{16,0},{24,8},{1,17},{9,25},{17,1},{25,9},{2,18},{10... | collective-permute-start | bytes 1548296 | tf_op jit(solution)/shard_map/ppermute | solution.py:357
  42.3 1.0 broadcast_select_fusion
  43.3 2.6 %shard_map.93 = (bf16[336,512]{1,0:T(8,128)(2,1)S(1)}, f32[1,512]{1,0:T(1,128)S(1)}) custom-call(bf16[16,324,128]{2,1,0:T(8,128)(2,1)S(1)} %bitcast.85, bf16[324,128]{1,0:T(8,128)(2,1)S(1)} %get-tuple-element.86.west_ref, bf16[324,128]{1,0:T(8,128)(2,1)S(1)} %get-tuple-element.85.east_ref, f32[16,128]{1,0:T(8,128)S(1)} %get-tuple-element.87.sea_ref, ...), custom_call_target="tpu_custom_call" | custom-call | flops 331776 | bytes 165888 | tf_op jit(solution)/shard_map/pallas_call | solution.py:126
  45.9 0.0 collective-permute-done.11.refs_3_
  45.9 6.2 %collective-permute-done.6.refs_3_ = bf16[336,768]{1,0:T(8,128)(2,1)S(1)} collective-permute-done((bf16[336,768]{1,0:T(8,128)(2,1)}, bf16[336,768]{1,0:T(8,128)(2,1)S(1)}, u32[]{:S(2)}, u32[]{:S(2)}) %collective-permute-start.6) | collective-permute-done | bytes 516128 | tf_op jit(solution)/shard_map/ppermute | solution.py:357
  52.1 0.0 collective-permute-done.9.refs_2_
  52.2 0.5 collective-permute-done.5.refs_4_
  52.6 0.7 collective-permute-done.8.refs_3_
  53.3 2.0 %collective-permute-start.16 = (bf16[324,1296]{1,0:T(8,128)(2,1)S(1)}, bf16[324,1296]{1,0:T(8,128)(2,1)S(1)}, u32[]{:S(2)}, u32[]{:S(2)}) collective-permute-start(bf16[324,1296]{1,0:T(8,128)(2,1)S(1)} %collective-permute-done.5.refs_4_), channel_id=1, source_target_pairs={{0,1},{1,0},{2,3},{3,2},{4,5},{5,4},{6,7},{7,6},{8,9},{9,8},{10,11... | collective-permute-start | bytes 2519432 | tf_op jit(solution)/shard_map/ppermute | solution.py:344
  55.3 0.5 collective-permute-start.12
  55.8 1.1 %collective-permute-start.13 = (bf16[336,512]{1,0:T(8,128)(2,1)S(1)}, bf16[336,512]{1,0:T(8,128)(2,1)S(1)}, u32[]{:S(2)}, u32[]{:S(2)}) collective-permute-start(bf16[336,512]{1,0:T(8,128)(2,1)S(1)} %get-tuple-element.52.refs_0_.refs_16_), channel_id=1, source_target_pairs={{0,8},{8,0},{16,24},{24,16},{1,9},{9,1},{17,25},{25,17},{2,10},{10... | collective-permute-start | bytes 1032200 | tf_op jit(solution)/shard_map/ppermute | solution.py:357
  56.9 1.2 %collective-permute-start.14 = (bf16[336,512]{1,0:T(8,128)(2,1)S(1)}, bf16[336,512]{1,0:T(8,128)(2,1)S(1)}, u32[]{:S(2)}, u32[]{:S(2)}) collective-permute-start(bf16[336,512]{1,0:T(8,128)(2,1)S(1)} %get-tuple-element.52.refs_0_.refs_16_), channel_id=1, source_target_pairs={{0,16},{8,24},{16,0},{24,8},{1,17},{9,25},{17,1},{25,9},{2,18},{10... | collective-permute-start | bytes 1032200 | tf_op jit(solution)/shard_map/ppermute | solution.py:357
  58.1 0.0 copy-start
  58.1 2.0 %copy-done = bf16[1296,1296]{1,0:T(8,128)(2,1)S(1)} copy-done((bf16[1296,1296]{1,0:T(8,128)(2,1)S(1)}, bf16[1296,1296]{1,0:T(8,128)(2,1)}, u32[]{:S(2)}) %copy-start) | copy-done | bytes 3359256
  60.2 5.8 %shard_map.94 = (bf16[1296,768]{1,0:T(8,128)(2,1)S(1)}, f32[1,768]{1,0:T(1,128)S(1)}) custom-call(s32[1]{0:T(128)} %bitcast.22.here_ref, bf16[336,768]{1,0:T(8,128)(2,1)} %get-tuple-element.43.refs_0_.refs_14_, bf16[336,768]{1,0:T(8,128)(2,1)} %collective-permute-done.3.refs_1_, bf16[336,768]{1,0:T(8,128)(2,1)} %collective-permute-done.4.refs_2_, ...), custom_call_target="tpu_custom_call" | custom-call | flops 322486272 | bytes 419904 | tf_op jit(solution)/shard_map/pallas_call | solution.py:185
  65.9 0.0 collective-permute-done.13.refs_1_
  65.9 0.0 collective-permute-done.14.refs_2_
  65.9 0.4 collective-permute-start.15
  66.4 0.1 convert_reduce_fusion.2
  66.5 0.1 convert_reduce_fusion
  66.6 0.1 pad_add_fusion.1.bounds_ref
  66.7 4.3 %shard_map.95 = (bf16[1296,768]{1,0:T(8,128)(2,1)S(1)}, f32[1,768]{1,0:T(1,128)S(1)}) custom-call(s32[1]{0:T(128)} %bitcast.22.here_ref, bf16[336,768]{1,0:T(8,128)(2,1)S(1)} %copy-done.3, bf16[336,768]{1,0:T(8,128)(2,1)S(1)} %collective-permute-done.7.refs_1_, bf16[336,768]{1,0:T(8,128)(2,1)S(1)} %collective-permute-done.9.refs_2_, ...), custom_call_target="tpu_custom_call" | custom-call | flops 322486272 | bytes 419904 | tf_op jit(solution)/shard_map/pallas_call | solution.py:185
  71.0 0.0 collective-permute-done.16.refs_5_
  71.0 8.6 %shard_map.96 = (bf16[324,768]{1,0:T(8,128)(2,1)S(1)}, bf16[324,768]{1,0:T(8,128)(2,1)S(1)}, f32[8,128]{1,0:T(8,128)S(1)}) custom-call(s32[27]{0:T(128)S(1)} %pad_add_fusion.1.bounds_ref, bf16[324,1296]{1,0:T(8,128)(2,1)S(1)} %dynamic-slice_bitcast_fusion.refs_0_, bf16[324,1296]{1,0:T(8,128)(2,1)S(1)} %collective-permute-done.10.refs_1_, ...), custom_call_target="tpu_custom_call" | custom-call | flops 483729408 | bytes 1127520 | tf_op jit(solution)/shard_map/pallas_call | solution.py:242
  79.6 0.0 collective-permute-done.15.refs_3_
  79.6 2.9 %shard_map.97 = (bf16[1296,512]{1,0:T(8,128)(2,1)S(1)}, f32[1,512]{1,0:T(1,128)S(1)}) custom-call(s32[1]{0:T(128)} %bitcast.22.here_ref, bf16[336,512]{1,0:T(8,128)(2,1)S(1)} %get-tuple-element.52.refs_0_.refs_16_, bf16[336,512]{1,0:T(8,128)(2,1)S(1)} %collective-permute-done.13.refs_1_, bf16[336,512]{1,0:T(8,128)(2,1)S(1)} %collective-permute-done.14.refs_2_, ...), custom_call_target="tpu_custom_call" | custom-call | flops 214990848 | bytes 419904 | tf_op jit(solution)/shard_map/pallas_call | solution.py:185
  82.5 0.0 collective-permute-done.12.refs_0_
  82.5 1.7 %collective-permute-start.17 = (bf16[324,1296]{1,0:T(8,128)(2,1)S(1)}, bf16[324,1296]{1,0:T(8,128)(2,1)S(1)}, u32[]{:S(2)}, u32[]{:S(2)}) collective-permute-start(bf16[324,1296]{1,0:T(8,128)(2,1)S(1)} %collective-permute-done.12.refs_0_), channel_id=1, source_target_pairs={{0,1},{1,0},{2,3},{3,2},{4,5},{5,4},{6,7},{7,6},{8,9},{9,8},{10,11... | collective-permute-start | bytes 2519432 | tf_op jit(solution)/shard_map/ppermute | solution.py:344
  84.2 4.3 %shard_map.98 = (bf16[324,512]{1,0:T(8,128)(2,1)S(1)}, f32[8,128]{1,0:T(8,128)S(1)}) custom-call(s32[27]{0:T(128)S(1)} %pad_add_fusion.1.bounds_ref, bf16[324,1296]{1,0:T(8,128)(2,1)S(1)} %dynamic-slice_bitcast_fusion.refs_0_, bf16[324,1296]{1,0:T(8,128)(2,1)S(1)} %collective-permute-done.10.refs_1_, bf16[324,1296]{1,0:T(8,128)(2,1)} %collective-permute-done.refs_2_, ...), custom_call_target="tpu_custom_call" | custom-call | flops 161243136 | bytes 795744 | tf_op jit(solution)/shard_map/pallas_call | solution.py:242
  88.6 0.0 collective-permute-done.17.refs_1_
  88.6 7.3 %shard_map.99 = bf16[16,324,128]{2,1,0:T(8,128)(2,1)S(1)} custom-call(s32[27]{0:T(128)S(1)} %pad_add_fusion.1.bounds_ref, f32[324,6]{1,0:T(8,128)S(1)} %copy.28.coef_ref, s32[16,128]{1,0:T(8,128)S(1)} %copy-done.5, bf16[16,128]{1,0:T(8,128)(2,1)S(1)} %copy-done.6, bf16[16,128]{1,0:T(8,128)(2,1)S(1)} %copy-done.7, ...), custom_call_target="tpu_custom_call" | custom-call | flops 214990848 | bytes 873504 | tf_op jit(solution)/shard_map/pallas_call | solution.py:302
  95.9 1.2 %copy.29 = bf16[324,16,128]{2,1,0:T(8,128)(2,1)} copy(bf16[324,16,128]{2,0,1:T(8,128)(2,1)S(1)} %bitcast.86) | data formatting | bytes 2654208 | tf_op jit(solution)/shard_map/transpose | solution.py:484
  (32 shorter events, 0.2 us)
Async XLA Ops:
  1.4 26.0 %collective-permute-start = (bf16[324,1296]{1,0:T(8,128)(2,1)S(1)}, bf16[324,1296]{1,0:T(8,128)(2,1)}, u32[]{:S(2)}, u32[]{:S(2)}) collective-permute-start(bf16[324,1296]{1,0:T(8,128)(2,1)S(1)} %dynamic-slice_bitcast_fusion.refs_0_), channel_id=1, source_target_pairs={{0,2},{2,4},{4,6},{6,0},{1,3},{3,5},{5,7},{7,1},{8,10},{10,12},{12... | collective-permute-start | bytes 2519432 | tf_op jit(solution)/shard_map/ppermute | solution.py:314
  4.0 1.7 %copy-start.9 = (s32[16,128]{1,0:T(8,128)S(1)}, s32[16,128]{1,0:T(8,128)}, u32[]{:S(2)}) copy-start(s32[16,128]{1,0:T(8,128)} %param.10) | copy-start | bytes 24580
  4.0 1.7 %copy-start.10 = (s32[16,128]{1,0:T(8,128)S(1)}, s32[16,128]{1,0:T(8,128)}, u32[]{:S(2)}) copy-start(s32[16,128]{1,0:T(8,128)} %param.15) | copy-start | bytes 24580
  4.0 1.8 %copy-start.4 = (f32[16,128]{1,0:T(8,128)S(1)}, f32[16,128]{1,0:T(8,128)}, u32[]{:S(2)}) copy-start(f32[16,128]{1,0:T(8,128)} %depth_ref.5) | copy-start | bytes 24580
  9.8 17.6 %collective-permute-start.3 = (bf16[336,768]{1,0:T(8,128)(2,1)}, bf16[336,768]{1,0:T(8,128)(2,1)}, u32[]{:S(2)}, u32[]{:S(2)}) collective-permute-start(bf16[336,768]{1,0:T(8,128)(2,1)} %get-tuple-element.43.refs_0_.refs_14_), channel_id=1, source_target_pairs={{0,8},{8,0},{16,24},{24,16},{1,9},{9,1},{17,25},{25,17},{2,10},{10... | collective-permute-start | bytes 1548296 | tf_op jit(solution)/shard_map/ppermute | solution.py:357
  11.0 16.4 %collective-permute-start.4 = (bf16[336,768]{1,0:T(8,128)(2,1)}, bf16[336,768]{1,0:T(8,128)(2,1)}, u32[]{:S(2)}, u32[]{:S(2)}) collective-permute-start(bf16[336,768]{1,0:T(8,128)(2,1)} %get-tuple-element.43.refs_0_.refs_14_), channel_id=1, source_target_pairs={{0,16},{8,24},{16,0},{24,8},{1,17},{9,25},{17,1},{25,9},{2,18},{10... | collective-permute-start | bytes 1548296 | tf_op jit(solution)/shard_map/ppermute | solution.py:357
  12.2 18.1 %collective-permute-start.10 = (bf16[324,1296]{1,0:T(8,128)(2,1)S(1)}, bf16[324,1296]{1,0:T(8,128)(2,1)S(1)}, u32[]{:S(2)}, u32[]{:S(2)}) collective-permute-start(bf16[324,1296]{1,0:T(8,128)(2,1)S(1)} %dynamic-slice_bitcast_fusion.refs_0_), channel_id=1, source_target_pairs={{0,1},{1,0},{2,3},{3,2},{4,5},{5,4},{6,7},{7,6},{8,9},{9,8},{10,11... | collective-permute-start | bytes 2519432 | tf_op jit(solution)/shard_map/ppermute | solution.py:344
  14.4 1.5 %collective-permute-start.1 = (bf16[324,128]{1,0:T(8,128)(2,1)S(1)}, bf16[324,128]{1,0:T(8,128)(2,1)S(1)}, u32[]{:S(2)}, u32[]{:S(2)}) collective-permute-start(bf16[324,128]{1,0:T(8,128)(2,1)S(1)} %get-tuple-element.82), channel_id=1, source_target_pairs={{0,1},{1,0},{2,3},{3,2},{4,5},{5,4},{6,7},{7,6},{8,9},{9,8},{10,11... | collective-permute-start | bytes 248840 | tf_op jit(solution)/shard_map/ppermute | solution.py:326
  15.9 0.6 copy-start.8
  16.6 10.8 %collective-permute-start.2 = (bf16[324,128]{1,0:T(8,128)(2,1)}, bf16[324,128]{1,0:T(8,128)(2,1)}, u32[]{:S(2)}, u32[]{:S(2)}) collective-permute-start(bf16[324,128]{1,0:T(8,128)(2,1)} %get-tuple-element.81), channel_id=1, source_target_pairs={{1,2},{3,4},{5,6},{2,1},{4,3},{6,5},{9,10},{11,12},{13,14},{10,9},... | collective-permute-start | bytes 248840 | tf_op jit(solution)/shard_map/ppermute | solution.py:328
  23.2 0.8 copy-start.2
  27.4 13.7 %collective-permute-start.7 = (bf16[336,768]{1,0:T(8,128)(2,1)}, bf16[336,768]{1,0:T(8,128)(2,1)S(1)}, u32[]{:S(2)}, u32[]{:S(2)}) collective-permute-start(bf16[336,768]{1,0:T(8,128)(2,1)} %copy-done.2), channel_id=1, source_target_pairs={{0,8},{8,0},{16,24},{24,16},{1,9},{9,1},{17,25},{25,17},{2,10},{10... | collective-permute-start | bytes 1548296 | tf_op jit(solution)/shard_map/ppermute | solution.py:357
  28.7 17.2 %collective-permute-start.11 = (bf16[324,1296]{1,0:T(8,128)(2,1)}, bf16[324,1296]{1,0:T(8,128)(2,1)S(1)}, u32[]{:S(2)}, u32[]{:S(2)}) collective-permute-start(bf16[324,1296]{1,0:T(8,128)(2,1)} %collective-permute-done.refs_2_), channel_id=1, source_target_pairs={{0,1},{1,0},{2,3},{3,2},{4,5},{5,4},{6,7},{7,6},{8,9},{9,8},{10,11... | collective-permute-start | bytes 2519432 | tf_op jit(solution)/shard_map/ppermute | solution.py:344
  28.9 23.7 %collective-permute-start.5 = (bf16[324,1296]{1,0:T(8,128)(2,1)}, bf16[324,1296]{1,0:T(8,128)(2,1)S(1)}, u32[]{:S(2)}, u32[]{:S(2)}) collective-permute-start(bf16[324,1296]{1,0:T(8,128)(2,1)} %collective-permute-done.refs_2_), channel_id=1, source_target_pairs={{0,2},{2,4},{4,6},{6,0},{1,3},{3,5},{5,7},{7,1},{8,10},{10,12},{12... | collective-permute-start | bytes 2519432 | tf_op jit(solution)/shard_map/ppermute | solution.py:314
  29.1 23.1 %collective-permute-start.9 = (bf16[336,768]{1,0:T(8,128)(2,1)}, bf16[336,768]{1,0:T(8,128)(2,1)S(1)}, u32[]{:S(2)}, u32[]{:S(2)}) collective-permute-start(bf16[336,768]{1,0:T(8,128)(2,1)} %copy-done.2), channel_id=1, source_target_pairs={{0,16},{8,24},{16,0},{24,8},{1,17},{9,25},{17,1},{25,9},{2,18},{10... | collective-permute-start | bytes 1548296 | tf_op jit(solution)/shard_map/ppermute | solution.py:357
  30.3 21.8 %collective-permute-start.6 = (bf16[336,768]{1,0:T(8,128)(2,1)}, bf16[336,768]{1,0:T(8,128)(2,1)S(1)}, u32[]{:S(2)}, u32[]{:S(2)}) collective-permute-start(bf16[336,768]{1,0:T(8,128)(2,1)} %collective-permute-done.4.refs_2_), channel_id=1, source_target_pairs={{0,8},{8,0},{16,24},{24,16},{1,9},{9,1},{17,25},{25,17},{2,10},{10... | collective-permute-start | bytes 1548296 | tf_op jit(solution)/shard_map/ppermute | solution.py:357
  41.1 12.2 %collective-permute-start.8 = (bf16[336,768]{1,0:T(8,128)(2,1)S(1)}, bf16[336,768]{1,0:T(8,128)(2,1)S(1)}, u32[]{:S(2)}, u32[]{:S(2)}) collective-permute-start(bf16[336,768]{1,0:T(8,128)(2,1)S(1)} %collective-permute-done.7.refs_1_), channel_id=1, source_target_pairs={{0,16},{8,24},{16,0},{24,8},{1,17},{9,25},{17,1},{25,9},{2,18},{10... | collective-permute-start | bytes 1548296 | tf_op jit(solution)/shard_map/ppermute | solution.py:357
  53.3 17.7 %collective-permute-start.16 = (bf16[324,1296]{1,0:T(8,128)(2,1)S(1)}, bf16[324,1296]{1,0:T(8,128)(2,1)S(1)}, u32[]{:S(2)}, u32[]{:S(2)}) collective-permute-start(bf16[324,1296]{1,0:T(8,128)(2,1)S(1)} %collective-permute-done.5.refs_4_), channel_id=1, source_target_pairs={{0,1},{1,0},{2,3},{3,2},{4,5},{5,4},{6,7},{7,6},{8,9},{9,8},{10,11... | collective-permute-start | bytes 2519432 | tf_op jit(solution)/shard_map/ppermute | solution.py:344
  55.3 27.3 %collective-permute-start.12 = (bf16[324,1296]{1,0:T(8,128)(2,1)S(1)}, bf16[324,1296]{1,0:T(8,128)(2,1)S(1)}, u32[]{:S(2)}, u32[]{:S(2)}) collective-permute-start(bf16[324,1296]{1,0:T(8,128)(2,1)S(1)} %collective-permute-done.5.refs_4_), channel_id=1, source_target_pairs={{0,2},{2,4},{4,6},{6,0},{1,3},{3,5},{5,7},{7,1},{8,10},{10,12},{12... | collective-permute-start | bytes 2519432 | tf_op jit(solution)/shard_map/ppermute | solution.py:314
  55.8 10.1 %collective-permute-start.13 = (bf16[336,512]{1,0:T(8,128)(2,1)S(1)}, bf16[336,512]{1,0:T(8,128)(2,1)S(1)}, u32[]{:S(2)}, u32[]{:S(2)}) collective-permute-start(bf16[336,512]{1,0:T(8,128)(2,1)S(1)} %get-tuple-element.52.refs_0_.refs_16_), channel_id=1, source_target_pairs={{0,8},{8,0},{16,24},{24,16},{1,9},{9,1},{17,25},{25,17},{2,10},{10... | collective-permute-start | bytes 1032200 | tf_op jit(solution)/shard_map/ppermute | solution.py:357
  56.9 9.1 %collective-permute-start.14 = (bf16[336,512]{1,0:T(8,128)(2,1)S(1)}, bf16[336,512]{1,0:T(8,128)(2,1)S(1)}, u32[]{:S(2)}, u32[]{:S(2)}) collective-permute-start(bf16[336,512]{1,0:T(8,128)(2,1)S(1)} %get-tuple-element.52.refs_0_.refs_16_), channel_id=1, source_target_pairs={{0,16},{8,24},{16,0},{24,8},{1,17},{9,25},{17,1},{25,9},{2,18},{10... | collective-permute-start | bytes 1032200 | tf_op jit(solution)/shard_map/ppermute | solution.py:357
  58.1 2.0 %copy-start = (bf16[1296,1296]{1,0:T(8,128)(2,1)S(1)}, bf16[1296,1296]{1,0:T(8,128)(2,1)}, u32[]{:S(2)}) copy-start(bf16[1296,1296]{1,0:T(8,128)(2,1)} %refs_4_.5) | copy-start | bytes 10077700
  60.2 6.6 %copy-start.1 = (bf16[1296,1296]{1,0:T(8,128)(2,1)S(1)}, bf16[1296,1296]{1,0:T(8,128)(2,1)}, u32[]{:S(2)}) copy-start(bf16[1296,1296]{1,0:T(8,128)(2,1)} %refs_4_.5) | copy-start | bytes 10077700
  60.2 6.6 %copy-start.3 = (bf16[336,768]{1,0:T(8,128)(2,1)S(1)}, bf16[336,768]{1,0:T(8,128)(2,1)}, u32[]{:S(2)}) copy-start(bf16[336,768]{1,0:T(8,128)(2,1)} %copy-done.2) | copy-start | bytes 1548292
  65.9 13.6 %collective-permute-start.15 = (bf16[336,512]{1,0:T(8,128)(2,1)S(1)}, bf16[336,512]{1,0:T(8,128)(2,1)S(1)}, u32[]{:S(2)}, u32[]{:S(2)}) collective-permute-start(bf16[336,512]{1,0:T(8,128)(2,1)S(1)} %collective-permute-done.14.refs_2_), channel_id=1, source_target_pairs={{0,8},{8,0},{16,24},{24,16},{1,9},{9,1},{17,25},{25,17},{2,10},{10... | collective-permute-start | bytes 1032200 | tf_op jit(solution)/shard_map/ppermute | solution.py:357
  82.5 6.0 %collective-permute-start.17 = (bf16[324,1296]{1,0:T(8,128)(2,1)S(1)}, bf16[324,1296]{1,0:T(8,128)(2,1)S(1)}, u32[]{:S(2)}, u32[]{:S(2)}) collective-permute-start(bf16[324,1296]{1,0:T(8,128)(2,1)S(1)} %collective-permute-done.12.refs_0_), channel_id=1, source_target_pairs={{0,1},{1,0},{2,3},{3,2},{4,5},{5,4},{6,7},{7,6},{8,9},{9,8},{10,11... | collective-permute-start | bytes 2519432 | tf_op jit(solution)/shard_map/ppermute | solution.py:344
  84.2 4.4 %copy-start.5 = (s32[16,128]{1,0:T(8,128)S(1)}, s32[16,128]{1,0:T(8,128)}, u32[]{:S(2)}) copy-start(s32[16,128]{1,0:T(8,128)} %ice_ref.1) | copy-start | bytes 24580
  84.2 4.4 %copy-start.6 = (bf16[16,128]{1,0:T(8,128)(2,1)S(1)}, bf16[16,128]{1,0:T(8,128)(2,1)}, u32[]{:S(2)}) copy-start(bf16[16,128]{1,0:T(8,128)(2,1)} %speed_ref.1) | copy-start | bytes 12292
  84.2 4.4 %copy-start.7 = (bf16[16,128]{1,0:T(8,128)(2,1)S(1)}, bf16[16,128]{1,0:T(8,128)(2,1)}, u32[]{:S(2)}) copy-start(bf16[16,128]{1,0:T(8,128)(2,1)} %angle_ref.1) | copy-start | bytes 12292

commit v5 on v4

--- a/solution.py
+++ b/solution.py
@@ -424,44 +424,52 @@
     parts, places = zip(*(move_rows(group, none, none) for group in groups[:2]))
     parts, places = list(parts), list(places)
     near = [meet(parts[0])]
-    one_back, halos, near[0], sent = lax.optimization_barrier(
-        (one_back, halos, near[0], parts[1])
-    )
-
+    one_back, halos, near[0], sent, own_now = lax.optimization_barrier(
+        (one_back, halos, near[0], parts[1], own_rows)
+    )
+
+    def pair_group(i, far):
+        (more,), (total,) = pair_up(here_ref, [[parts[i], *near[i], far]], pair_kernel)
+        paired.append(more)
+        totals.append(total)
+
+    paired, totals = [], []
     two_back = next_plane(one_back)
-    near.append(meet(sent))
-    crossed = [send_spec(near[0][1], 1), send_spec(near[1][0], 2)]
+    crossed = send_spec(near[0][1], 1)
+    other = send_spec(sent, 2)
     part, place = move_rows(groups[2], *before_and_after(*halos))
+    crossed, sent, place = lax.optimization_barrier((crossed, sent, place))
+    near.append([send_spec(sent, 1), other])
     parts.append(part)
     places.append(place)
-    found = with_partners(own_rows) + with_partners(one_back)
+    second = send_spec(part, 2)
+    found = with_partners(own_now) + with_partners(one_back)
     marks = [value[:8, :128] for value in (found[1], found[count + 1])]
-    two_back, crossed, near[1], sent, marks = lax.optimization_barrier(
-        (two_back, crossed, near[1], parts[2], marks)
-    )
-    near.append(meet(sent))
+    pair_group(0, crossed)
+    two_back, near[1], second, sent, totals, marks = lax.optimization_barrier(
+        (two_back, near[1], second, part, totals, marks)
+    )
+
     three_back = next_plane(two_back)
     later = with_partners(two_back)
-    paired, totals = [], []
-
-    def pair_group(i, far):
-        more, total = pair_up(here_ref, [[parts[i], *near[i], far]], pair_kernel)
-        paired.extend(more)
-        return total[0]
-
-    totals.append(pair_group(0, crossed[0]))
-    near[2], totals[0] = lax.optimization_barrier((near[2], totals[0]))
-    last_cross = send_spec(near[2][1], 1)
-    totals.append(pair_group(1, crossed[1]))
+    crossed = send_spec(near[1][0], 2)
+    near.append([send_spec(sent, 1), second])
+    last_cross = send_spec(second, 1)
     some = found + later
-    held, mark = transfer_all(some, 0, strides[:2], bounds, paired, [None] * 2)
-    last_cross, mark = lax.optimization_barrier((last_cross, mark))
-    total = pair_group(2, last_cross)
-    three_back, total = lax.optimization_barrier((three_back, total))
-    totals.append(total)
+    held, mark = transfer_all(some, 0, strides[:1], bounds, paired, [None])
+    crossed, mark = lax.optimization_barrier((crossed, mark))
+    marks.append(mark)
+    pair_group(1, crossed)
+    last_cross, totals[1] = lax.optimization_barrier((last_cross, totals[1]))
+    pair_group(2, last_cross)
+    more, mark = transfer_all(some, 0, strides[1:2], bounds, paired[1:2], [None])
+    held += more
+    three_back, mark, totals[2] = lax.optimization_barrier((three_back, mark, totals[2]))
+    marks.append(mark)
     last = with_partners(three_back)
-    more, other = transfer_all(some, 0, strides[2:], bounds, paired[2:], [None])
+    more, mark = transfer_all(some, 0, strides[2:], bounds, paired[2:], [None])
     held += more
+    marks.append(mark)
     if last[:-2]:
         held, _ = transfer_all(last[:-2], 3 * count, strides, bounds, paired, held)
     last = last[-2:]
@@ -479,7 +487,7 @@
         paired,
         held,
         parts,
-        [mark, other, *marks],
+        marks,
     )
     return out.transpose(1, 0, 2)
 

time: 97.5 us -> 94.6 us (0.970)
  waiting for transfers between devices: 22.8 us -> 21.4 us
  Pallas kernels: 42.8 us -> 41.7 us
    ppermute x9, waiting for transfers between devices: 17.4 us -> 13.7 us  [send_spec(): return lax.ppermute(value, 'spec', [(i, i ^ flip) for i in range(4)])]
    ppermute x1, waiting for transfers between devices: 3.39 us -> 5.94 us  [boundaries(): lax.ppermute(jnp.where(first, top, bottom), geo, pairs + [(j, i) for i, j...]
    ppermute x4, starting transfers between devices: 5.4 us -> 3.53 us  [with_partners(): found.append(lax.ppermute(kernel, 'place', pairs))]
    ppermute x1, waiting for transfers between devices: 1.54 us -> 0.01 us  [boundaries(): lax.ppermute(jnp.where(first, bottom, top), 'place', [(0, 1), (1, 0)])]
    ppermute x1, starting transfers between devices: 0.01 us -> 1.51 us  [boundaries(): lax.ppermute(jnp.where(first, bottom, top), 'place', [(0, 1), (1, 0)])]
    ppermute x3, waiting for transfers between devices: 0.46 us -> 1.68 us  [next_plane(): lax.ppermute(value, 'plane', [(i, (i + 1) % PLANES) for i in range(PLANES)])]
    ppermute x9, starting transfers between devices: 9.19 us -> 10.2 us  [send_spec(): return lax.ppermute(value, 'spec', [(i, i ^ flip) for i in range(4)])]
    pallas_call x2 -> x3, Pallas kernels: 12.9 us -> 12.1 us  [transfer(): pl.pallas_call(functools.partial(transfer_body, uses, strides, kept), out...]
  transfers between devices with their start and end apart: 18 -> 18, of which waited for: 6 -> 6; matrix products, arithmetic and copies ran while one was open for 4% -> 4% of each run, Pallas kernels for 37% -> 36%
where the time goes in v5:
time: 94.6 us; the launch traced here: 94.3 us
  Pallas kernels  41.7 us (44%)
  waiting for transfers between devices  21.4 us (23%)
  starting transfers between devices  21.2 us (22%)
  local copies, waits for them, and re-layouts  7.42 us (8%)
  other arithmetic  2.25 us (2%)
    ppermute x9, waiting for transfers between devices, send_spec(): return lax.ppermute(value, 'spec', [(i, i ^ flip) for i in range(4)])  13.7 us
    pallas_call x3, Pallas kernels, pair_up(): pl.pallas_call(functools.partial(pair_body, tile, sizes), grid=(comps //...  12.7 us
    pallas_call x3, Pallas kernels, transfer(): pl.pallas_call(functools.partial(transfer_body, uses, strides, kept), out...  12.1 us
    ppermute x9, starting transfers between devices, send_spec(): return lax.ppermute(value, 'spec', [(i, i ^ flip) for i in range(4)])  10.2 us
    pallas_call x3, Pallas kernels, propagate(): pl.pallas_call(functools.partial(propagate_kernel, wanted, count), out_sh...  9.63 us
    pallas_call x1, Pallas kernels, finish(): pl.pallas_call(functools.partial(finish_body, len(kernels), first, groups...  7.3 us
    ppermute x1, waiting for transfers between devices, boundaries(): lax.ppermute(jnp.where(first, top, bottom), geo, pairs + [(j, i) for i, j...  5.94 us
    unnamed x26, local copies, waits for them, and re-layouts  4.57 us
  transfers between devices with their start and end apart: 18, of which 6 were waited for; matrix products, arithmetic and copies ran while one was open for 4% of the time, Pallas kernels for 36%

profile of v5, /device:TPU:1, one launch (start us, length us, event | category | flops | bytes accessed | tf_op | source)
XLA Modules:
  0.0 94.3 jit_solution(12543970495505438665)
XLA Ops:
  0.0 1.4 %dynamic-slice_bitcast_fusion.refs_0_ = bf16[324,1296]{1,0:T(8,128)(2,1)S(1)} fusion(bf16[1,1296,1296]{2,1,0:T(8,128)(2,1)} %param.17, s32[]{:T(128)S(6)} %select_n.81), kind=kLoop, calls=%fused_computation | loop fusion | bytes 1679620 | tf_op jit(solution)/shard_map/dynamic_slice | solution.py:374
  1.4 2.2 %collective-permute-start = (bf16[324,1296]{1,0:T(8,128)(2,1)S(1)}, bf16[324,1296]{1,0:T(8,128)(2,1)S(1)}, u32[]{:S(2)}, u32[]{:S(2)}) collective-permute-start(bf16[324,1296]{1,0:T(8,128)(2,1)S(1)} %dynamic-slice_bitcast_fusion.refs_0_), channel_id=1, source_target_pairs={{0,2},{2,4},{4,6},{6,0},{1,3},{3,5},{5,7},{7,1},{8,10},{10,12},{12... | collective-permute-start | bytes 2519432 | tf_op jit(solution)/shard_map/ppermute | solution.py:314
  3.6 0.1 compare_convert_fusion
  3.7 0.1 abs_multiply_fusion
  3.8 0.1 fusion.13
  3.9 0.1 copy.28.coef_ref
  4.1 0.0 copy-start.9
  4.1 0.0 copy-start.4
  4.1 1.7 %copy.32 = bf16[324,16,128]{2,0,1:T(8,128)(2,1)S(1)} copy(bf16[324,16,128]{2,1,0:T(8,128)(2,1)} %param.9) | data formatting | bytes 2654208 | tf_op args[0]
  5.8 0.0 copy-done.9
  5.8 3.9 %shard_map.91 = (bf16[336,768]{1,0:T(8,128)(2,1)}, f32[1,768]{1,0:T(1,128)S(1)}) custom-call(bf16[16,324,128]{2,1,0:T(8,128)(2,1)S(1)} %bitcast.83, bf16[324,128]{1,0:T(8,128)(2,1)S(1)} %broadcast_in_dim.2.west_ref.east_ref, bf16[324,128]{1,0:T(8,128)(2,1)S(1)} %broadcast_in_dim.2.west_ref.east_ref, f32[16,128]{1,0:T(8,128)S(1)} %get-tuple-element.97.sea_ref, ...), custom_call_target="tpu_custom_call" | custom-call | flops 497664 | bytes 248832 | tf_op jit(solution)/shard_map/pallas_call | solution.py:126
  9.7 1.2 %collective-permute-start.3 = (bf16[336,768]{1,0:T(8,128)(2,1)}, bf16[336,768]{1,0:T(8,128)(2,1)}, u32[]{:S(2)}, u32[]{:S(2)}) collective-permute-start(bf16[336,768]{1,0:T(8,128)(2,1)} %get-tuple-element.48.refs_0_.refs_14_), channel_id=1, source_target_pairs={{0,8},{8,0},{16,24},{24,16},{1,9},{9,1},{17,25},{25,17},{2,10},{10... | collective-permute-start | bytes 1548296 | tf_op jit(solution)/shard_map/ppermute | solution.py:357
  11.0 1.2 %collective-permute-start.4 = (bf16[336,768]{1,0:T(8,128)(2,1)}, bf16[336,768]{1,0:T(8,128)(2,1)}, u32[]{:S(2)}, u32[]{:S(2)}) collective-permute-start(bf16[336,768]{1,0:T(8,128)(2,1)} %get-tuple-element.48.refs_0_.refs_14_), channel_id=1, source_target_pairs={{0,16},{8,24},{16,0},{24,8},{1,17},{9,25},{17,1},{25,9},{2,18},{10... | collective-permute-start | bytes 1548296 | tf_op jit(solution)/shard_map/ppermute | solution.py:357
  12.2 0.7 broadcast_select_fusion.2
  12.9 1.5 %collective-permute-start.1 = (bf16[324,128]{1,0:T(8,128)(2,1)}, bf16[324,128]{1,0:T(8,128)(2,1)}, u32[]{:S(2)}, u32[]{:S(2)}) collective-permute-start(bf16[324,128]{1,0:T(8,128)(2,1)} %get-tuple-element.92), channel_id=1, source_target_pairs={{0,1},{1,0},{2,3},{3,2},{4,5},{5,4},{6,7},{7,6},{8,9},{9,8},{10,11... | collective-permute-start | bytes 248840 | tf_op jit(solution)/shard_map/ppermute | solution.py:326
  14.4 3.1 %collective-permute-start.2 = (bf16[324,128]{1,0:T(8,128)(2,1)}, bf16[324,128]{1,0:T(8,128)(2,1)}, u32[]{:S(2)}, u32[]{:S(2)}) collective-permute-start(bf16[324,128]{1,0:T(8,128)(2,1)} %get-tuple-element.91), channel_id=1, source_target_pairs={{1,2},{3,4},{5,6},{2,1},{4,3},{6,5},{9,10},{11,12},{13,14},{10,9},... | collective-permute-start | bytes 248840 | tf_op jit(solution)/shard_map/ppermute | solution.py:328
  17.5 3.1 %shard_map.92 = (bf16[336,768]{1,0:T(8,128)(2,1)S(1)}, f32[1,768]{1,0:T(1,128)S(1)}) custom-call(bf16[16,324,128]{2,1,0:T(8,128)(2,1)S(1)} %bitcast.84, bf16[324,128]{1,0:T(8,128)(2,1)S(1)} %broadcast_in_dim.2.west_ref.east_ref, bf16[324,128]{1,0:T(8,128)(2,1)S(1)} %broadcast_in_dim.2.west_ref.east_ref, f32[16,128]{1,0:T(8,128)S(1)} %get-tuple-element.97.sea_ref, ...), custom_call_target="tpu_custom_call" | custom-call | flops 497664 | bytes 248832 | tf_op jit(solution)/shard_map/pallas_call | solution.py:126
  20.6 0.8 copy-done.2
  21.4 0.0 collective-permute-done.1
  21.4 5.9 %collective-permute-done.2 = bf16[324,128]{1,0:T(8,128)(2,1)} collective-permute-done((bf16[324,128]{1,0:T(8,128)(2,1)}, bf16[324,128]{1,0:T(8,128)(2,1)}, u32[]{:S(2)}, u32[]{:S(2)}) %collective-permute-start.2) | collective-permute-done | bytes 82976 | tf_op jit(solution)/shard_map/ppermute | solution.py:328
  27.4 0.0 collective-permute-done.3.refs_1_
  27.4 0.0 collective-permute-done.4.refs_2_
  27.4 0.0 collective-permute-done.refs_2_
  27.4 1.3 %collective-permute-start.6 = (bf16[336,768]{1,0:T(8,128)(2,1)}, bf16[336,768]{1,0:T(8,128)(2,1)S(1)}, u32[]{:S(2)}, u32[]{:S(2)}) collective-permute-start(bf16[336,768]{1,0:T(8,128)(2,1)} %collective-permute-done.4.refs_2_), channel_id=1, source_target_pairs={{0,8},{8,0},{16,24},{24,16},{1,9},{9,1},{17,25},{25,17},{2,10},{10... | collective-permute-start | bytes 1548296 | tf_op jit(solution)/shard_map/ppermute | solution.py:357
  28.7 0.0 collective-permute-start.10
  28.7 0.5 collective-permute-start.11
  29.3 0.3 collective-permute-start.5
  29.5 1.2 %collective-permute-start.8 = (bf16[336,768]{1,0:T(8,128)(2,1)}, bf16[336,768]{1,0:T(8,128)(2,1)S(1)}, u32[]{:S(2)}, u32[]{:S(2)}) collective-permute-start(bf16[336,768]{1,0:T(8,128)(2,1)} %copy-done.2), channel_id=1, source_target_pairs={{0,16},{8,24},{16,0},{24,8},{1,17},{9,25},{17,1},{25,9},{2,18},{10... | collective-permute-start | bytes 1548296 | tf_op jit(solution)/shard_map/ppermute | solution.py:357
  30.8 1.0 %broadcast_select_fusion = (bf16[324,128]{1,0:T(8,128)(2,1)S(1)}, bf16[324,128]{1,0:T(8,128)(2,1)S(1)}) fusion(bf16[324,128]{1,0:T(8,128)(2,1)} %collective-permute-done.1, bf16[324,128]{1,0:T(8,128)(2,1)} %collective-permute-done.2, pred[]{:T(512)S(6)} %eq.6), kind=kLoop, calls=%fused_computation.5 | loop fusion | flops 82944 | bytes 331777 | tf_op jit(solution)/shard_map/jit(_where)/select_n | solution.py:336
  31.7 2.6 %shard_map.93 = (bf16[336,512]{1,0:T(8,128)(2,1)S(1)}, f32[1,512]{1,0:T(1,128)S(1)}) custom-call(bf16[16,324,128]{2,1,0:T(8,128)(2,1)S(1)} %bitcast.85, bf16[324,128]{1,0:T(8,128)(2,1)S(1)} %get-tuple-element.96.west_ref, bf16[324,128]{1,0:T(8,128)(2,1)S(1)} %get-tuple-element.95.east_ref, f32[16,128]{1,0:T(8,128)S(1)} %get-tuple-element.97.sea_ref, ...), custom_call_target="tpu_custom_call" | custom-call | flops 331776 | bytes 165888 | tf_op jit(solution)/shard_map/pallas_call | solution.py:126
  34.3 6.9 %collective-permute-done.6.refs_3_ = bf16[336,768]{1,0:T(8,128)(2,1)S(1)} collective-permute-done((bf16[336,768]{1,0:T(8,128)(2,1)}, bf16[336,768]{1,0:T(8,128)(2,1)S(1)}, u32[]{:S(2)}, u32[]{:S(2)}) %collective-permute-start.6) | collective-permute-done | bytes 516128 | tf_op jit(solution)/shard_map/ppermute | solution.py:357
  41.2 1.2 %collective-permute-start.7 = (bf16[336,768]{1,0:T(8,128)(2,1)S(1)}, bf16[336,768]{1,0:T(8,128)(2,1)S(1)}, u32[]{:S(2)}, u32[]{:S(2)}) collective-permute-start(bf16[336,768]{1,0:T(8,128)(2,1)S(1)} %copy-done.3), channel_id=1, source_target_pairs={{0,8},{8,0},{16,24},{24,16},{1,9},{9,1},{17,25},{25,17},{2,10},{10... | collective-permute-start | bytes 1548296 | tf_op jit(solution)/shard_map/ppermute | solution.py:357
  42.4 0.0 collective-permute-done.10.refs_1_
  42.4 1.3 %collective-permute-start.9 = (bf16[336,512]{1,0:T(8,128)(2,1)S(1)}, bf16[336,512]{1,0:T(8,128)(2,1)S(1)}, u32[]{:S(2)}, u32[]{:S(2)}) collective-permute-start(bf16[336,512]{1,0:T(8,128)(2,1)S(1)} %get-tuple-element.70.refs_0_.refs_16_), channel_id=1, source_target_pairs={{0,16},{8,24},{16,0},{24,8},{1,17},{9,25},{17,1},{25,9},{2,18},{10... | collective-permute-start | bytes 1032200 | tf_op jit(solution)/shard_map/ppermute | solution.py:357
  43.7 0.0 copy-start
  43.8 2.0 %copy-done = bf16[1296,1296]{1,0:T(8,128)(2,1)S(1)} copy-done((bf16[1296,1296]{1,0:T(8,128)(2,1)S(1)}, bf16[1296,1296]{1,0:T(8,128)(2,1)}, u32[]{:S(2)}) %copy-start) | copy-done | bytes 3359256
  45.8 5.6 %shard_map.94 = (bf16[1296,768]{1,0:T(8,128)(2,1)S(1)}, f32[1,768]{1,0:T(1,128)S(1)}) custom-call(s32[1]{0:T(128)} %bitcast.22.here_ref, bf16[336,768]{1,0:T(8,128)(2,1)} %get-tuple-element.48.refs_0_.refs_14_, bf16[336,768]{1,0:T(8,128)(2,1)} %collective-permute-done.3.refs_1_, bf16[336,768]{1,0:T(8,128)(2,1)} %collective-permute-done.4.refs_2_, ...), custom_call_target="tpu_custom_call" | custom-call | flops 322486272 | bytes 419904 | tf_op jit(solution)/shard_map/pallas_call | solution.py:185
  51.4 0.0 collective-permute-done.11.refs_3_
  51.4 0.0 collective-permute-done.9.refs_2_
  51.4 0.0 collective-permute-done.8.refs_2_
  51.4 1.7 %collective-permute-done.5.refs_4_ = bf16[324,1296]{1,0:T(8,128)(2,1)S(1)} collective-permute-done((bf16[324,1296]{1,0:T(8,128)(2,1)S(1)}, bf16[324,1296]{1,0:T(8,128)(2,1)S(1)}, u32[]{:S(2)}, u32[]{:S(2)}) %collective-permute-start.5) | collective-permute-done | bytes 839840 | tf_op jit(solution)/shard_map/ppermute | solution.py:314
  53.1 0.8 collective-permute-done.7.refs_1_
  53.9 1.5 %collective-permute-start.13 = (bf16[324,1296]{1,0:T(8,128)(2,1)S(1)}, bf16[324,1296]{1,0:T(8,128)(2,1)S(1)}, u32[]{:S(2)}, u32[]{:S(2)}) collective-permute-start(bf16[324,1296]{1,0:T(8,128)(2,1)S(1)} %collective-permute-done.5.refs_4_), channel_id=1, source_target_pairs={{0,1},{1,0},{2,3},{3,2},{4,5},{5,4},{6,7},{7,6},{8,9},{9,8},{10,11... | collective-permute-start | bytes 2519432 | tf_op jit(solution)/shard_map/ppermute | solution.py:344
  55.4 0.4 collective-permute-start.12
  55.8 1.2 %collective-permute-start.14 = (bf16[336,768]{1,0:T(8,128)(2,1)S(1)}, bf16[336,768]{1,0:T(8,128)(2,1)S(1)}, u32[]{:S(2)}, u32[]{:S(2)}) collective-permute-start(bf16[336,768]{1,0:T(8,128)(2,1)S(1)} %collective-permute-done.7.refs_1_), channel_id=1, source_target_pairs={{0,16},{8,24},{16,0},{24,8},{1,17},{9,25},{17,1},{25,9},{2,18},{10... | collective-permute-start | bytes 1548296 | tf_op jit(solution)/shard_map/ppermute | solution.py:357
  57.0 1.3 %collective-permute-start.16 = (bf16[336,512]{1,0:T(8,128)(2,1)S(1)}, bf16[336,512]{1,0:T(8,128)(2,1)S(1)}, u32[]{:S(2)}, u32[]{:S(2)}) collective-permute-start(bf16[336,512]{1,0:T(8,128)(2,1)S(1)} %collective-permute-done.9.refs_2_), channel_id=1, source_target_pairs={{0,8},{8,0},{16,24},{24,16},{1,9},{9,1},{17,25},{25,17},{2,10},{10... | collective-permute-start | bytes 1032200 | tf_op jit(solution)/shard_map/ppermute | solution.py:357
  58.3 0.3 collective-permute-start.15
  58.6 0.1 convert_reduce_fusion.2
  58.7 0.1 convert_reduce_fusion
  58.8 0.1 pad_add_fusion.1.bounds_ref
  58.9 0.0 collective-permute-done.13.refs_5_
  58.9 4.3 %shard_map.95 = (bf16[324,768]{1,0:T(8,128)(2,1)S(1)}, f32[8,128]{1,0:T(8,128)S(1)}) custom-call(s32[27]{0:T(128)S(1)} %pad_add_fusion.1.bounds_ref, bf16[324,1296]{1,0:T(8,128)(2,1)S(1)} %dynamic-slice_bitcast_fusion.refs_0_, bf16[324,1296]{1,0:T(8,128)(2,1)S(1)} %collective-permute-done.10.refs_1_, bf16[324,1296]{1,0:T(8,128)(2,1)S(1)} %collective-permute-done.refs_2_, ...), custom_call_target="tpu_custom_call" | custom-call | flops 241864704 | bytes 878688 | tf_op jit(solution)/shard_map/pallas_call | solution.py:242
  63.2 5.6 %collective-permute-done.14.refs_3_ = bf16[336,768]{1,0:T(8,128)(2,1)S(1)} collective-permute-done((bf16[336,768]{1,0:T(8,128)(2,1)S(1)}, bf16[336,768]{1,0:T(8,128)(2,1)S(1)}, u32[]{:S(2)}, u32[]{:S(2)}) %collective-permute-start.14) | collective-permute-done | bytes 516128 | tf_op jit(solution)/shard_map/ppermute | solution.py:357
  68.8 4.2 %shard_map.96 = (bf16[1296,768]{1,0:T(8,128)(2,1)S(1)}, f32[1,768]{1,0:T(1,128)S(1)}) custom-call(s32[1]{0:T(128)} %bitcast.22.here_ref, bf16[336,768]{1,0:T(8,128)(2,1)S(1)} %copy-done.3, bf16[336,768]{1,0:T(8,128)(2,1)S(1)} %collective-permute-done.7.refs_1_, bf16[336,768]{1,0:T(8,128)(2,1)S(1)} %collective-permute-done.8.refs_2_, ...), custom_call_target="tpu_custom_call" | custom-call | flops 322486272 | bytes 419904 | tf_op jit(solution)/shard_map/pallas_call | solution.py:185
  73.1 0.0 collective-permute-done.16.refs_3_
  73.1 0.4 collective-permute-done.15.refs_1_
  73.5 2.9 %shard_map.98 = (bf16[1296,512]{1,0:T(8,128)(2,1)S(1)}, f32[1,512]{1,0:T(1,128)S(1)}) custom-call(s32[1]{0:T(128)} %bitcast.22.here_ref, bf16[336,512]{1,0:T(8,128)(2,1)S(1)} %get-tuple-element.70.refs_0_.refs_16_, bf16[336,512]{1,0:T(8,128)(2,1)S(1)} %collective-permute-done.15.refs_1_, bf16[336,512]{1,0:T(8,128)(2,1)S(1)} %collective-permute-done.9.refs_2_, ...), custom_call_target="tpu_custom_call" | custom-call | flops 214990848 | bytes 419904 | tf_op jit(solution)/shard_map/pallas_call | solution.py:185
  76.4 4.1 %shard_map.97 = (bf16[324,768]{1,0:T(8,128)(2,1)S(1)}, f32[8,128]{1,0:T(8,128)S(1)}) custom-call(s32[27]{0:T(128)S(1)} %pad_add_fusion.1.bounds_ref, bf16[324,1296]{1,0:T(8,128)(2,1)S(1)} %dynamic-slice_bitcast_fusion.refs_0_, bf16[324,1296]{1,0:T(8,128)(2,1)S(1)} %collective-permute-done.10.refs_1_, bf16[324,1296]{1,0:T(8,128)(2,1)S(1)} %collective-permute-done.refs_2_, ...), custom_call_target="tpu_custom_call" | custom-call | flops 241864704 | bytes 878688 | tf_op jit(solution)/shard_map/pallas_call | solution.py:242
  80.6 0.0 collective-permute-done.12.refs_0_
  80.6 1.5 %collective-permute-start.17 = (bf16[324,1296]{1,0:T(8,128)(2,1)S(1)}, bf16[324,1296]{1,0:T(8,128)(2,1)S(1)}, u32[]{:S(2)}, u32[]{:S(2)}) collective-permute-start(bf16[324,1296]{1,0:T(8,128)(2,1)S(1)} %collective-permute-done.12.refs_0_), channel_id=1, source_target_pairs={{0,1},{1,0},{2,3},{3,2},{4,5},{5,4},{6,7},{7,6},{8,9},{9,8},{10,11... | collective-permute-start | bytes 2519432 | tf_op jit(solution)/shard_map/ppermute | solution.py:344
  82.1 3.6 %shard_map.99 = (bf16[324,512]{1,0:T(8,128)(2,1)S(1)}, f32[8,128]{1,0:T(8,128)S(1)}) custom-call(s32[27]{0:T(128)S(1)} %pad_add_fusion.1.bounds_ref, bf16[324,1296]{1,0:T(8,128)(2,1)S(1)} %dynamic-slice_bitcast_fusion.refs_0_, bf16[324,1296]{1,0:T(8,128)(2,1)S(1)} %collective-permute-done.10.refs_1_, bf16[324,1296]{1,0:T(8,128)(2,1)S(1)} %collective-permute-done.refs_2_, ...), custom_call_target="tpu_custom_call" | custom-call | flops 161243136 | bytes 795744 | tf_op jit(solution)/shard_map/pallas_call | solution.py:242
  85.7 0.0 collective-permute-done.17.refs_1_
  85.7 7.3 %shard_map.100 = bf16[16,324,128]{2,1,0:T(8,128)(2,1)S(1)} custom-call(s32[27]{0:T(128)S(1)} %pad_add_fusion.1.bounds_ref, f32[324,6]{1,0:T(8,128)S(1)} %copy.28.coef_ref, s32[16,128]{1,0:T(8,128)S(1)} %copy-done.5, bf16[16,128]{1,0:T(8,128)(2,1)S(1)} %copy-done.6, bf16[16,128]{1,0:T(8,128)(2,1)S(1)} %copy-done.7, ...), custom_call_target="tpu_custom_call" | custom-call | flops 214990848 | bytes 873504 | tf_op jit(solution)/shard_map/pallas_call | solution.py:302
  93.0 1.2 %copy.29 = bf16[324,16,128]{2,1,0:T(8,128)(2,1)} copy(bf16[324,16,128]{2,0,1:T(8,128)(2,1)S(1)} %bitcast.86) | data formatting | bytes 2654208 | tf_op jit(solution)/shard_map/transpose | solution.py:492
  (31 shorter events, 0.2 us)
Async XLA Ops:
  0.0 3.8 %copy-start.8 = (s32[16,128]{1,0:T(8,128)S(1)}, s32[16,128]{1,0:T(8,128)}, u32[]{:S(2)}) copy-start(s32[16,128]{1,0:T(8,128)} %param.15) | copy-start | bytes 24580
  1.4 26.0 %collective-permute-start = (bf16[324,1296]{1,0:T(8,128)(2,1)S(1)}, bf16[324,1296]{1,0:T(8,128)(2,1)S(1)}, u32[]{:S(2)}, u32[]{:S(2)}) collective-permute-start(bf16[324,1296]{1,0:T(8,128)(2,1)S(1)} %dynamic-slice_bitcast_fusion.refs_0_), channel_id=1, source_target_pairs={{0,2},{2,4},{4,6},{6,0},{1,3},{3,5},{5,7},{7,1},{8,10},{10,12},{12... | collective-permute-start | bytes 2519432 | tf_op jit(solution)/shard_map/ppermute | solution.py:314
  4.1 1.7 %copy-start.9 = (s32[16,128]{1,0:T(8,128)S(1)}, s32[16,128]{1,0:T(8,128)}, u32[]{:S(2)}) copy-start(s32[16,128]{1,0:T(8,128)} %param.10) | copy-start | bytes 24580
  4.1 1.7 %copy-start.4 = (f32[16,128]{1,0:T(8,128)S(1)}, f32[16,128]{1,0:T(8,128)}, u32[]{:S(2)}) copy-start(f32[16,128]{1,0:T(8,128)} %depth_ref.5) | copy-start | bytes 24580
  9.7 17.6 %collective-permute-start.3 = (bf16[336,768]{1,0:T(8,128)(2,1)}, bf16[336,768]{1,0:T(8,128)(2,1)}, u32[]{:S(2)}, u32[]{:S(2)}) collective-permute-start(bf16[336,768]{1,0:T(8,128)(2,1)} %get-tuple-element.48.refs_0_.refs_14_), channel_id=1, source_target_pairs={{0,8},{8,0},{16,24},{24,16},{1,9},{9,1},{17,25},{25,17},{2,10},{10... | collective-permute-start | bytes 1548296 | tf_op jit(solution)/shard_map/ppermute | solution.py:357
  11.0 16.4 %collective-permute-start.4 = (bf16[336,768]{1,0:T(8,128)(2,1)}, bf16[336,768]{1,0:T(8,128)(2,1)}, u32[]{:S(2)}, u32[]{:S(2)}) collective-permute-start(bf16[336,768]{1,0:T(8,128)(2,1)} %get-tuple-element.48.refs_0_.refs_14_), channel_id=1, source_target_pairs={{0,16},{8,24},{16,0},{24,8},{1,17},{9,25},{17,1},{25,9},{2,18},{10... | collective-permute-start | bytes 1548296 | tf_op jit(solution)/shard_map/ppermute | solution.py:357
  12.9 8.5 %collective-permute-start.1 = (bf16[324,128]{1,0:T(8,128)(2,1)}, bf16[324,128]{1,0:T(8,128)(2,1)}, u32[]{:S(2)}, u32[]{:S(2)}) collective-permute-start(bf16[324,128]{1,0:T(8,128)(2,1)} %get-tuple-element.92), channel_id=1, source_target_pairs={{0,1},{1,0},{2,3},{3,2},{4,5},{5,4},{6,7},{7,6},{8,9},{9,8},{10,11... | collective-permute-start | bytes 248840 | tf_op jit(solution)/shard_map/ppermute | solution.py:326
  14.4 13.0 %collective-permute-start.2 = (bf16[324,128]{1,0:T(8,128)(2,1)}, bf16[324,128]{1,0:T(8,128)(2,1)}, u32[]{:S(2)}, u32[]{:S(2)}) collective-permute-start(bf16[324,128]{1,0:T(8,128)(2,1)} %get-tuple-element.91), channel_id=1, source_target_pairs={{1,2},{3,4},{5,6},{2,1},{4,3},{6,5},{9,10},{11,12},{13,14},{10,9},... | collective-permute-start | bytes 248840 | tf_op jit(solution)/shard_map/ppermute | solution.py:328
  20.6 0.8 copy-start.2
  21.4 19.8 %copy-start.3 = (bf16[336,768]{1,0:T(8,128)(2,1)S(1)}, bf16[336,768]{1,0:T(8,128)(2,1)}, u32[]{:S(2)}) copy-start(bf16[336,768]{1,0:T(8,128)(2,1)} %copy-done.2) | copy-start | bytes 1548292
  27.4 13.8 %collective-permute-start.6 = (bf16[336,768]{1,0:T(8,128)(2,1)}, bf16[336,768]{1,0:T(8,128)(2,1)S(1)}, u32[]{:S(2)}, u32[]{:S(2)}) collective-permute-start(bf16[336,768]{1,0:T(8,128)(2,1)} %collective-permute-done.4.refs_2_), channel_id=1, source_target_pairs={{0,8},{8,0},{16,24},{24,16},{1,9},{9,1},{17,25},{25,17},{2,10},{10... | collective-permute-start | bytes 1548296 | tf_op jit(solution)/shard_map/ppermute | solution.py:357
  28.7 13.8 %collective-permute-start.10 = (bf16[324,1296]{1,0:T(8,128)(2,1)S(1)}, bf16[324,1296]{1,0:T(8,128)(2,1)S(1)}, u32[]{:S(2)}, u32[]{:S(2)}) collective-permute-start(bf16[324,1296]{1,0:T(8,128)(2,1)S(1)} %dynamic-slice_bitcast_fusion.refs_0_), channel_id=1, source_target_pairs={{0,1},{1,0},{2,3},{3,2},{4,5},{5,4},{6,7},{7,6},{8,9},{9,8},{10,11... | collective-permute-start | bytes 2519432 | tf_op jit(solution)/shard_map/ppermute | solution.py:344
  28.7 22.7 %collective-permute-start.11 = (bf16[324,1296]{1,0:T(8,128)(2,1)S(1)}, bf16[324,1296]{1,0:T(8,128)(2,1)S(1)}, u32[]{:S(2)}, u32[]{:S(2)}) collective-permute-start(bf16[324,1296]{1,0:T(8,128)(2,1)S(1)} %collective-permute-done.refs_2_), channel_id=1, source_target_pairs={{0,1},{1,0},{2,3},{3,2},{4,5},{5,4},{6,7},{7,6},{8,9},{9,8},{10,11... | collective-permute-start | bytes 2519432 | tf_op jit(solution)/shard_map/ppermute | solution.py:344
  29.3 23.8 %collective-permute-start.5 = (bf16[324,1296]{1,0:T(8,128)(2,1)S(1)}, bf16[324,1296]{1,0:T(8,128)(2,1)S(1)}, u32[]{:S(2)}, u32[]{:S(2)}) collective-permute-start(bf16[324,1296]{1,0:T(8,128)(2,1)S(1)} %collective-permute-done.refs_2_), channel_id=1, source_target_pairs={{0,2},{2,4},{4,6},{6,0},{1,3},{3,5},{5,7},{7,1},{8,10},{10,12},{12... | collective-permute-start | bytes 2519432 | tf_op jit(solution)/shard_map/ppermute | solution.py:314
  29.5 21.9 %collective-permute-start.8 = (bf16[336,768]{1,0:T(8,128)(2,1)}, bf16[336,768]{1,0:T(8,128)(2,1)S(1)}, u32[]{:S(2)}, u32[]{:S(2)}) collective-permute-start(bf16[336,768]{1,0:T(8,128)(2,1)} %copy-done.2), channel_id=1, source_target_pairs={{0,16},{8,24},{16,0},{24,8},{1,17},{9,25},{17,1},{25,9},{2,18},{10... | collective-permute-start | bytes 1548296 | tf_op jit(solution)/shard_map/ppermute | solution.py:357
  41.2 12.7 %collective-permute-start.7 = (bf16[336,768]{1,0:T(8,128)(2,1)S(1)}, bf16[336,768]{1,0:T(8,128)(2,1)S(1)}, u32[]{:S(2)}, u32[]{:S(2)}) collective-permute-start(bf16[336,768]{1,0:T(8,128)(2,1)S(1)} %copy-done.3), channel_id=1, source_target_pairs={{0,8},{8,0},{16,24},{24,16},{1,9},{9,1},{17,25},{25,17},{2,10},{10... | collective-permute-start | bytes 1548296 | tf_op jit(solution)/shard_map/ppermute | solution.py:357
  42.4 9.0 %collective-permute-start.9 = (bf16[336,512]{1,0:T(8,128)(2,1)S(1)}, bf16[336,512]{1,0:T(8,128)(2,1)S(1)}, u32[]{:S(2)}, u32[]{:S(2)}) collective-permute-start(bf16[336,512]{1,0:T(8,128)(2,1)S(1)} %get-tuple-element.70.refs_0_.refs_16_), channel_id=1, source_target_pairs={{0,16},{8,24},{16,0},{24,8},{1,17},{9,25},{17,1},{25,9},{2,18},{10... | collective-permute-start | bytes 1032200 | tf_op jit(solution)/shard_map/ppermute | solution.py:357
  43.7 2.0 %copy-start = (bf16[1296,1296]{1,0:T(8,128)(2,1)S(1)}, bf16[1296,1296]{1,0:T(8,128)(2,1)}, u32[]{:S(2)}) copy-start(bf16[1296,1296]{1,0:T(8,128)(2,1)} %refs_4_.5) | copy-start | bytes 10077700
  53.9 5.0 %collective-permute-start.13 = (bf16[324,1296]{1,0:T(8,128)(2,1)S(1)}, bf16[324,1296]{1,0:T(8,128)(2,1)S(1)}, u32[]{:S(2)}, u32[]{:S(2)}) collective-permute-start(bf16[324,1296]{1,0:T(8,128)(2,1)S(1)} %collective-permute-done.5.refs_4_), channel_id=1, source_target_pairs={{0,1},{1,0},{2,3},{3,2},{4,5},{5,4},{6,7},{7,6},{8,9},{9,8},{10,11... | collective-permute-start | bytes 2519432 | tf_op jit(solution)/shard_map/ppermute | solution.py:344
  55.4 25.2 %collective-permute-start.12 = (bf16[324,1296]{1,0:T(8,128)(2,1)S(1)}, bf16[324,1296]{1,0:T(8,128)(2,1)S(1)}, u32[]{:S(2)}, u32[]{:S(2)}) collective-permute-start(bf16[324,1296]{1,0:T(8,128)(2,1)S(1)} %collective-permute-done.5.refs_4_), channel_id=1, source_target_pairs={{0,2},{2,4},{4,6},{6,0},{1,3},{3,5},{5,7},{7,1},{8,10},{10,12},{12... | collective-permute-start | bytes 2519432 | tf_op jit(solution)/shard_map/ppermute | solution.py:314
  55.8 13.1 %collective-permute-start.14 = (bf16[336,768]{1,0:T(8,128)(2,1)S(1)}, bf16[336,768]{1,0:T(8,128)(2,1)S(1)}, u32[]{:S(2)}, u32[]{:S(2)}) collective-permute-start(bf16[336,768]{1,0:T(8,128)(2,1)S(1)} %collective-permute-done.7.refs_1_), channel_id=1, source_target_pairs={{0,16},{8,24},{16,0},{24,8},{1,17},{9,25},{17,1},{25,9},{2,18},{10... | collective-permute-start | bytes 1548296 | tf_op jit(solution)/shard_map/ppermute | solution.py:357
  57.0 16.0 %collective-permute-start.16 = (bf16[336,512]{1,0:T(8,128)(2,1)S(1)}, bf16[336,512]{1,0:T(8,128)(2,1)S(1)}, u32[]{:S(2)}, u32[]{:S(2)}) collective-permute-start(bf16[336,512]{1,0:T(8,128)(2,1)S(1)} %collective-permute-done.9.refs_2_), channel_id=1, source_target_pairs={{0,8},{8,0},{16,24},{24,16},{1,9},{9,1},{17,25},{25,17},{2,10},{10... | collective-permute-start | bytes 1032200 | tf_op jit(solution)/shard_map/ppermute | solution.py:357
  58.3 15.2 %collective-permute-start.15 = (bf16[336,512]{1,0:T(8,128)(2,1)S(1)}, bf16[336,512]{1,0:T(8,128)(2,1)S(1)}, u32[]{:S(2)}, u32[]{:S(2)}) collective-permute-start(bf16[336,512]{1,0:T(8,128)(2,1)S(1)} %get-tuple-element.70.refs_0_.refs_16_), channel_id=1, source_target_pairs={{0,8},{8,0},{16,24},{24,16},{1,9},{9,1},{17,25},{25,17},{2,10},{10... | collective-permute-start | bytes 1032200 | tf_op jit(solution)/shard_map/ppermute | solution.py:357
  58.9 9.9 %copy-start.1 = (bf16[1296,1296]{1,0:T(8,128)(2,1)S(1)}, bf16[1296,1296]{1,0:T(8,128)(2,1)}, u32[]{:S(2)}) copy-start(bf16[1296,1296]{1,0:T(8,128)(2,1)} %refs_4_.5) | copy-start | bytes 10077700
  80.6 5.1 %collective-permute-start.17 = (bf16[324,1296]{1,0:T(8,128)(2,1)S(1)}, bf16[324,1296]{1,0:T(8,128)(2,1)S(1)}, u32[]{:S(2)}, u32[]{:S(2)}) collective-permute-start(bf16[324,1296]{1,0:T(8,128)(2,1)S(1)} %collective-permute-done.12.refs_0_), channel_id=1, source_target_pairs={{0,1},{1,0},{2,3},{3,2},{4,5},{5,4},{6,7},{7,6},{8,9},{9,8},{10,11... | collective-permute-start | bytes 2519432 | tf_op jit(solution)/shard_map/ppermute | solution.py:344
  82.0 3.7 %copy-start.5 = (s32[16,128]{1,0:T(8,128)S(1)}, s32[16,128]{1,0:T(8,128)}, u32[]{:S(2)}) copy-start(s32[16,128]{1,0:T(8,128)} %ice_ref.1) | copy-start | bytes 24580
  82.0 3.7 %copy-start.6 = (bf16[16,128]{1,0:T(8,128)(2,1)S(1)}, bf16[16,128]{1,0:T(8,128)(2,1)}, u32[]{:S(2)}) copy-start(bf16[16,128]{1,0:T(8,128)(2,1)} %speed_ref.1) | copy-start | bytes 12292
  82.1 3.7 %copy-start.7 = (bf16[16,128]{1,0:T(8,128)(2,1)S(1)}, bf16[16,128]{1,0:T(8,128)(2,1)}, u32[]{:S(2)}) copy-start(bf16[16,128]{1,0:T(8,128)(2,1)} %angle_ref.1) | copy-start | bytes 12292

commit v6 on v5

--- a/solution.py
+++ b/solution.py
@@ -116,7 +116,7 @@
         tile(slice(whole * SUB, comps), comps - whole * SUB)
     place = places_of(cells_of(rank_ref, wanted), count)
     place_ref[...] = place
-    sorted_ref[...] = put_in_order(out_ref[...], moves(place)).astype(BF16)
+    sorted_ref[...] = put_in_order(out_ref[...], moves(place))[:comps].astype(BF16)
 
 
 def propagate(wanted, count, x, west, east, sea, depth, coef, rank_map):
@@ -126,7 +126,7 @@
     return pl.pallas_call(
         functools.partial(propagate_kernel, wanted, count),
         out_shape=[
-            jax.ShapeDtypeStruct((padded, cells), BF16),
+            jax.ShapeDtypeStruct((comps, cells), BF16),
             jax.ShapeDtypeStruct((1, cells), F32),
         ],
         in_specs=[VMEM] * 7,
@@ -259,16 +259,39 @@
     return held, mark
 
 
+def wind_body(groups, ice_ref, speed_ref, angle_ref, *refs):
+    places, outs = split(refs, len(groups), len(groups))
+    maps = [speed_ref[...].astype(F32), angle_ref[...].astype(F32), ice_ref[...].astype(F32)]
+    for rows, place, out_ref in zip(groups, places, outs):
+        given = [cells_of(values, rows) for values in maps]
+        given = jnp.concatenate(given + [jnp.zeros_like(given[0])] * 5, axis=0)
+        given = put_in_order(given.astype(BF16), moves(place[...]))
+        speed, angle, frozen = 0.3 * given[0:1], given[1:2], given[2:3]
+        rest = [jnp.zeros_like(frozen)] * 5
+        rows_out = [speed * jnp.cos(angle), speed * jnp.sin(angle), frozen] + rest
+        out_ref[...] = jnp.concatenate(rows_out, axis=0)
+
+
+def wind(groups, maps, places):
+    return pl.pallas_call(
+        functools.partial(wind_body, groups),
+        out_shape=[jax.ShapeDtypeStruct((8, place.shape[1]), F32) for place in places],
+        in_specs=[VMEM] * (len(maps) + len(places)),
+        out_specs=[VMEM] * len(places),
+        compiler_params=params(12),
+        cost_estimate=pl.CostEstimate(flops=0, bytes_accessed=0, transcendentals=0),
+    )(*maps, *places)
+
+
 def finish_body(
-    count, first, groups, strides, bounds_ref, coef_ref, ice_ref, speed_ref, angle_ref, *refs
+    count, first, groups, strides, bounds_ref, coef_ref, *refs
 ):
     chunks = len(groups)
-    kernels, places, totals, paired, held, parts = split(
-        refs, count, chunks, chunks, chunks, chunks, chunks
+    kernels, places, winds, totals, paired, held, parts = split(
+        refs, count, chunks, chunks, chunks, chunks, chunks, chunks
     )
     out_ref, *works = refs[len(refs) - 1 - chunks :]
     comps, width = out_ref.shape[1:]
-    maps = [speed_ref[...].astype(F32), angle_ref[...].astype(F32), ice_ref[...].astype(F32)]
     cosine, sine = coef_ref[:, 4:5], coef_ref[:, 5:6]
     for chunk, rows in enumerate(groups):
         work = works[chunk]
@@ -276,29 +299,25 @@
         which = [(first + k, k) for k in range(count)]
         apply_ranks(bounds_ref, strides[chunk], which, paired[chunk], kernels, work)
         matrix = moves(places[chunk][...])
-        given = [cells_of(values, rows) for values in maps]
-        given = jnp.concatenate(given + [jnp.zeros_like(given[0])] * 5, axis=0)
-        given = put_in_order(given.astype(BF16), matrix)
-        speed, angle, frozen = 0.3 * given[0:1], given[1:2], given[2:3] > 0.5
-        along, across = speed * jnp.cos(angle), speed * jnp.sin(angle)
+        along, across, frozen = (winds[chunk][i : i + 1, :] for i in range(3))
         total = totals[chunk][...]
         shrink = 1.0 / (1.0 + total)
         base = 1.0 - 0.5 * total * shrink
         energy = parts[chunk][:comps, :].astype(F32)
         forcing = jnp.maximum(cosine * along + sine * across, 0.0)
         result = energy * (base + forcing) + (0.2 * shrink) * work[...].astype(F32)
-        result = jnp.where(frozen, energy, result).astype(BF16)
+        result = jnp.where(frozen > 0.5, energy, result).astype(BF16)
         result = jnp.dot(result, matrix, preferred_element_type=F32).astype(BF16)
         for k, row in enumerate(rows):
             out_ref[row] = result[:, k * width : (k + 1) * width]
 
 
 def finish(
-    kernels, first, groups, strides, bounds, coef, maps, places, totals, paired, held, parts, marks
+    kernels, first, groups, width, strides, bounds, coef, places, winds, totals, paired, held, parts, marks
 ):
     comps = kernels[0].shape[0]
-    rows, width = maps[0].shape
-    operands = [coef, *maps, *kernels, *places, *totals, *paired, *held, *parts]
+    rows = sum(place.shape[1] for place in places) // width
+    operands = [coef, *kernels, *places, *winds, *totals, *paired, *held, *parts]
     return pl.pallas_call(
         functools.partial(finish_body, len(kernels), first, groups, strides),
         out_shape=jax.ShapeDtypeStruct((rows, comps, width), BF16),
@@ -446,8 +465,9 @@
     found = with_partners(own_now) + with_partners(one_back)
     marks = [value[:8, :128] for value in (found[1], found[count + 1])]
     pair_group(0, crossed)
-    two_back, near[1], second, sent, totals, marks = lax.optimization_barrier(
-        (two_back, near[1], second, part, totals, marks)
+    winds = wind(groups, [ice_mask, wind_speed, wind_dir], places)
+    two_back, near[1], second, sent, totals, winds, marks = lax.optimization_barrier(
+        (two_back, near[1], second, part, totals, winds, marks)
     )
 
     three_back = next_plane(two_back)
@@ -473,16 +493,16 @@
     if last[:-2]:
         held, _ = transfer_all(last[:-2], 3 * count, strides, bounds, paired, held)
     last = last[-2:]
-    maps = [ice_mask, wind_speed, wind_dir]
     out = finish(
         last,
         owners - len(last),
         groups,
+        width,
         strides,
         bounds,
         coef,
-        maps,
         places,
+        winds,
         totals,
         paired,
         held,

time: 94.6 us -> 92.7 us (0.980)
  waiting for transfers between devices: 21.4 us -> 19.4 us
    ppermute x9, waiting for transfers between devices: 13.7 us -> 12.6 us  [send_spec(): return lax.ppermute(value, 'spec', [(i, i ^ flip) for i in range(4)])]
    pallas_call x0 -> x1, Pallas kernels: none -> 1.02 us  [wind(): pl.pallas_call(functools.partial(wind_body, groups), out_shape=[jax.Shape...]
    pallas_call x1, Pallas kernels: 7.3 us -> 6.3 us  [finish(): pl.pallas_call(functools.partial(finish_body, len(kernels), first, groups...]
  transfers between devices with their start and end apart: 18 -> 18, of which waited for: 6 -> 6; matrix products, arithmetic and copies ran while one was open for 4% -> 5% of each run, Pallas kernels for 36% -> 38%
where the time goes in v6:
time: 92.7 us; the launch traced here: 92.4 us
  Pallas kernels  41.8 us (45%)
  starting transfers between devices  21.2 us (23%)
  waiting for transfers between devices  19.4 us (21%)
  local copies, waits for them, and re-layouts  7.41 us (8%)
  other arithmetic  2.25 us (2%)
    pallas_call x3, Pallas kernels, pair_up(): pl.pallas_call(functools.partial(pair_body, tile, sizes), grid=(comps //...  12.7 us
    ppermute x9, waiting for transfers between devices, send_spec(): return lax.ppermute(value, 'spec', [(i, i ^ flip) for i in range(4)])  12.6 us
    pallas_call x3, Pallas kernels, transfer(): pl.pallas_call(functools.partial(transfer_body, uses, strides, kept), out...  12.1 us
    ppermute x9, starting transfers between devices, send_spec(): return lax.ppermute(value, 'spec', [(i, i ^ flip) for i in range(4)])  10.2 us
    pallas_call x3, Pallas kernels, propagate(): pl.pallas_call(functools.partial(propagate_kernel, wanted, count), out_sh...  9.63 us
    pallas_call x1, Pallas kernels, finish(): pl.pallas_call(functools.partial(finish_body, len(kernels), first, groups...  6.3 us
    ppermute x1, waiting for transfers between devices, boundaries(): lax.ppermute(jnp.where(first, top, bottom), geo, pairs + [(j, i) for i, j...  5.93 us
    unnamed x26, local copies, waits for them, and re-layouts  4.55 us
  transfers between devices with their start and end apart: 18, of which 6 were waited for; matrix products, arithmetic and copies ran while one was open for 5% of the time, Pallas kernels for 38%

profile of v6, /device:TPU:1, one launch (start us, length us, event | category | flops | bytes accessed | tf_op | source)
XLA Modules:
  0.0 92.4 jit_solution(5239211101515336812)
XLA Ops:
  0.0 1.4 %dynamic-slice_bitcast_fusion.refs_0_ = bf16[324,1296]{1,0:T(8,128)(2,1)S(1)} fusion(bf16[1,1296,1296]{2,1,0:T(8,128)(2,1)} %param.17, s32[]{:T(128)S(6)} %select_n.81), kind=kLoop, calls=%fused_computation | loop fusion | bytes 1679620 | tf_op jit(solution)/shard_map/dynamic_slice | solution.py:393
  1.4 2.2 %collective-permute-start = (bf16[324,1296]{1,0:T(8,128)(2,1)S(1)}, bf16[324,1296]{1,0:T(8,128)(2,1)S(1)}, u32[]{:S(2)}, u32[]{:S(2)}) collective-permute-start(bf16[324,1296]{1,0:T(8,128)(2,1)S(1)} %dynamic-slice_bitcast_fusion.refs_0_), channel_id=1, source_target_pairs={{0,2},{2,4},{4,6},{6,0},{1,3},{3,5},{5,7},{7,1},{8,10},{10,12},{12... | collective-permute-start | bytes 2519432 | tf_op jit(solution)/shard_map/ppermute | solution.py:333
  3.6 0.1 compare_convert_fusion
  3.7 0.1 abs_multiply_fusion
  3.8 0.1 fusion.13
  3.9 0.1 copy.28.coef_ref
  4.1 0.0 copy-start.9
  4.1 0.0 copy-start.4
  4.1 1.7 %copy.32 = bf16[324,16,128]{2,0,1:T(8,128)(2,1)S(1)} copy(bf16[324,16,128]{2,1,0:T(8,128)(2,1)} %param.9) | data formatting | bytes 2654208 | tf_op args[0]
  5.8 3.9 %shard_map.91 = (bf16[324,768]{1,0:T(8,128)(2,1)}, f32[1,768]{1,0:T(1,128)S(1)}) custom-call(bf16[16,324,128]{2,1,0:T(8,128)(2,1)S(1)} %bitcast.83, bf16[324,128]{1,0:T(8,128)(2,1)S(1)} %broadcast_in_dim.2.west_ref.east_ref, bf16[324,128]{1,0:T(8,128)(2,1)S(1)} %broadcast_in_dim.2.west_ref.east_ref, f32[16,128]{1,0:T(8,128)S(1)} %get-tuple-element.109.sea_ref, ...), custom_call_target="tpu_custom_call" | custom-call | flops 497664 | bytes 248832 | tf_op jit(solution)/shard_map/pallas_call | solution.py:126
  9.7 1.2 %collective-permute-start.3 = (bf16[324,768]{1,0:T(8,128)(2,1)}, bf16[324,768]{1,0:T(8,128)(2,1)}, u32[]{:S(2)}, u32[]{:S(2)}) collective-permute-start(bf16[324,768]{1,0:T(8,128)(2,1)} %get-tuple-element.54.refs_0_.refs_17_), channel_id=1, source_target_pairs={{0,8},{8,0},{16,24},{24,16},{1,9},{9,1},{17,25},{25,17},{2,10},{10... | collective-permute-start | bytes 1493000 | tf_op jit(solution)/shard_map/ppermute | solution.py:376
  11.0 1.2 %collective-permute-start.4 = (bf16[324,768]{1,0:T(8,128)(2,1)}, bf16[324,768]{1,0:T(8,128)(2,1)}, u32[]{:S(2)}, u32[]{:S(2)}) collective-permute-start(bf16[324,768]{1,0:T(8,128)(2,1)} %get-tuple-element.54.refs_0_.refs_17_), channel_id=1, source_target_pairs={{0,16},{8,24},{16,0},{24,8},{1,17},{9,25},{17,1},{25,9},{2,18},{10... | collective-permute-start | bytes 1493000 | tf_op jit(solution)/shard_map/ppermute | solution.py:376
  12.2 0.7 broadcast_select_fusion.2
  12.9 1.5 %collective-permute-start.1 = (bf16[324,128]{1,0:T(8,128)(2,1)}, bf16[324,128]{1,0:T(8,128)(2,1)}, u32[]{:S(2)}, u32[]{:S(2)}) collective-permute-start(bf16[324,128]{1,0:T(8,128)(2,1)} %get-tuple-element.104), channel_id=1, source_target_pairs={{0,1},{1,0},{2,3},{3,2},{4,5},{5,4},{6,7},{7,6},{8,9},{9,8},{10,11... | collective-permute-start | bytes 248840 | tf_op jit(solution)/shard_map/ppermute | solution.py:345
  14.4 3.1 %collective-permute-start.2 = (bf16[324,128]{1,0:T(8,128)(2,1)}, bf16[324,128]{1,0:T(8,128)(2,1)}, u32[]{:S(2)}, u32[]{:S(2)}) collective-permute-start(bf16[324,128]{1,0:T(8,128)(2,1)} %get-tuple-element.103), channel_id=1, source_target_pairs={{1,2},{3,4},{5,6},{2,1},{4,3},{6,5},{9,10},{11,12},{13,14},{10,9},... | collective-permute-start | bytes 248840 | tf_op jit(solution)/shard_map/ppermute | solution.py:347
  17.5 3.1 %shard_map.92 = (bf16[324,768]{1,0:T(8,128)(2,1)S(1)}, f32[1,768]{1,0:T(1,128)S(1)}) custom-call(bf16[16,324,128]{2,1,0:T(8,128)(2,1)S(1)} %bitcast.84, bf16[324,128]{1,0:T(8,128)(2,1)S(1)} %broadcast_in_dim.2.west_ref.east_ref, bf16[324,128]{1,0:T(8,128)(2,1)S(1)} %broadcast_in_dim.2.west_ref.east_ref, f32[16,128]{1,0:T(8,128)S(1)} %get-tuple-element.109.sea_ref, ...), custom_call_target="tpu_custom_call" | custom-call | flops 497664 | bytes 248832 | tf_op jit(solution)/shard_map/pallas_call | solution.py:126
  20.6 0.8 copy-done.2
  21.4 0.0 collective-permute-done.1
  21.4 5.9 %collective-permute-done.2 = bf16[324,128]{1,0:T(8,128)(2,1)} collective-permute-done((bf16[324,128]{1,0:T(8,128)(2,1)}, bf16[324,128]{1,0:T(8,128)(2,1)}, u32[]{:S(2)}, u32[]{:S(2)}) %collective-permute-start.2) | collective-permute-done | bytes 82976 | tf_op jit(solution)/shard_map/ppermute | solution.py:347
  27.4 0.0 collective-permute-done.3.refs_1_
  27.4 0.0 collective-permute-done.4.refs_2_
  27.4 0.0 collective-permute-done.refs_2_
  27.4 1.3 %collective-permute-start.6 = (bf16[324,768]{1,0:T(8,128)(2,1)}, bf16[324,768]{1,0:T(8,128)(2,1)S(1)}, u32[]{:S(2)}, u32[]{:S(2)}) collective-permute-start(bf16[324,768]{1,0:T(8,128)(2,1)} %collective-permute-done.4.refs_2_), channel_id=1, source_target_pairs={{0,8},{8,0},{16,24},{24,16},{1,9},{9,1},{17,25},{25,17},{2,10},{10... | collective-permute-start | bytes 1493000 | tf_op jit(solution)/shard_map/ppermute | solution.py:376
  28.7 0.0 collective-permute-start.10
  28.7 0.5 collective-permute-start.11
  29.3 0.3 collective-permute-start.5
  29.5 1.2 %collective-permute-start.8 = (bf16[324,768]{1,0:T(8,128)(2,1)}, bf16[324,768]{1,0:T(8,128)(2,1)S(1)}, u32[]{:S(2)}, u32[]{:S(2)}) collective-permute-start(bf16[324,768]{1,0:T(8,128)(2,1)} %copy-done.2), channel_id=1, source_target_pairs={{0,16},{8,24},{16,0},{24,8},{1,17},{9,25},{17,1},{25,9},{2,18},{10... | collective-permute-start | bytes 1493000 | tf_op jit(solution)/shard_map/ppermute | solution.py:376
  30.8 1.0 %broadcast_select_fusion = (bf16[324,128]{1,0:T(8,128)(2,1)S(1)}, bf16[324,128]{1,0:T(8,128)(2,1)S(1)}) fusion(bf16[324,128]{1,0:T(8,128)(2,1)} %collective-permute-done.1, bf16[324,128]{1,0:T(8,128)(2,1)} %collective-permute-done.2, pred[]{:T(512)S(6)} %eq.6), kind=kLoop, calls=%fused_computation.5 | loop fusion | flops 82944 | bytes 331777 | tf_op jit(solution)/shard_map/jit(_where)/select_n | solution.py:355
  31.7 2.6 %shard_map.93 = (bf16[324,512]{1,0:T(8,128)(2,1)S(1)}, f32[1,512]{1,0:T(1,128)S(1)}) custom-call(bf16[16,324,128]{2,1,0:T(8,128)(2,1)S(1)} %bitcast.85, bf16[324,128]{1,0:T(8,128)(2,1)S(1)} %get-tuple-element.108.west_ref, bf16[324,128]{1,0:T(8,128)(2,1)S(1)} %get-tuple-element.107.east_ref, f32[16,128]{1,0:T(8,128)S(1)} %get-tuple-element.109.sea_ref, ...), custom_call_target="tpu_custom_call" | custom-call | flops 331776 | bytes 165888 | tf_op jit(solution)/shard_map/pallas_call | solution.py:126
  34.3 6.6 %collective-permute-done.6.refs_3_ = bf16[324,768]{1,0:T(8,128)(2,1)S(1)} collective-permute-done((bf16[324,768]{1,0:T(8,128)(2,1)}, bf16[324,768]{1,0:T(8,128)(2,1)S(1)}, u32[]{:S(2)}, u32[]{:S(2)}) %collective-permute-start.6) | collective-permute-done | bytes 497696 | tf_op jit(solution)/shard_map/ppermute | solution.py:376
  40.9 1.2 %collective-permute-start.7 = (bf16[324,768]{1,0:T(8,128)(2,1)S(1)}, bf16[324,768]{1,0:T(8,128)(2,1)S(1)}, u32[]{:S(2)}, u32[]{:S(2)}) collective-permute-start(bf16[324,768]{1,0:T(8,128)(2,1)S(1)} %copy-done.3), channel_id=1, source_target_pairs={{0,8},{8,0},{16,24},{24,16},{1,9},{9,1},{17,25},{25,17},{2,10},{10... | collective-permute-start | bytes 1493000 | tf_op jit(solution)/shard_map/ppermute | solution.py:376
  42.2 0.0 collective-permute-done.10.refs_1_
  42.2 1.3 %collective-permute-start.9 = (bf16[324,512]{1,0:T(8,128)(2,1)S(1)}, bf16[324,512]{1,0:T(8,128)(2,1)S(1)}, u32[]{:S(2)}, u32[]{:S(2)}) collective-permute-start(bf16[324,512]{1,0:T(8,128)(2,1)S(1)} %get-tuple-element.82.refs_0_.refs_19_), channel_id=1, source_target_pairs={{0,16},{8,24},{16,0},{24,8},{1,17},{9,25},{17,1},{25,9},{2,18},{10... | collective-permute-start | bytes 995336 | tf_op jit(solution)/shard_map/ppermute | solution.py:376
  43.5 1.0 %shard_map.95 = (f32[8,768]{1,0:T(8,128)S(1)}, f32[8,768]{1,0:T(8,128)S(1)}, f32[8,512]{1,0:T(8,128)S(1)}) custom-call(s32[16,128]{1,0:T(8,128)S(1)} %copy-done.5, bf16[16,128]{1,0:T(8,128)(2,1)S(1)} %copy-done.6, bf16[16,128]{1,0:T(8,128)(2,1)S(1)} %copy-done.7, f32[1,768]{1,0:T(1,128)S(1)} %get-tuple-element.67.refs_0_.refs_2_, ...), custom_call_target="tpu_custom_call" | custom-call | tf_op jit(solution)/shard_map/pallas_call | solution.py:276
  44.5 0.0 copy-start
  44.6 2.0 %copy-done = bf16[1296,1296]{1,0:T(8,128)(2,1)S(1)} copy-done((bf16[1296,1296]{1,0:T(8,128)(2,1)S(1)}, bf16[1296,1296]{1,0:T(8,128)(2,1)}, u32[]{:S(2)}) %copy-start) | copy-done | bytes 3359256
  46.6 5.6 %shard_map.94 = (bf16[1296,768]{1,0:T(8,128)(2,1)S(1)}, f32[1,768]{1,0:T(1,128)S(1)}) custom-call(s32[1]{0:T(128)} %bitcast.22.here_ref, bf16[324,768]{1,0:T(8,128)(2,1)} %get-tuple-element.54.refs_0_.refs_17_, bf16[324,768]{1,0:T(8,128)(2,1)} %collective-permute-done.3.refs_1_, bf16[324,768]{1,0:T(8,128)(2,1)} %collective-permute-done.4.refs_2_, ...), custom_call_target="tpu_custom_call" | custom-call | flops 322486272 | bytes 419904 | tf_op jit(solution)/shard_map/pallas_call | solution.py:185
  52.2 0.0 collective-permute-done.11.refs_3_
  52.2 0.0 collective-permute-done.9.refs_2_
  52.2 0.0 collective-permute-done.8.refs_2_
  52.2 0.9 collective-permute-done.5.refs_4_
  53.1 0.2 collective-permute-done.7.refs_1_
  53.4 1.5 %collective-permute-start.13 = (bf16[324,1296]{1,0:T(8,128)(2,1)S(1)}, bf16[324,1296]{1,0:T(8,128)(2,1)S(1)}, u32[]{:S(2)}, u32[]{:S(2)}) collective-permute-start(bf16[324,1296]{1,0:T(8,128)(2,1)S(1)} %collective-permute-done.5.refs_4_), channel_id=1, source_target_pairs={{0,1},{1,0},{2,3},{3,2},{4,5},{5,4},{6,7},{7,6},{8,9},{9,8},{10,11... | collective-permute-start | bytes 2519432 | tf_op jit(solution)/shard_map/ppermute | solution.py:363
  54.8 0.4 collective-permute-start.12
  55.2 1.2 %collective-permute-start.14 = (bf16[324,768]{1,0:T(8,128)(2,1)S(1)}, bf16[324,768]{1,0:T(8,128)(2,1)S(1)}, u32[]{:S(2)}, u32[]{:S(2)}) collective-permute-start(bf16[324,768]{1,0:T(8,128)(2,1)S(1)} %collective-permute-done.7.refs_1_), channel_id=1, source_target_pairs={{0,16},{8,24},{16,0},{24,8},{1,17},{9,25},{17,1},{25,9},{2,18},{10... | collective-permute-start | bytes 1493000 | tf_op jit(solution)/shard_map/ppermute | solution.py:376
  56.5 1.3 %collective-permute-start.16 = (bf16[324,512]{1,0:T(8,128)(2,1)S(1)}, bf16[324,512]{1,0:T(8,128)(2,1)S(1)}, u32[]{:S(2)}, u32[]{:S(2)}) collective-permute-start(bf16[324,512]{1,0:T(8,128)(2,1)S(1)} %collective-permute-done.9.refs_2_), channel_id=1, source_target_pairs={{0,8},{8,0},{16,24},{24,16},{1,9},{9,1},{17,25},{25,17},{2,10},{10... | collective-permute-start | bytes 995336 | tf_op jit(solution)/shard_map/ppermute | solution.py:376
  57.8 0.3 collective-permute-start.15
  58.0 0.1 convert_reduce_fusion.2
  58.1 0.1 convert_reduce_fusion
  58.3 0.1 pad_add_fusion.1.bounds_ref
  58.4 0.0 collective-permute-done.13.refs_5_
  58.4 4.3 %shard_map.96 = (bf16[324,768]{1,0:T(8,128)(2,1)S(1)}, f32[8,128]{1,0:T(8,128)S(1)}) custom-call(s32[27]{0:T(128)S(1)} %pad_add_fusion.1.bounds_ref, bf16[324,1296]{1,0:T(8,128)(2,1)S(1)} %dynamic-slice_bitcast_fusion.refs_0_, bf16[324,1296]{1,0:T(8,128)(2,1)S(1)} %collective-permute-done.10.refs_1_, bf16[324,1296]{1,0:T(8,128)(2,1)S(1)} %collective-permute-done.refs_2_, ...), custom_call_target="tpu_custom_call" | custom-call | flops 241864704 | bytes 878688 | tf_op jit(solution)/shard_map/pallas_call | solution.py:242
  62.7 5.3 %collective-permute-done.14.refs_3_ = bf16[324,768]{1,0:T(8,128)(2,1)S(1)} collective-permute-done((bf16[324,768]{1,0:T(8,128)(2,1)S(1)}, bf16[324,768]{1,0:T(8,128)(2,1)S(1)}, u32[]{:S(2)}, u32[]{:S(2)}) %collective-permute-start.14) | collective-permute-done | bytes 497696 | tf_op jit(solution)/shard_map/ppermute | solution.py:376
  68.0 4.2 %shard_map.97 = (bf16[1296,768]{1,0:T(8,128)(2,1)S(1)}, f32[1,768]{1,0:T(1,128)S(1)}) custom-call(s32[1]{0:T(128)} %bitcast.22.here_ref, bf16[324,768]{1,0:T(8,128)(2,1)S(1)} %copy-done.3, bf16[324,768]{1,0:T(8,128)(2,1)S(1)} %collective-permute-done.7.refs_1_, bf16[324,768]{1,0:T(8,128)(2,1)S(1)} %collective-permute-done.8.refs_2_, ...), custom_call_target="tpu_custom_call" | custom-call | flops 322486272 | bytes 419904 | tf_op jit(solution)/shard_map/pallas_call | solution.py:185
  72.3 0.0 collective-permute-done.16.refs_3_
  72.3 0.3 collective-permute-done.15.refs_1_
  72.6 2.9 %shard_map.99 = (bf16[1296,512]{1,0:T(8,128)(2,1)S(1)}, f32[1,512]{1,0:T(1,128)S(1)}) custom-call(s32[1]{0:T(128)} %bitcast.22.here_ref, bf16[324,512]{1,0:T(8,128)(2,1)S(1)} %get-tuple-element.82.refs_0_.refs_19_, bf16[324,512]{1,0:T(8,128)(2,1)S(1)} %collective-permute-done.15.refs_1_, bf16[324,512]{1,0:T(8,128)(2,1)S(1)} %collective-permute-done.9.refs_2_, ...), custom_call_target="tpu_custom_call" | custom-call | flops 214990848 | bytes 419904 | tf_op jit(solution)/shard_map/pallas_call | solution.py:185
  75.6 4.1 %shard_map.98 = (bf16[324,768]{1,0:T(8,128)(2,1)S(1)}, f32[8,128]{1,0:T(8,128)S(1)}) custom-call(s32[27]{0:T(128)S(1)} %pad_add_fusion.1.bounds_ref, bf16[324,1296]{1,0:T(8,128)(2,1)S(1)} %dynamic-slice_bitcast_fusion.refs_0_, bf16[324,1296]{1,0:T(8,128)(2,1)S(1)} %collective-permute-done.10.refs_1_, bf16[324,1296]{1,0:T(8,128)(2,1)S(1)} %collective-permute-done.refs_2_, ...), custom_call_target="tpu_custom_call" | custom-call | flops 241864704 | bytes 878688 | tf_op jit(solution)/shard_map/pallas_call | solution.py:242
  79.7 0.0 collective-permute-done.12.refs_0_
  79.7 1.5 %collective-permute-start.17 = (bf16[324,1296]{1,0:T(8,128)(2,1)S(1)}, bf16[324,1296]{1,0:T(8,128)(2,1)S(1)}, u32[]{:S(2)}, u32[]{:S(2)}) collective-permute-start(bf16[324,1296]{1,0:T(8,128)(2,1)S(1)} %collective-permute-done.12.refs_0_), channel_id=1, source_target_pairs={{0,1},{1,0},{2,3},{3,2},{4,5},{5,4},{6,7},{7,6},{8,9},{9,8},{10,11... | collective-permute-start | bytes 2519432 | tf_op jit(solution)/shard_map/ppermute | solution.py:363
  81.2 3.6 %shard_map.100 = (bf16[324,512]{1,0:T(8,128)(2,1)S(1)}, f32[8,128]{1,0:T(8,128)S(1)}) custom-call(s32[27]{0:T(128)S(1)} %pad_add_fusion.1.bounds_ref, bf16[324,1296]{1,0:T(8,128)(2,1)S(1)} %dynamic-slice_bitcast_fusion.refs_0_, bf16[324,1296]{1,0:T(8,128)(2,1)S(1)} %collective-permute-done.10.refs_1_, bf16[324,1296]{1,0:T(8,128)(2,1)S(1)} %collective-permute-done.refs_2_, ...), custom_call_target="tpu_custom_call" | custom-call | flops 161243136 | bytes 795744 | tf_op jit(solution)/shard_map/pallas_call | solution.py:242
  84.8 0.0 collective-permute-done.17.refs_1_
  84.8 6.3 %shard_map.101 = bf16[16,324,128]{2,1,0:T(8,128)(2,1)S(1)} custom-call(s32[27]{0:T(128)S(1)} %pad_add_fusion.1.bounds_ref, f32[324,6]{1,0:T(8,128)S(1)} %copy.28.coef_ref, bf16[324,1296]{1,0:T(8,128)(2,1)S(1)} %collective-permute-done.12.refs_0_, bf16[324,1296]{1,0:T(8,128)(2,1)S(1)} %collective-permute-done.17.refs_1_, ...), custom_call_target="tpu_custom_call" | custom-call | flops 214990848 | bytes 873504 | tf_op jit(solution)/shard_map/pallas_call | solution.py:321
  91.2 1.2 %copy.29 = bf16[324,16,128]{2,1,0:T(8,128)(2,1)} copy(bf16[324,16,128]{2,0,1:T(8,128)(2,1)S(1)} %bitcast.86) | data formatting | bytes 2654208 | tf_op jit(solution)/shard_map/transpose | solution.py:512
  (32 shorter events, 0.2 us)
Async XLA Ops:
  0.0 3.8 %copy-start.8 = (s32[16,128]{1,0:T(8,128)S(1)}, s32[16,128]{1,0:T(8,128)}, u32[]{:S(2)}) copy-start(s32[16,128]{1,0:T(8,128)} %param.15) | copy-start | bytes 24580
  1.4 26.0 %collective-permute-start = (bf16[324,1296]{1,0:T(8,128)(2,1)S(1)}, bf16[324,1296]{1,0:T(8,128)(2,1)S(1)}, u32[]{:S(2)}, u32[]{:S(2)}) collective-permute-start(bf16[324,1296]{1,0:T(8,128)(2,1)S(1)} %dynamic-slice_bitcast_fusion.refs_0_), channel_id=1, source_target_pairs={{0,2},{2,4},{4,6},{6,0},{1,3},{3,5},{5,7},{7,1},{8,10},{10,12},{12... | collective-permute-start | bytes 2519432 | tf_op jit(solution)/shard_map/ppermute | solution.py:333
  4.1 1.7 %copy-start.9 = (s32[16,128]{1,0:T(8,128)S(1)}, s32[16,128]{1,0:T(8,128)}, u32[]{:S(2)}) copy-start(s32[16,128]{1,0:T(8,128)} %param.10) | copy-start | bytes 24580
  4.1 1.7 %copy-start.4 = (f32[16,128]{1,0:T(8,128)S(1)}, f32[16,128]{1,0:T(8,128)}, u32[]{:S(2)}) copy-start(f32[16,128]{1,0:T(8,128)} %depth_ref.5) | copy-start | bytes 24580
  9.7 17.6 %collective-permute-start.3 = (bf16[324,768]{1,0:T(8,128)(2,1)}, bf16[324,768]{1,0:T(8,128)(2,1)}, u32[]{:S(2)}, u32[]{:S(2)}) collective-permute-start(bf16[324,768]{1,0:T(8,128)(2,1)} %get-tuple-element.54.refs_0_.refs_17_), channel_id=1, source_target_pairs={{0,8},{8,0},{16,24},{24,16},{1,9},{9,1},{17,25},{25,17},{2,10},{10... | collective-permute-start | bytes 1493000 | tf_op jit(solution)/shard_map/ppermute | solution.py:376
  11.0 16.4 %collective-permute-start.4 = (bf16[324,768]{1,0:T(8,128)(2,1)}, bf16[324,768]{1,0:T(8,128)(2,1)}, u32[]{:S(2)}, u32[]{:S(2)}) collective-permute-start(bf16[324,768]{1,0:T(8,128)(2,1)} %get-tuple-element.54.refs_0_.refs_17_), channel_id=1, source_target_pairs={{0,16},{8,24},{16,0},{24,8},{1,17},{9,25},{17,1},{25,9},{2,18},{10... | collective-permute-start | bytes 1493000 | tf_op jit(solution)/shard_map/ppermute | solution.py:376
  12.9 8.5 %collective-permute-start.1 = (bf16[324,128]{1,0:T(8,128)(2,1)}, bf16[324,128]{1,0:T(8,128)(2,1)}, u32[]{:S(2)}, u32[]{:S(2)}) collective-permute-start(bf16[324,128]{1,0:T(8,128)(2,1)} %get-tuple-element.104), channel_id=1, source_target_pairs={{0,1},{1,0},{2,3},{3,2},{4,5},{5,4},{6,7},{7,6},{8,9},{9,8},{10,11... | collective-permute-start | bytes 248840 | tf_op jit(solution)/shard_map/ppermute | solution.py:345
  14.4 13.0 %collective-permute-start.2 = (bf16[324,128]{1,0:T(8,128)(2,1)}, bf16[324,128]{1,0:T(8,128)(2,1)}, u32[]{:S(2)}, u32[]{:S(2)}) collective-permute-start(bf16[324,128]{1,0:T(8,128)(2,1)} %get-tuple-element.103), channel_id=1, source_target_pairs={{1,2},{3,4},{5,6},{2,1},{4,3},{6,5},{9,10},{11,12},{13,14},{10,9},... | collective-permute-start | bytes 248840 | tf_op jit(solution)/shard_map/ppermute | solution.py:347
  20.6 0.8 copy-start.2
  21.4 22.1 %copy-start.5 = (s32[16,128]{1,0:T(8,128)S(1)}, s32[16,128]{1,0:T(8,128)}, u32[]{:S(2)}) copy-start(s32[16,128]{1,0:T(8,128)} %ice_ref.1) | copy-start | bytes 24580
  21.4 22.1 %copy-start.6 = (bf16[16,128]{1,0:T(8,128)(2,1)S(1)}, bf16[16,128]{1,0:T(8,128)(2,1)}, u32[]{:S(2)}) copy-start(bf16[16,128]{1,0:T(8,128)(2,1)} %speed_ref.1) | copy-start | bytes 12292
  21.4 22.1 %copy-start.7 = (bf16[16,128]{1,0:T(8,128)(2,1)S(1)}, bf16[16,128]{1,0:T(8,128)(2,1)}, u32[]{:S(2)}) copy-start(bf16[16,128]{1,0:T(8,128)(2,1)} %angle_ref.1) | copy-start | bytes 12292
  21.4 19.5 %copy-start.3 = (bf16[324,768]{1,0:T(8,128)(2,1)S(1)}, bf16[324,768]{1,0:T(8,128)(2,1)}, u32[]{:S(2)}) copy-start(bf16[324,768]{1,0:T(8,128)(2,1)} %copy-done.2) | copy-start | bytes 1492996
  27.4 13.6 %collective-permute-start.6 = (bf16[324,768]{1,0:T(8,128)(2,1)}, bf16[324,768]{1,0:T(8,128)(2,1)S(1)}, u32[]{:S(2)}, u32[]{:S(2)}) collective-permute-start(bf16[324,768]{1,0:T(8,128)(2,1)} %collective-permute-done.4.refs_2_), channel_id=1, source_target_pairs={{0,8},{8,0},{16,24},{24,16},{1,9},{9,1},{17,25},{25,17},{2,10},{10... | collective-permute-start | bytes 1493000 | tf_op jit(solution)/shard_map/ppermute | solution.py:376
  28.7 13.5 %collective-permute-start.10 = (bf16[324,1296]{1,0:T(8,128)(2,1)S(1)}, bf16[324,1296]{1,0:T(8,128)(2,1)S(1)}, u32[]{:S(2)}, u32[]{:S(2)}) collective-permute-start(bf16[324,1296]{1,0:T(8,128)(2,1)S(1)} %dynamic-slice_bitcast_fusion.refs_0_), channel_id=1, source_target_pairs={{0,1},{1,0},{2,3},{3,2},{4,5},{5,4},{6,7},{7,6},{8,9},{9,8},{10,11... | collective-permute-start | bytes 2519432 | tf_op jit(solution)/shard_map/ppermute | solution.py:363
  28.7 23.4 %collective-permute-start.11 = (bf16[324,1296]{1,0:T(8,128)(2,1)S(1)}, bf16[324,1296]{1,0:T(8,128)(2,1)S(1)}, u32[]{:S(2)}, u32[]{:S(2)}) collective-permute-start(bf16[324,1296]{1,0:T(8,128)(2,1)S(1)} %collective-permute-done.refs_2_), channel_id=1, source_target_pairs={{0,1},{1,0},{2,3},{3,2},{4,5},{5,4},{6,7},{7,6},{8,9},{9,8},{10,11... | collective-permute-start | bytes 2519432 | tf_op jit(solution)/shard_map/ppermute | solution.py:363
  29.3 23.8 %collective-permute-start.5 = (bf16[324,1296]{1,0:T(8,128)(2,1)S(1)}, bf16[324,1296]{1,0:T(8,128)(2,1)S(1)}, u32[]{:S(2)}, u32[]{:S(2)}) collective-permute-start(bf16[324,1296]{1,0:T(8,128)(2,1)S(1)} %collective-permute-done.refs_2_), channel_id=1, source_target_pairs={{0,2},{2,4},{4,6},{6,0},{1,3},{3,5},{5,7},{7,1},{8,10},{10,12},{12... | collective-permute-start | bytes 2519432 | tf_op jit(solution)/shard_map/ppermute | solution.py:333
  29.5 22.7 %collective-permute-start.8 = (bf16[324,768]{1,0:T(8,128)(2,1)}, bf16[324,768]{1,0:T(8,128)(2,1)S(1)}, u32[]{:S(2)}, u32[]{:S(2)}) collective-permute-start(bf16[324,768]{1,0:T(8,128)(2,1)} %copy-done.2), channel_id=1, source_target_pairs={{0,16},{8,24},{16,0},{24,8},{1,17},{9,25},{17,1},{25,9},{2,18},{10... | collective-permute-start | bytes 1493000 | tf_op jit(solution)/shard_map/ppermute | solution.py:376
  40.9 12.4 %collective-permute-start.7 = (bf16[324,768]{1,0:T(8,128)(2,1)S(1)}, bf16[324,768]{1,0:T(8,128)(2,1)S(1)}, u32[]{:S(2)}, u32[]{:S(2)}) collective-permute-start(bf16[324,768]{1,0:T(8,128)(2,1)S(1)} %copy-done.3), channel_id=1, source_target_pairs={{0,8},{8,0},{16,24},{24,16},{1,9},{9,1},{17,25},{25,17},{2,10},{10... | collective-permute-start | bytes 1493000 | tf_op jit(solution)/shard_map/ppermute | solution.py:376
  42.2 10.0 %collective-permute-start.9 = (bf16[324,512]{1,0:T(8,128)(2,1)S(1)}, bf16[324,512]{1,0:T(8,128)(2,1)S(1)}, u32[]{:S(2)}, u32[]{:S(2)}) collective-permute-start(bf16[324,512]{1,0:T(8,128)(2,1)S(1)} %get-tuple-element.82.refs_0_.refs_19_), channel_id=1, source_target_pairs={{0,16},{8,24},{16,0},{24,8},{1,17},{9,25},{17,1},{25,9},{2,18},{10... | collective-permute-start | bytes 995336 | tf_op jit(solution)/shard_map/ppermute | solution.py:376
  44.5 2.0 %copy-start = (bf16[1296,1296]{1,0:T(8,128)(2,1)S(1)}, bf16[1296,1296]{1,0:T(8,128)(2,1)}, u32[]{:S(2)}) copy-start(bf16[1296,1296]{1,0:T(8,128)(2,1)} %refs_4_.5) | copy-start | bytes 10077700
  53.4 5.0 %collective-permute-start.13 = (bf16[324,1296]{1,0:T(8,128)(2,1)S(1)}, bf16[324,1296]{1,0:T(8,128)(2,1)S(1)}, u32[]{:S(2)}, u32[]{:S(2)}) collective-permute-start(bf16[324,1296]{1,0:T(8,128)(2,1)S(1)} %collective-permute-done.5.refs_4_), channel_id=1, source_target_pairs={{0,1},{1,0},{2,3},{3,2},{4,5},{5,4},{6,7},{7,6},{8,9},{9,8},{10,11... | collective-permute-start | bytes 2519432 | tf_op jit(solution)/shard_map/ppermute | solution.py:363
  54.8 24.9 %collective-permute-start.12 = (bf16[324,1296]{1,0:T(8,128)(2,1)S(1)}, bf16[324,1296]{1,0:T(8,128)(2,1)S(1)}, u32[]{:S(2)}, u32[]{:S(2)}) collective-permute-start(bf16[324,1296]{1,0:T(8,128)(2,1)S(1)} %collective-permute-done.5.refs_4_), channel_id=1, source_target_pairs={{0,2},{2,4},{4,6},{6,0},{1,3},{3,5},{5,7},{7,1},{8,10},{10,12},{12... | collective-permute-start | bytes 2519432 | tf_op jit(solution)/shard_map/ppermute | solution.py:333
  55.2 12.8 %collective-permute-start.14 = (bf16[324,768]{1,0:T(8,128)(2,1)S(1)}, bf16[324,768]{1,0:T(8,128)(2,1)S(1)}, u32[]{:S(2)}, u32[]{:S(2)}) collective-permute-start(bf16[324,768]{1,0:T(8,128)(2,1)S(1)} %collective-permute-done.7.refs_1_), channel_id=1, source_target_pairs={{0,16},{8,24},{16,0},{24,8},{1,17},{9,25},{17,1},{25,9},{2,18},{10... | collective-permute-start | bytes 1493000 | tf_op jit(solution)/shard_map/ppermute | solution.py:376
  56.5 15.8 %collective-permute-start.16 = (bf16[324,512]{1,0:T(8,128)(2,1)S(1)}, bf16[324,512]{1,0:T(8,128)(2,1)S(1)}, u32[]{:S(2)}, u32[]{:S(2)}) collective-permute-start(bf16[324,512]{1,0:T(8,128)(2,1)S(1)} %collective-permute-done.9.refs_2_), channel_id=1, source_target_pairs={{0,8},{8,0},{16,24},{24,16},{1,9},{9,1},{17,25},{25,17},{2,10},{10... | collective-permute-start | bytes 995336 | tf_op jit(solution)/shard_map/ppermute | solution.py:376
  57.8 14.9 %collective-permute-start.15 = (bf16[324,512]{1,0:T(8,128)(2,1)S(1)}, bf16[324,512]{1,0:T(8,128)(2,1)S(1)}, u32[]{:S(2)}, u32[]{:S(2)}) collective-permute-start(bf16[324,512]{1,0:T(8,128)(2,1)S(1)} %get-tuple-element.82.refs_0_.refs_19_), channel_id=1, source_target_pairs={{0,8},{8,0},{16,24},{24,16},{1,9},{9,1},{17,25},{25,17},{2,10},{10... | collective-permute-start | bytes 995336 | tf_op jit(solution)/shard_map/ppermute | solution.py:376
  58.4 9.7 %copy-start.1 = (bf16[1296,1296]{1,0:T(8,128)(2,1)S(1)}, bf16[1296,1296]{1,0:T(8,128)(2,1)}, u32[]{:S(2)}) copy-start(bf16[1296,1296]{1,0:T(8,128)(2,1)} %refs_4_.5) | copy-start | bytes 10077700
  79.7 5.1 %collective-permute-start.17 = (bf16[324,1296]{1,0:T(8,128)(2,1)S(1)}, bf16[324,1296]{1,0:T(8,128)(2,1)S(1)}, u32[]{:S(2)}, u32[]{:S(2)}) collective-permute-start(bf16[324,1296]{1,0:T(8,128)(2,1)S(1)} %collective-permute-done.12.refs_0_), channel_id=1, source_target_pairs={{0,1},{1,0},{2,3},{3,2},{4,5},{5,4},{6,7},{7,6},{8,9},{9,8},{10,11... | collective-permute-start | bytes 2519432 | tf_op jit(solution)/shard_map/ppermute | solution.py:363

commit v7 on v6

--- a/solution.py
+++ b/solution.py
@@ -165,13 +165,15 @@
                         at = (here ^ flip) * some
                         whole[at : at + some, :] = piece[:some, :]
 
-        for total, whole in zip(totals, wholes):
-            total[...] = jnp.sum(whole[...].astype(F32), axis=0, keepdims=True) / comps
-
-    for out_ref, whole in zip(paired, wholes):
+        for total in totals:
+            total[...] = jnp.zeros(total.shape, F32)
+
+    for out_ref, total, whole in zip(paired, totals, wholes):
         coupled = jnp.dot(pair_ref[...], whole[...], preferred_element_type=F32)
         own = whole[pl.ds(pl.multiple_of(step * tile, SUB), tile), :]
-        out_ref[...] = (own.astype(F32) * coupled).astype(BF16)
+        own = own.astype(F32)
+        total[...] += jnp.sum(own, axis=0, keepdims=True) / comps
+        out_ref[...] = (own * coupled).astype(BF16)
 
 
 def pair_up(here, groups, pair, tile=432):
@@ -480,12 +482,12 @@
     crossed, mark = lax.optimization_barrier((crossed, mark))
     marks.append(mark)
     pair_group(1, crossed)
-    last_cross, totals[1] = lax.optimization_barrier((last_cross, totals[1]))
-    pair_group(2, last_cross)
     more, mark = transfer_all(some, 0, strides[1:2], bounds, paired[1:2], [None])
     held += more
-    three_back, mark, totals[2] = lax.optimization_barrier((three_back, mark, totals[2]))
+    last_cross, mark = lax.optimization_barrier((last_cross, mark))
     marks.append(mark)
+    pair_group(2, last_cross)
+    three_back, totals[2] = lax.optimization_barrier((three_back, totals[2]))
     last = with_partners(three_back)
     more, mark = transfer_all(some, 0, strides[2:], bounds, paired[2:], [None])
     held += more

time: 92.7 us -> 91.8 us (level)
  Pallas kernels: 41.8 us -> 40.8 us
    ppermute x1, starting transfers between devices: 3.08 us -> 4.59 us  [boundaries(): lax.ppermute(jnp.where(first, top, bottom), geo, pairs + [(j, i) for i, j...]
    ppermute x1, starting transfers between devices: 1.51 us -> 0.07 us  [boundaries(): lax.ppermute(jnp.where(first, bottom, top), 'place', [(0, 1), (1, 0)])]
  transfers between devices with their start and end apart: 18 -> 18, of which waited for: 6 -> 6; matrix products, arithmetic and copies ran while one was open for 5% -> 5% of each run, Pallas kernels for 38% -> 37%
where the time goes in v7:
time: 91.8 us; the launch traced here: 91.6 us
  Pallas kernels  40.8 us (44%)
  starting transfers between devices  20.6 us (22%)
  waiting for transfers between devices  20.2 us (22%)
  local copies, waits for them, and re-layouts  7.41 us (8%)
  other arithmetic  2.25 us (2%)
    ppermute x9, waiting for transfers between devices, send_spec(): return lax.ppermute(value, 'spec', [(i, i ^ flip) for i in range(4)])  12.7 us
    pallas_call x3, Pallas kernels, pair_up(): pl.pallas_call(functools.partial(pair_body, tile, sizes), grid=(comps //...  11.9 us
    pallas_call x3, Pallas kernels, transfer(): pl.pallas_call(functools.partial(transfer_body, uses, strides, kept), out...  11.2 us
    ppermute x9, starting transfers between devices, send_spec(): return lax.ppermute(value, 'spec', [(i, i ^ flip) for i in range(4)])  10.2 us
    pallas_call x3, Pallas kernels, propagate(): pl.pallas_call(functools.partial(propagate_kernel, wanted, count), out_sh...  9.62 us
    pallas_call x1, Pallas kernels, finish(): pl.pallas_call(functools.partial(finish_body, len(kernels), first, groups...  7.17 us
    ppermute x1, waiting for transfers between devices, boundaries(): lax.ppermute(jnp.where(first, top, bottom), geo, pairs + [(j, i) for i, j...  5.87 us
    ppermute x1, starting transfers between devices, boundaries(): lax.ppermute(jnp.where(first, top, bottom), geo, pairs + [(j, i) for i, j...  4.59 us
  transfers between devices with their start and end apart: 18, of which 6 were waited for; matrix products, arithmetic and copies ran while one was open for 5% of the time, Pallas kernels for 37%

profile of v7, /device:TPU:1, one launch (start us, length us, event | category | flops | bytes accessed | tf_op | source)
XLA Modules:
  0.0 91.6 jit_solution(12798606798381062900)
XLA Ops:
  0.0 1.4 %dynamic-slice_bitcast_fusion.refs_0_ = bf16[324,1296]{1,0:T(8,128)(2,1)S(1)} fusion(bf16[1,1296,1296]{2,1,0:T(8,128)(2,1)} %param.17, s32[]{:T(128)S(6)} %select_n.81), kind=kLoop, calls=%fused_computation | loop fusion | bytes 1679620 | tf_op jit(solution)/shard_map/dynamic_slice | solution.py:395
  1.4 2.2 %collective-permute-start = (bf16[324,1296]{1,0:T(8,128)(2,1)S(1)}, bf16[324,1296]{1,0:T(8,128)(2,1)S(1)}, u32[]{:S(2)}, u32[]{:S(2)}) collective-permute-start(bf16[324,1296]{1,0:T(8,128)(2,1)S(1)} %dynamic-slice_bitcast_fusion.refs_0_), channel_id=1, source_target_pairs={{0,2},{2,4},{4,6},{6,0},{1,3},{3,5},{5,7},{7,1},{8,10},{10,12},{12... | collective-permute-start | bytes 2519432 | tf_op jit(solution)/shard_map/ppermute | solution.py:335
  3.6 0.1 fusion.13
  3.7 0.1 abs_multiply_fusion
  3.8 0.1 compare_convert_fusion
  3.9 0.1 copy.28.coef_ref
  4.1 0.0 copy-start.9
  4.1 0.0 copy-start.4
  4.1 1.7 %copy.32 = bf16[324,16,128]{2,0,1:T(8,128)(2,1)S(1)} copy(bf16[324,16,128]{2,1,0:T(8,128)(2,1)} %param.9) | data formatting | bytes 2654208 | tf_op args[0]
  5.8 3.9 %shard_map.91 = (bf16[324,768]{1,0:T(8,128)(2,1)}, f32[1,768]{1,0:T(1,128)S(1)}) custom-call(bf16[16,324,128]{2,1,0:T(8,128)(2,1)S(1)} %bitcast.83, bf16[324,128]{1,0:T(8,128)(2,1)S(1)} %broadcast_in_dim.2.west_ref.east_ref, bf16[324,128]{1,0:T(8,128)(2,1)S(1)} %broadcast_in_dim.2.west_ref.east_ref, f32[16,128]{1,0:T(8,128)S(1)} %get-tuple-element.107.sea_ref, ...), custom_call_target="tpu_custom_call" | custom-call | flops 497664 | bytes 248832 | tf_op jit(solution)/shard_map/pallas_call | solution.py:126
  9.7 1.2 %collective-permute-start.4 = (bf16[324,768]{1,0:T(8,128)(2,1)}, bf16[324,768]{1,0:T(8,128)(2,1)}, u32[]{:S(2)}, u32[]{:S(2)}) collective-permute-start(bf16[324,768]{1,0:T(8,128)(2,1)} %get-tuple-element.53.refs_0_.refs_17_), channel_id=1, source_target_pairs={{0,16},{8,24},{16,0},{24,8},{1,17},{9,25},{17,1},{25,9},{2,18},{10... | collective-permute-start | bytes 1493000 | tf_op jit(solution)/shard_map/ppermute | solution.py:378
  11.0 1.2 %collective-permute-start.3 = (bf16[324,768]{1,0:T(8,128)(2,1)}, bf16[324,768]{1,0:T(8,128)(2,1)}, u32[]{:S(2)}, u32[]{:S(2)}) collective-permute-start(bf16[324,768]{1,0:T(8,128)(2,1)} %get-tuple-element.53.refs_0_.refs_17_), channel_id=1, source_target_pairs={{0,8},{8,0},{16,24},{24,16},{1,9},{9,1},{17,25},{25,17},{2,10},{10... | collective-permute-start | bytes 1493000 | tf_op jit(solution)/shard_map/ppermute | solution.py:378
  12.2 0.7 broadcast_select_fusion.2
  12.9 4.6 %collective-permute-start.2 = (bf16[324,128]{1,0:T(8,128)(2,1)}, bf16[324,128]{1,0:T(8,128)(2,1)}, u32[]{:S(2)}, u32[]{:S(2)}) collective-permute-start(bf16[324,128]{1,0:T(8,128)(2,1)} %get-tuple-element.101), channel_id=1, source_target_pairs={{1,2},{3,4},{5,6},{2,1},{4,3},{6,5},{9,10},{11,12},{13,14},{10,9},... | collective-permute-start | bytes 248840 | tf_op jit(solution)/shard_map/ppermute | solution.py:349
  17.5 0.1 collective-permute-start.1
  17.6 3.1 %shard_map.92 = (bf16[324,768]{1,0:T(8,128)(2,1)S(1)}, f32[1,768]{1,0:T(1,128)S(1)}) custom-call(bf16[16,324,128]{2,1,0:T(8,128)(2,1)S(1)} %bitcast.84, bf16[324,128]{1,0:T(8,128)(2,1)S(1)} %broadcast_in_dim.2.west_ref.east_ref, bf16[324,128]{1,0:T(8,128)(2,1)S(1)} %broadcast_in_dim.2.west_ref.east_ref, f32[16,128]{1,0:T(8,128)S(1)} %get-tuple-element.107.sea_ref, ...), custom_call_target="tpu_custom_call" | custom-call | flops 497664 | bytes 248832 | tf_op jit(solution)/shard_map/pallas_call | solution.py:126
  20.7 0.8 copy-done.2
  21.5 5.9 %collective-permute-done.2 = bf16[324,128]{1,0:T(8,128)(2,1)} collective-permute-done((bf16[324,128]{1,0:T(8,128)(2,1)}, bf16[324,128]{1,0:T(8,128)(2,1)}, u32[]{:S(2)}, u32[]{:S(2)}) %collective-permute-start.2) | collective-permute-done | bytes 82976 | tf_op jit(solution)/shard_map/ppermute | solution.py:349
  27.4 0.0 collective-permute-done.1
  27.4 0.0 collective-permute-done.4.refs_2_
  27.4 0.0 collective-permute-done.3.refs_1_
  27.4 0.0 collective-permute-done.refs_2_
  27.4 1.3 %collective-permute-start.6 = (bf16[324,768]{1,0:T(8,128)(2,1)}, bf16[324,768]{1,0:T(8,128)(2,1)S(1)}, u32[]{:S(2)}, u32[]{:S(2)}) collective-permute-start(bf16[324,768]{1,0:T(8,128)(2,1)} %collective-permute-done.4.refs_2_), channel_id=1, source_target_pairs={{0,8},{8,0},{16,24},{24,16},{1,9},{9,1},{17,25},{25,17},{2,10},{10... | collective-permute-start | bytes 1493000 | tf_op jit(solution)/shard_map/ppermute | solution.py:378
  28.7 0.0 collective-permute-start.10
  28.7 0.5 collective-permute-start.11
  29.3 0.3 collective-permute-start.5
  29.6 1.2 %collective-permute-start.8 = (bf16[324,768]{1,0:T(8,128)(2,1)}, bf16[324,768]{1,0:T(8,128)(2,1)S(1)}, u32[]{:S(2)}, u32[]{:S(2)}) collective-permute-start(bf16[324,768]{1,0:T(8,128)(2,1)} %copy-done.2), channel_id=1, source_target_pairs={{0,16},{8,24},{16,0},{24,8},{1,17},{9,25},{17,1},{25,9},{2,18},{10... | collective-permute-start | bytes 1493000 | tf_op jit(solution)/shard_map/ppermute | solution.py:378
  30.8 1.0 %broadcast_select_fusion = (bf16[324,128]{1,0:T(8,128)(2,1)S(1)}, bf16[324,128]{1,0:T(8,128)(2,1)S(1)}) fusion(bf16[324,128]{1,0:T(8,128)(2,1)} %collective-permute-done.1, bf16[324,128]{1,0:T(8,128)(2,1)} %collective-permute-done.2, pred[]{:T(512)S(6)} %eq.6), kind=kLoop, calls=%fused_computation.5 | loop fusion | flops 82944 | bytes 331777 | tf_op jit(solution)/shard_map/jit(_where)/select_n | solution.py:357
  31.8 2.6 %shard_map.93 = (bf16[324,512]{1,0:T(8,128)(2,1)S(1)}, f32[1,512]{1,0:T(1,128)S(1)}) custom-call(bf16[16,324,128]{2,1,0:T(8,128)(2,1)S(1)} %bitcast.85, bf16[324,128]{1,0:T(8,128)(2,1)S(1)} %get-tuple-element.106.west_ref, bf16[324,128]{1,0:T(8,128)(2,1)S(1)} %get-tuple-element.105.east_ref, f32[16,128]{1,0:T(8,128)S(1)} %get-tuple-element.107.sea_ref, ...), custom_call_target="tpu_custom_call" | custom-call | flops 331776 | bytes 165888 | tf_op jit(solution)/shard_map/pallas_call | solution.py:126
  34.3 6.6 %collective-permute-done.6.refs_3_ = bf16[324,768]{1,0:T(8,128)(2,1)S(1)} collective-permute-done((bf16[324,768]{1,0:T(8,128)(2,1)}, bf16[324,768]{1,0:T(8,128)(2,1)S(1)}, u32[]{:S(2)}, u32[]{:S(2)}) %collective-permute-start.6) | collective-permute-done | bytes 497696 | tf_op jit(solution)/shard_map/ppermute | solution.py:378
  41.0 1.2 %collective-permute-start.7 = (bf16[324,768]{1,0:T(8,128)(2,1)S(1)}, bf16[324,768]{1,0:T(8,128)(2,1)S(1)}, u32[]{:S(2)}, u32[]{:S(2)}) collective-permute-start(bf16[324,768]{1,0:T(8,128)(2,1)S(1)} %copy-done.3), channel_id=1, source_target_pairs={{0,8},{8,0},{16,24},{24,16},{1,9},{9,1},{17,25},{25,17},{2,10},{10... | collective-permute-start | bytes 1493000 | tf_op jit(solution)/shard_map/ppermute | solution.py:378
  42.2 0.0 collective-permute-done.10.refs_1_
  42.2 1.3 %collective-permute-start.9 = (bf16[324,512]{1,0:T(8,128)(2,1)S(1)}, bf16[324,512]{1,0:T(8,128)(2,1)S(1)}, u32[]{:S(2)}, u32[]{:S(2)}) collective-permute-start(bf16[324,512]{1,0:T(8,128)(2,1)S(1)} %get-tuple-element.74.refs_0_.refs_19_), channel_id=1, source_target_pairs={{0,16},{8,24},{16,0},{24,8},{1,17},{9,25},{17,1},{25,9},{2,18},{10... | collective-permute-start | bytes 995336 | tf_op jit(solution)/shard_map/ppermute | solution.py:378
  43.5 1.0 %shard_map.95 = (f32[8,768]{1,0:T(8,128)S(1)}, f32[8,768]{1,0:T(8,128)S(1)}, f32[8,512]{1,0:T(8,128)S(1)}) custom-call(s32[16,128]{1,0:T(8,128)S(1)} %copy-done.5, bf16[16,128]{1,0:T(8,128)(2,1)S(1)} %copy-done.6, bf16[16,128]{1,0:T(8,128)(2,1)S(1)} %copy-done.7, f32[1,768]{1,0:T(1,128)S(1)} %get-tuple-element.66.refs_0_.refs_2_, ...), custom_call_target="tpu_custom_call" | custom-call | tf_op jit(solution)/shard_map/pallas_call | solution.py:278
  44.6 0.0 copy-start
  44.6 2.0 %copy-done = bf16[1296,1296]{1,0:T(8,128)(2,1)S(1)} copy-done((bf16[1296,1296]{1,0:T(8,128)(2,1)S(1)}, bf16[1296,1296]{1,0:T(8,128)(2,1)}, u32[]{:S(2)}) %copy-start) | copy-done | bytes 3359256
  46.6 5.2 %shard_map.94 = (bf16[1296,768]{1,0:T(8,128)(2,1)S(1)}, f32[1,768]{1,0:T(1,128)S(1)}) custom-call(s32[1]{0:T(128)} %bitcast.22.here_ref, bf16[324,768]{1,0:T(8,128)(2,1)} %get-tuple-element.53.refs_0_.refs_17_, bf16[324,768]{1,0:T(8,128)(2,1)} %collective-permute-done.3.refs_1_, bf16[324,768]{1,0:T(8,128)(2,1)} %collective-permute-done.4.refs_2_, ...), custom_call_target="tpu_custom_call" | custom-call | flops 322486272 | bytes 419904 | tf_op jit(solution)/shard_map/pallas_call | solution.py:187
  51.8 0.0 collective-permute-done.11.refs_3_
  51.9 0.0 collective-permute-done.9.refs_2_
  51.9 0.0 collective-permute-done.8.refs_2_
  51.9 1.2 %collective-permute-done.5.refs_4_ = bf16[324,1296]{1,0:T(8,128)(2,1)S(1)} collective-permute-done((bf16[324,1296]{1,0:T(8,128)(2,1)S(1)}, bf16[324,1296]{1,0:T(8,128)(2,1)S(1)}, u32[]{:S(2)}, u32[]{:S(2)}) %collective-permute-start.5) | collective-permute-done | bytes 839840 | tf_op jit(solution)/shard_map/ppermute | solution.py:335
  53.1 0.3 collective-permute-done.7.refs_1_
  53.4 1.5 %collective-permute-start.15 = (bf16[324,1296]{1,0:T(8,128)(2,1)S(1)}, bf16[324,1296]{1,0:T(8,128)(2,1)S(1)}, u32[]{:S(2)}, u32[]{:S(2)}) collective-permute-start(bf16[324,1296]{1,0:T(8,128)(2,1)S(1)} %collective-permute-done.5.refs_4_), channel_id=1, source_target_pairs={{0,1},{1,0},{2,3},{3,2},{4,5},{5,4},{6,7},{7,6},{8,9},{9,8},{10,11... | collective-permute-start | bytes 2519432 | tf_op jit(solution)/shard_map/ppermute | solution.py:365
  54.9 0.4 collective-permute-start.12
  55.2 1.2 %collective-permute-start.16 = (bf16[324,768]{1,0:T(8,128)(2,1)S(1)}, bf16[324,768]{1,0:T(8,128)(2,1)S(1)}, u32[]{:S(2)}, u32[]{:S(2)}) collective-permute-start(bf16[324,768]{1,0:T(8,128)(2,1)S(1)} %collective-permute-done.7.refs_1_), channel_id=1, source_target_pairs={{0,16},{8,24},{16,0},{24,8},{1,17},{9,25},{17,1},{25,9},{2,18},{10... | collective-permute-start | bytes 1493000 | tf_op jit(solution)/shard_map/ppermute | solution.py:378
  56.5 1.3 %collective-permute-start.13 = (bf16[324,512]{1,0:T(8,128)(2,1)S(1)}, bf16[324,512]{1,0:T(8,128)(2,1)S(1)}, u32[]{:S(2)}, u32[]{:S(2)}) collective-permute-start(bf16[324,512]{1,0:T(8,128)(2,1)S(1)} %get-tuple-element.74.refs_0_.refs_19_), channel_id=1, source_target_pairs={{0,8},{8,0},{16,24},{24,16},{1,9},{9,1},{17,25},{25,17},{2,10},{10... | collective-permute-start | bytes 995336 | tf_op jit(solution)/shard_map/ppermute | solution.py:378
  57.8 0.3 collective-permute-start.14
  58.0 0.1 convert_reduce_fusion.2
  58.2 0.1 convert_reduce_fusion
  58.3 0.1 pad_add_fusion.1.bounds_ref
  58.4 0.0 collective-permute-done.15.refs_5_
  58.4 3.9 %shard_map.96 = (bf16[324,768]{1,0:T(8,128)(2,1)S(1)}, f32[8,128]{1,0:T(8,128)S(1)}) custom-call(s32[27]{0:T(128)S(1)} %pad_add_fusion.1.bounds_ref, bf16[324,1296]{1,0:T(8,128)(2,1)S(1)} %dynamic-slice_bitcast_fusion.refs_0_, bf16[324,1296]{1,0:T(8,128)(2,1)S(1)} %collective-permute-done.10.refs_1_, bf16[324,1296]{1,0:T(8,128)(2,1)S(1)} %collective-permute-done.refs_2_, ...), custom_call_target="tpu_custom_call" | custom-call | flops 241864704 | bytes 878688 | tf_op jit(solution)/shard_map/pallas_call | solution.py:244
  62.2 5.8 %collective-permute-done.16.refs_3_ = bf16[324,768]{1,0:T(8,128)(2,1)S(1)} collective-permute-done((bf16[324,768]{1,0:T(8,128)(2,1)S(1)}, bf16[324,768]{1,0:T(8,128)(2,1)S(1)}, u32[]{:S(2)}, u32[]{:S(2)}) %collective-permute-start.16) | collective-permute-done | bytes 497696 | tf_op jit(solution)/shard_map/ppermute | solution.py:378
  68.0 3.9 %shard_map.97 = (bf16[1296,768]{1,0:T(8,128)(2,1)S(1)}, f32[1,768]{1,0:T(1,128)S(1)}) custom-call(s32[1]{0:T(128)} %bitcast.22.here_ref, bf16[324,768]{1,0:T(8,128)(2,1)S(1)} %copy-done.3, bf16[324,768]{1,0:T(8,128)(2,1)S(1)} %collective-permute-done.7.refs_1_, bf16[324,768]{1,0:T(8,128)(2,1)S(1)} %collective-permute-done.8.refs_2_, ...), custom_call_target="tpu_custom_call" | custom-call | flops 322486272 | bytes 419904 | tf_op jit(solution)/shard_map/pallas_call | solution.py:187
  71.9 3.7 %shard_map.98 = (bf16[324,768]{1,0:T(8,128)(2,1)S(1)}, f32[8,128]{1,0:T(8,128)S(1)}) custom-call(s32[27]{0:T(128)S(1)} %pad_add_fusion.1.bounds_ref, bf16[324,1296]{1,0:T(8,128)(2,1)S(1)} %dynamic-slice_bitcast_fusion.refs_0_, bf16[324,1296]{1,0:T(8,128)(2,1)S(1)} %collective-permute-done.10.refs_1_, bf16[324,1296]{1,0:T(8,128)(2,1)S(1)} %collective-permute-done.refs_2_, ...), custom_call_target="tpu_custom_call" | custom-call | flops 241864704 | bytes 878688 | tf_op jit(solution)/shard_map/pallas_call | solution.py:244
  75.6 0.0 collective-permute-done.14.refs_3_
  75.6 0.0 collective-permute-done.13.refs_1_
  75.6 2.8 %shard_map.99 = (bf16[1296,512]{1,0:T(8,128)(2,1)S(1)}, f32[1,512]{1,0:T(1,128)S(1)}) custom-call(s32[1]{0:T(128)} %bitcast.22.here_ref, bf16[324,512]{1,0:T(8,128)(2,1)S(1)} %get-tuple-element.74.refs_0_.refs_19_, bf16[324,512]{1,0:T(8,128)(2,1)S(1)} %collective-permute-done.13.refs_1_, bf16[324,512]{1,0:T(8,128)(2,1)S(1)} %collective-permute-done.9.refs_2_, ...), custom_call_target="tpu_custom_call" | custom-call | flops 214990848 | bytes 419904 | tf_op jit(solution)/shard_map/pallas_call | solution.py:187
  78.4 0.4 collective-permute-done.12.refs_0_
  78.8 0.8 collective-permute-start.17
  79.6 3.6 %shard_map.100 = (bf16[324,512]{1,0:T(8,128)(2,1)S(1)}, f32[8,128]{1,0:T(8,128)S(1)}) custom-call(s32[27]{0:T(128)S(1)} %pad_add_fusion.1.bounds_ref, bf16[324,1296]{1,0:T(8,128)(2,1)S(1)} %dynamic-slice_bitcast_fusion.refs_0_, bf16[324,1296]{1,0:T(8,128)(2,1)S(1)} %collective-permute-done.10.refs_1_, bf16[324,1296]{1,0:T(8,128)(2,1)S(1)} %collective-permute-done.refs_2_, ...), custom_call_target="tpu_custom_call" | custom-call | flops 161243136 | bytes 795744 | tf_op jit(solution)/shard_map/pallas_call | solution.py:244
  83.2 0.0 collective-permute-done.17.refs_1_
  83.2 7.2 %shard_map.101 = bf16[16,324,128]{2,1,0:T(8,128)(2,1)S(1)} custom-call(s32[27]{0:T(128)S(1)} %pad_add_fusion.1.bounds_ref, f32[324,6]{1,0:T(8,128)S(1)} %copy.28.coef_ref, bf16[324,1296]{1,0:T(8,128)(2,1)S(1)} %collective-permute-done.12.refs_0_, bf16[324,1296]{1,0:T(8,128)(2,1)S(1)} %collective-permute-done.17.refs_1_, ...), custom_call_target="tpu_custom_call" | custom-call | flops 214990848 | bytes 873504 | tf_op jit(solution)/shard_map/pallas_call | solution.py:323
  90.4 1.2 %copy.29 = bf16[324,16,128]{2,1,0:T(8,128)(2,1)} copy(bf16[324,16,128]{2,0,1:T(8,128)(2,1)S(1)} %bitcast.86) | data formatting | bytes 2654208 | tf_op jit(solution)/shard_map/transpose | solution.py:514
  (32 shorter events, 0.2 us)
Async XLA Ops:
  0.0 3.8 %copy-start.8 = (s32[16,128]{1,0:T(8,128)S(1)}, s32[16,128]{1,0:T(8,128)}, u32[]{:S(2)}) copy-start(s32[16,128]{1,0:T(8,128)} %param.15) | copy-start | bytes 24580
  1.4 26.0 %collective-permute-start = (bf16[324,1296]{1,0:T(8,128)(2,1)S(1)}, bf16[324,1296]{1,0:T(8,128)(2,1)S(1)}, u32[]{:S(2)}, u32[]{:S(2)}) collective-permute-start(bf16[324,1296]{1,0:T(8,128)(2,1)S(1)} %dynamic-slice_bitcast_fusion.refs_0_), channel_id=1, source_target_pairs={{0,2},{2,4},{4,6},{6,0},{1,3},{3,5},{5,7},{7,1},{8,10},{10,12},{12... | collective-permute-start | bytes 2519432 | tf_op jit(solution)/shard_map/ppermute | solution.py:335
  4.1 1.7 %copy-start.9 = (s32[16,128]{1,0:T(8,128)S(1)}, s32[16,128]{1,0:T(8,128)}, u32[]{:S(2)}) copy-start(s32[16,128]{1,0:T(8,128)} %param.10) | copy-start | bytes 24580
  4.1 1.7 %copy-start.4 = (f32[16,128]{1,0:T(8,128)S(1)}, f32[16,128]{1,0:T(8,128)}, u32[]{:S(2)}) copy-start(f32[16,128]{1,0:T(8,128)} %depth_ref.5) | copy-start | bytes 24580
  9.7 17.6 %collective-permute-start.4 = (bf16[324,768]{1,0:T(8,128)(2,1)}, bf16[324,768]{1,0:T(8,128)(2,1)}, u32[]{:S(2)}, u32[]{:S(2)}) collective-permute-start(bf16[324,768]{1,0:T(8,128)(2,1)} %get-tuple-element.53.refs_0_.refs_17_), channel_id=1, source_target_pairs={{0,16},{8,24},{16,0},{24,8},{1,17},{9,25},{17,1},{25,9},{2,18},{10... | collective-permute-start | bytes 1493000 | tf_op jit(solution)/shard_map/ppermute | solution.py:378
  11.0 16.4 %collective-permute-start.3 = (bf16[324,768]{1,0:T(8,128)(2,1)}, bf16[324,768]{1,0:T(8,128)(2,1)}, u32[]{:S(2)}, u32[]{:S(2)}) collective-permute-start(bf16[324,768]{1,0:T(8,128)(2,1)} %get-tuple-element.53.refs_0_.refs_17_), channel_id=1, source_target_pairs={{0,8},{8,0},{16,24},{24,16},{1,9},{9,1},{17,25},{25,17},{2,10},{10... | collective-permute-start | bytes 1493000 | tf_op jit(solution)/shard_map/ppermute | solution.py:378
  12.9 14.5 %collective-permute-start.2 = (bf16[324,128]{1,0:T(8,128)(2,1)}, bf16[324,128]{1,0:T(8,128)(2,1)}, u32[]{:S(2)}, u32[]{:S(2)}) collective-permute-start(bf16[324,128]{1,0:T(8,128)(2,1)} %get-tuple-element.101), channel_id=1, source_target_pairs={{1,2},{3,4},{5,6},{2,1},{4,3},{6,5},{9,10},{11,12},{13,14},{10,9},... | collective-permute-start | bytes 248840 | tf_op jit(solution)/shard_map/ppermute | solution.py:349
  17.5 9.9 %collective-permute-start.1 = (bf16[324,128]{1,0:T(8,128)(2,1)}, bf16[324,128]{1,0:T(8,128)(2,1)}, u32[]{:S(2)}, u32[]{:S(2)}) collective-permute-start(bf16[324,128]{1,0:T(8,128)(2,1)} %get-tuple-element.102), channel_id=1, source_target_pairs={{0,1},{1,0},{2,3},{3,2},{4,5},{5,4},{6,7},{7,6},{8,9},{9,8},{10,11... | collective-permute-start | bytes 248840 | tf_op jit(solution)/shard_map/ppermute | solution.py:347
  20.7 0.8 copy-start.2
  21.5 22.0 %copy-start.5 = (s32[16,128]{1,0:T(8,128)S(1)}, s32[16,128]{1,0:T(8,128)}, u32[]{:S(2)}) copy-start(s32[16,128]{1,0:T(8,128)} %ice_ref.1) | copy-start | bytes 24580
  21.5 22.0 %copy-start.6 = (bf16[16,128]{1,0:T(8,128)(2,1)S(1)}, bf16[16,128]{1,0:T(8,128)(2,1)}, u32[]{:S(2)}) copy-start(bf16[16,128]{1,0:T(8,128)(2,1)} %speed_ref.1) | copy-start | bytes 12292
  21.5 22.0 %copy-start.7 = (bf16[16,128]{1,0:T(8,128)(2,1)S(1)}, bf16[16,128]{1,0:T(8,128)(2,1)}, u32[]{:S(2)}) copy-start(bf16[16,128]{1,0:T(8,128)(2,1)} %angle_ref.1) | copy-start | bytes 12292
  21.5 19.5 %copy-start.3 = (bf16[324,768]{1,0:T(8,128)(2,1)S(1)}, bf16[324,768]{1,0:T(8,128)(2,1)}, u32[]{:S(2)}) copy-start(bf16[324,768]{1,0:T(8,128)(2,1)} %copy-done.2) | copy-start | bytes 1492996
  27.4 13.6 %collective-permute-start.6 = (bf16[324,768]{1,0:T(8,128)(2,1)}, bf16[324,768]{1,0:T(8,128)(2,1)S(1)}, u32[]{:S(2)}, u32[]{:S(2)}) collective-permute-start(bf16[324,768]{1,0:T(8,128)(2,1)} %collective-permute-done.4.refs_2_), channel_id=1, source_target_pairs={{0,8},{8,0},{16,24},{24,16},{1,9},{9,1},{17,25},{25,17},{2,10},{10... | collective-permute-start | bytes 1493000 | tf_op jit(solution)/shard_map/ppermute | solution.py:378
  28.7 13.5 %collective-permute-start.10 = (bf16[324,1296]{1,0:T(8,128)(2,1)S(1)}, bf16[324,1296]{1,0:T(8,128)(2,1)S(1)}, u32[]{:S(2)}, u32[]{:S(2)}) collective-permute-start(bf16[324,1296]{1,0:T(8,128)(2,1)S(1)} %dynamic-slice_bitcast_fusion.refs_0_), channel_id=1, source_target_pairs={{0,1},{1,0},{2,3},{3,2},{4,5},{5,4},{6,7},{7,6},{8,9},{9,8},{10,11... | collective-permute-start | bytes 2519432 | tf_op jit(solution)/shard_map/ppermute | solution.py:365
  28.7 23.1 %collective-permute-start.11 = (bf16[324,1296]{1,0:T(8,128)(2,1)S(1)}, bf16[324,1296]{1,0:T(8,128)(2,1)S(1)}, u32[]{:S(2)}, u32[]{:S(2)}) collective-permute-start(bf16[324,1296]{1,0:T(8,128)(2,1)S(1)} %collective-permute-done.refs_2_), channel_id=1, source_target_pairs={{0,1},{1,0},{2,3},{3,2},{4,5},{5,4},{6,7},{7,6},{8,9},{9,8},{10,11... | collective-permute-start | bytes 2519432 | tf_op jit(solution)/shard_map/ppermute | solution.py:365
  29.3 23.8 %collective-permute-start.5 = (bf16[324,1296]{1,0:T(8,128)(2,1)S(1)}, bf16[324,1296]{1,0:T(8,128)(2,1)S(1)}, u32[]{:S(2)}, u32[]{:S(2)}) collective-permute-start(bf16[324,1296]{1,0:T(8,128)(2,1)S(1)} %collective-permute-done.refs_2_), channel_id=1, source_target_pairs={{0,2},{2,4},{4,6},{6,0},{1,3},{3,5},{5,7},{7,1},{8,10},{10,12},{12... | collective-permute-start | bytes 2519432 | tf_op jit(solution)/shard_map/ppermute | solution.py:335
  29.6 22.3 %collective-permute-start.8 = (bf16[324,768]{1,0:T(8,128)(2,1)}, bf16[324,768]{1,0:T(8,128)(2,1)S(1)}, u32[]{:S(2)}, u32[]{:S(2)}) collective-permute-start(bf16[324,768]{1,0:T(8,128)(2,1)} %copy-done.2), channel_id=1, source_target_pairs={{0,16},{8,24},{16,0},{24,8},{1,17},{9,25},{17,1},{25,9},{2,18},{10... | collective-permute-start | bytes 1493000 | tf_op jit(solution)/shard_map/ppermute | solution.py:378
  41.0 12.4 %collective-permute-start.7 = (bf16[324,768]{1,0:T(8,128)(2,1)S(1)}, bf16[324,768]{1,0:T(8,128)(2,1)S(1)}, u32[]{:S(2)}, u32[]{:S(2)}) collective-permute-start(bf16[324,768]{1,0:T(8,128)(2,1)S(1)} %copy-done.3), channel_id=1, source_target_pairs={{0,8},{8,0},{16,24},{24,16},{1,9},{9,1},{17,25},{25,17},{2,10},{10... | collective-permute-start | bytes 1493000 | tf_op jit(solution)/shard_map/ppermute | solution.py:378
  42.2 9.7 %collective-permute-start.9 = (bf16[324,512]{1,0:T(8,128)(2,1)S(1)}, bf16[324,512]{1,0:T(8,128)(2,1)S(1)}, u32[]{:S(2)}, u32[]{:S(2)}) collective-permute-start(bf16[324,512]{1,0:T(8,128)(2,1)S(1)} %get-tuple-element.74.refs_0_.refs_19_), channel_id=1, source_target_pairs={{0,16},{8,24},{16,0},{24,8},{1,17},{9,25},{17,1},{25,9},{2,18},{10... | collective-permute-start | bytes 995336 | tf_op jit(solution)/shard_map/ppermute | solution.py:378
  44.6 2.0 %copy-start = (bf16[1296,1296]{1,0:T(8,128)(2,1)S(1)}, bf16[1296,1296]{1,0:T(8,128)(2,1)}, u32[]{:S(2)}) copy-start(bf16[1296,1296]{1,0:T(8,128)(2,1)} %refs_4_.5) | copy-start | bytes 10077700
  53.4 5.0 %collective-permute-start.15 = (bf16[324,1296]{1,0:T(8,128)(2,1)S(1)}, bf16[324,1296]{1,0:T(8,128)(2,1)S(1)}, u32[]{:S(2)}, u32[]{:S(2)}) collective-permute-start(bf16[324,1296]{1,0:T(8,128)(2,1)S(1)} %collective-permute-done.5.refs_4_), channel_id=1, source_target_pairs={{0,1},{1,0},{2,3},{3,2},{4,5},{5,4},{6,7},{7,6},{8,9},{9,8},{10,11... | collective-permute-start | bytes 2519432 | tf_op jit(solution)/shard_map/ppermute | solution.py:365
  54.9 23.9 %collective-permute-start.12 = (bf16[324,1296]{1,0:T(8,128)(2,1)S(1)}, bf16[324,1296]{1,0:T(8,128)(2,1)S(1)}, u32[]{:S(2)}, u32[]{:S(2)}) collective-permute-start(bf16[324,1296]{1,0:T(8,128)(2,1)S(1)} %collective-permute-done.5.refs_4_), channel_id=1, source_target_pairs={{0,2},{2,4},{4,6},{6,0},{1,3},{3,5},{5,7},{7,1},{8,10},{10,12},{12... | collective-permute-start | bytes 2519432 | tf_op jit(solution)/shard_map/ppermute | solution.py:335
  55.2 12.8 %collective-permute-start.16 = (bf16[324,768]{1,0:T(8,128)(2,1)S(1)}, bf16[324,768]{1,0:T(8,128)(2,1)S(1)}, u32[]{:S(2)}, u32[]{:S(2)}) collective-permute-start(bf16[324,768]{1,0:T(8,128)(2,1)S(1)} %collective-permute-done.7.refs_1_), channel_id=1, source_target_pairs={{0,16},{8,24},{16,0},{24,8},{1,17},{9,25},{17,1},{25,9},{2,18},{10... | collective-permute-start | bytes 1493000 | tf_op jit(solution)/shard_map/ppermute | solution.py:378
  56.5 19.1 %collective-permute-start.13 = (bf16[324,512]{1,0:T(8,128)(2,1)S(1)}, bf16[324,512]{1,0:T(8,128)(2,1)S(1)}, u32[]{:S(2)}, u32[]{:S(2)}) collective-permute-start(bf16[324,512]{1,0:T(8,128)(2,1)S(1)} %get-tuple-element.74.refs_0_.refs_19_), channel_id=1, source_target_pairs={{0,8},{8,0},{16,24},{24,16},{1,9},{9,1},{17,25},{25,17},{2,10},{10... | collective-permute-start | bytes 995336 | tf_op jit(solution)/shard_map/ppermute | solution.py:378
  57.8 17.9 %collective-permute-start.14 = (bf16[324,512]{1,0:T(8,128)(2,1)S(1)}, bf16[324,512]{1,0:T(8,128)(2,1)S(1)}, u32[]{:S(2)}, u32[]{:S(2)}) collective-permute-start(bf16[324,512]{1,0:T(8,128)(2,1)S(1)} %collective-permute-done.9.refs_2_), channel_id=1, source_target_pairs={{0,8},{8,0},{16,24},{24,16},{1,9},{9,1},{17,25},{25,17},{2,10},{10... | collective-permute-start | bytes 995336 | tf_op jit(solution)/shard_map/ppermute | solution.py:378
  58.4 9.7 %copy-start.1 = (bf16[1296,1296]{1,0:T(8,128)(2,1)S(1)}, bf16[1296,1296]{1,0:T(8,128)(2,1)}, u32[]{:S(2)}) copy-start(bf16[1296,1296]{1,0:T(8,128)(2,1)} %refs_4_.5) | copy-start | bytes 10077700
  78.8 4.4 %collective-permute-start.17 = (bf16[324,1296]{1,0:T(8,128)(2,1)S(1)}, bf16[324,1296]{1,0:T(8,128)(2,1)S(1)}, u32[]{:S(2)}, u32[]{:S(2)}) collective-permute-start(bf16[324,1296]{1,0:T(8,128)(2,1)S(1)} %collective-permute-done.12.refs_0_), channel_id=1, source_target_pairs={{0,1},{1,0},{2,3},{3,2},{4,5},{5,4},{6,7},{7,6},{8,9},{9,8},{10,11... | collective-permute-start | bytes 2519432 | tf_op jit(solution)/shard_map/ppermute | solution.py:365
